TPU v7x, 128 devices: a whole 4x4x4 slice. The times are simulated.
128 devices in a mesh: rows: 16 (over z, x_lo, core), ch: 8 (over x_hi, y).
Axes of the slice: x: 4 (x_hi: 2, x_lo: 2; x = x_hi * 2 + x_lo), y: 4, z: 4, core: 2. Of those that a mesh axis runs over, the one named last changes fastest.
Arguments:
- x_band: bfloat16 [512, 128, 128], P('ch', 'rows'), may hold values from -40 to 40
- first_filter: bfloat16 [3, 3, 512, 512], P(None, None, 'ch'), may hold values from -0.09375 to 0.09375
- second_filter: bfloat16 [3, 3, 512, 512], P(None, None, 'ch'), may hold values from -0.09375 to 0.09375
- norm_gain: float32 [512], P('ch'), may hold values from 0.5 to 2
- norm_shift: float32 [512], P('ch'), may hold values from -3 to 3
- out_cotangent: bfloat16 [512, 128, 128], P('ch', 'rows'), may hold values from -6 to 6
Outputs:
- band_grad: bfloat16 [512, 128, 128], P('ch', 'rows')
- first_grad: float32 [3, 3, 512, 512], P(None, None, 'ch')
- second_grad: float32 [3, 3, 512, 512], P(None, None, 'ch')
- gain_grad: float32 [512], P('ch')
- shift_grad: float32 [512], P('ch')
All inputs are finite; a program needn't handle non-finite values.
Results may differ from a plain program's by a relative error of at most 0.028.
Values may be sent and summed in bfloat16 or wider, within the bound.
No kernel may reach another device: no remote copies, remote signals or barrier semaphores. Data moves between devices by JAX's collectives and lax.ppermute only.
A program may use at most 128 MiB of HBM per device.

v0:
```python
import jax
import jax.numpy as jnp
from jax import lax
from jax.sharding import PartitionSpec as P

C = 512
G = 32


epsilon = 1e-06


def with_halo(x, sides, width):
    for axis, dim in sides:
        size, length = (lax.axis_size(axis), x.shape[dim])
        up = [(i, (i + 1) % size) for i in range(size - 1)]
        down = [(j, i) for i, j in up]
        last = lax.slice_in_dim(x, length - width, length, axis=dim)
        initial = lax.slice_in_dim(x, 0, width, axis=dim)
        before = lax.ppermute(last, axis, up)
        after = lax.ppermute(initial, axis, down)
        x = jnp.concatenate([before, x, after], axis=dim)
    return x


def pad_cols(values):
    return jnp.pad(values, ((0, 0), (0, 0), (1, 1)))


def rims(values):
    return with_halo(values, (("rows", 1),), 1)


def widen(values):
    gathered = lax.all_gather(values, "ch", axis=0, tiled=True)
    return pad_cols(rims(gathered))


def conv_local(padded, weight, strip_rows, strip_cols):
    running = jnp.zeros((weight.shape[2], strip_rows * strip_cols), jnp.float32)
    for row_tap in range(3):
        for col_tap in range(3):
            slab = padded[
                :, row_tap : row_tap + strip_rows, col_tap : col_tap + strip_cols
            ].reshape(padded.shape[0], -1)
            running = running + jnp.dot(
                weight[row_tap, col_tap], slab, preferred_element_type=jnp.float32
            )
    return running


def filter_local(gradient, padded, strip_rows, strip_cols):
    outer = []
    for row_tap in range(3):
        inner = []
        for col_tap in range(3):
            slab = padded[
                :, row_tap : row_tap + strip_rows, col_tap : col_tap + strip_cols
            ].reshape(padded.shape[0], -1)
            inner.append(
                lax.dot_general(
                    gradient, slab, (((1,), (1,)), ((), ())), preferred_element_type=jnp.float32
                )
            )
        outer.append(jnp.stack(inner))
    return jnp.stack(outer)


def transpose_local(weight, padded, strip_rows, strip_cols):
    running = jnp.zeros((weight.shape[3], strip_rows * strip_cols), jnp.float32)
    for row_tap in range(3):
        for col_tap in range(3):
            slab = padded[
                :, 2 - row_tap : 2 - row_tap + strip_rows, 2 - col_tap : 2 - col_tap + strip_cols
            ].reshape(padded.shape[0], -1)
            running = running + lax.dot_general(
                weight[row_tap, col_tap],
                slab,
                (((0,), (0,)), ((), ())),
                preferred_element_type=jnp.float32,
            )
    return running


def input_grad(gradient, weight):
    chans, strip_rows, strip_cols = gradient.shape
    padded = pad_cols(rims(gradient))
    summed = lax.psum_scatter(
        transpose_local(weight, padded, strip_rows, strip_cols)
        .reshape(lax.axis_size("ch") * chans, strip_rows, strip_cols)
        .astype(jnp.bfloat16),
        "ch",
        scatter_dimension=0,
        tiled=True,
    ).astype(jnp.float32)
    return summed.reshape(chans, -1)


def body(x_band, first_filter, second_filter, norm_gain, norm_shift, out_cotangent):
    chans, strip_rows, strip_cols = x_band.shape
    group_size = C // G
    groups = chans // group_size
    cell_count = group_size * strip_rows * lax.axis_size("rows") * strip_cols
    x_pad = widen(x_band)
    hidden = conv_local(x_pad, first_filter, strip_rows, strip_cols)
    grouped = hidden.reshape(groups, -1)
    group_sum, group_square = lax.psum(
        (jnp.sum(grouped, axis=1), jnp.sum(grouped * grouped, axis=1)), "rows"
    )
    group_mean = group_sum / cell_count
    group_var = group_square / cell_count - group_mean * group_mean
    inv_std = lax.rsqrt(group_var + epsilon)
    channel_mean = jnp.repeat(group_mean, group_size)
    channel_scale = jnp.repeat(inv_std, group_size)
    normed = (hidden - channel_mean[:, None]) * channel_scale[:, None]
    shifted = normed * norm_gain[:, None] + norm_shift[:, None]
    squashed = jax.nn.sigmoid(shifted)
    activation = (shifted * squashed).astype(jnp.bfloat16).reshape(chans, strip_rows, strip_cols)
    act_pad = widen(activation)
    second_grad = filter_local(out_cotangent.reshape(chans, -1), act_pad, strip_rows, strip_cols)
    act_grad = input_grad(out_cotangent, second_filter)
    pre_grad = act_grad * squashed * (1.0 + shifted * (1.0 - squashed))
    gain_grad, shift_grad = lax.psum(
        (jnp.sum(pre_grad * normed, axis=1), jnp.sum(pre_grad, axis=1)), "rows"
    )
    first_term = jnp.sum((norm_gain * shift_grad).reshape(groups, group_size), axis=1) / cell_count
    second_term = jnp.sum((norm_gain * gain_grad).reshape(groups, group_size), axis=1) / cell_count
    hidden_grad = channel_scale[:, None] * (
        pre_grad * norm_gain[:, None]
        - jnp.repeat(first_term, group_size)[:, None]
        - normed * jnp.repeat(second_term, group_size)[:, None]
    )
    hidden_grad = hidden_grad.astype(jnp.bfloat16)
    first_grad = filter_local(hidden_grad, x_pad, strip_rows, strip_cols)
    band_grad = input_grad(hidden_grad.reshape(chans, strip_rows, strip_cols), first_filter)
    band_grad = band_grad.reshape(chans, strip_rows, strip_cols).astype(jnp.bfloat16)
    first_grad, second_grad = (
        lax.psum(first_grad.astype(jnp.bfloat16), "rows").astype(jnp.float32),
        lax.psum(second_grad.astype(jnp.bfloat16), "rows").astype(jnp.float32),
    )
    return (band_grad, first_grad, second_grad, gain_grad, shift_grad)


def solution(mesh):
    return jax.shard_map(
        body,
        mesh=mesh,
        in_specs=(
            P("ch", "rows", None),
            P(None, None, "ch", None),
            P(None, None, "ch", None),
            P("ch"),
            P("ch"),
            P("ch", "rows", None),
        ),
        out_specs=(
            P("ch", "rows", None),
            P(None, None, "ch", None),
            P(None, None, "ch", None),
            P("ch"),
            P("ch"),
        ),
        check_vma=False,
    )
```

profile of v0, /device:TPU:1, one launch (start us, length us, event | category | flops | bytes accessed | tf_op | source)
XLA Modules:
  0.0 452.5 jit_solution(10929868525126233738)
XLA Ops:
  9.0 3.3 collective-permute-start.3
  12.3 3.1 collective-permute-start.2
  23.6 34.9 %all-gather.3.cloned.1.call-done = bf16[512,8,128]{2,1,0:T(8,128)(2,1)} async-done(((bf16[64,8,128]{2,1,0:T(8,128)(2,1)}), bf16[512,8,128]{2,1,0:T(8,128)(2,1)}) %all-gather.3.cloned.1.call-update) | async-done | bytes 1048592 | tf_op jit(solution)/shard_map/all_gather | solution.py:35
  58.5 2.1 fusion.239
  60.6 4.0 collective-permute-start.1
  64.6 2.3 collective-permute-start
  68.9 4.3 fusion.6
  73.2 2.2 fusion.237
  80.6 28.6 %all-reduce.5 = (f32[4]{0:T(128)S(1)}, f32[4]{0:T(128)}) all-reduce(f32[4]{0:T(128)} %reduce_sum.73, f32[4]{0:T(128)S(1)} %reduce_sum.70), channel_id=1, replica_groups=mesh['rows'=16,'ch'=8] {'rows'}, use_global_device_ids=true, to_apply=%region_5.6 | all-reduce | flops 8 | bytes 64 | tf_op jit(solution)/shard_map/psum | solution.py:107
  110.1 22.5 %reduce-scatter.3.cloned.1.call-done = bf16[64,8,128]{2,1,0:T(8,128)(2,1)} async-done(((bf16[512,8,128]{2,1,0:T(8,128)(2,1)}), bf16[64,8,128]{2,1,0:T(8,128)(2,1)}) %reduce-scatter.3.cloned.1.call-update) | async-done | bytes 131088 | tf_op jit(solution)/shard_map/reduce_scatter | solution.py:88
  133.6 2.3 fusion.235
  135.9 29.7 %all-reduce.4 = (f32[64]{0:T(128)}, f32[64]{0:T(128)}) all-reduce(f32[64]{0:T(128)} %get-tuple-element.6, f32[64]{0:T(128)S(1)} %get-tuple-element.5), channel_id=1, replica_groups=mesh['rows'=16,'ch'=8] {'rows'}, use_global_device_ids=true, to_apply=%region_11.12 | all-reduce | flops 128 | bytes 1024 | tf_op jit(solution)/shard_map/psum | solution.py:123
  173.5 2.4 fusion.67
  175.9 2.3 fusion.66
  184.0 3.5 collective-permute-start.5
  187.5 2.1 collective-permute-start.4
  201.6 30.0 %all-gather.5.cloned.1.call-done = bf16[512,8,128]{2,0,1:T(8,128)(2,1)} async-done(((bf16[64,8,128]{2,0,1:T(8,128)(2,1)}), bf16[512,8,128]{2,0,1:T(8,128)(2,1)}) %all-gather.5.cloned.1.call-update) | async-done | bytes 1048592 | tf_op jit(solution)/shard_map/all_gather | solution.py:35
  232.7 4.2 collective-permute-start.6
  236.9 1.9 collective-permute-start.7
  240.5 2.7 collective-permute-done.7
  252.2 4.1 add_convert_fusion
  257.8 113.1 %all-reduce.9.cloned.1.call-done = (bf16[3,3,64,512]{3,2,1,0:T(8,128)(2,1)}, bf16[3,3,64,512]{3,2,1,0:T(8,128)(2,1)}) async-done(((bf16[3,3,64,512]{3,2,1,0:T(8,128)(2,1)}, bf16[3,3,64,512]{3,2,1,0:T(8,128)(2,1)}), (bf16[3,3,64,512]{3,2,1,0:T(8,128)(2,1)}, bf16[3,3,64,512]{3,2,1,0:T(8,128)(2,1)})) %all-reduce.9.cloned.1.call-update) | async-done | bytes 1179664 | tf_op jit(solution)/shard_map/psum | solution.py:138
  370.9 2.3 convert_element_type.40
  374.4 71.6 %reduce-scatter.5.cloned.1.call-done = bf16[64,8,128]{2,1,0:T(8,128)(2,1)} async-done(((bf16[512,8,128]{2,1,0:T(8,128)(2,1)}), bf16[64,8,128]{2,1,0:T(8,128)(2,1)}) %reduce-scatter.5.cloned.1.call-update) | async-done | bytes 131088 | tf_op jit(solution)/shard_map/reduce_scatter | solution.py:88
  (155 shorter events, 58.6 us)
Async XLA Ops:
  7.2 9.8 %copy-start.14 = (bf16[64,8,128]{2,1,0:T(8,128)(2,1)S(1)}, bf16[64,8,128]{2,1,0:T(8,128)(2,1)}, u32[]{:S(2)}) copy-start(bf16[64,8,128]{2,1,0:T(8,128)(2,1)} %param.11) | copy-start | bytes 393220
  7.2 51.3 %all-gather.3.cloned.1.call-start = ((), (), s32[]{:S(2)}) async-start(), calls=%async_computation.2 | async-start | bytes 1179648 | tf_op jit(solution)/shard_map/all_gather | solution.py:35
  7.9 124.7 %reduce-scatter.3.cloned.1.call-start = ((), (), s32[]{:S(2)}) async-start(), calls=%async_computation.3 | async-start | bytes 1179648 | tf_op jit(solution)/shard_map/reduce_scatter | solution.py:88
  9.0 7.9 %collective-permute-start.3 = (bf16[64,1,128]{2,1,0:T(2,128)(2,1)S(1)}, bf16[64,1,128]{2,1,0:T(2,128)(2,1)S(1)}, u32[]{:S(2)}, u32[]{:S(2)}) collective-permute-start(bf16[64,1,128]{2,1,0:T(2,128)(2,1)S(1)} %get-tuple-element.47), channel_id=1, source_target_pairs={{8,0},{16,8},{24,16},{32,24},{40,32},{48,40},{56,48},{64,56},{72,6... | collective-permute-start | bytes 49160 | tf_op jit(solution)/shard_map/ppermute | solution.py:21
  12.3 4.6 %collective-permute-start.2 = (bf16[64,1,128]{2,1,0:T(2,128)(2,1)S(1)}, bf16[64,1,128]{2,1,0:T(2,128)(2,1)S(1)}, u32[]{:S(2)}, u32[]{:S(2)}) collective-permute-start(bf16[64,1,128]{2,1,0:T(2,128)(2,1)S(1)} %get-tuple-element.48), channel_id=1, source_target_pairs={{0,8},{8,16},{16,24},{24,32},{32,40},{40,48},{48,56},{56,64},{64,7... | collective-permute-start | bytes 49160 | tf_op jit(solution)/shard_map/ppermute | solution.py:20
  23.6 208.1 %all-gather.5.cloned.1.call-start = ((), (), s32[]{:S(2)}) async-start(), calls=%async_computation.5 | async-start | bytes 1179648 | tf_op jit(solution)/shard_map/all_gather | solution.py:35
  58.5 10.4 %copy-start = (bf16[512,8,128]{2,1,0:T(8,128)(2,1)S(1)}, bf16[512,8,128]{2,1,0:T(8,128)(2,1)}, u32[]{:S(2)}) copy-start(bf16[512,8,128]{2,1,0:T(8,128)(2,1)} %all-gather.3.cloned.1.call-done) | copy-start | bytes 3145732
  60.6 7.9 %collective-permute-start.1 = (bf16[512,1,128]{2,0,1:T(8,128)(2,1)S(1)}, bf16[512,1,128]{2,0,1:T(8,128)(2,1)S(1)}, u32[]{:S(2)}, u32[]{:S(2)}) collective-permute-start(bf16[512,1,128]{2,0,1:T(8,128)(2,1)S(1)} %copy.25), channel_id=1, source_target_pairs={{8,0},{16,8},{24,16},{32,24},{40,32},{48,40},{56,48},{64,56},{72,6... | collective-permute-start | bytes 393224 | tf_op jit(solution)/shard_map/ppermute | solution.py:21
  64.6 4.1 collective-permute-start
  75.5 3.7 copy-start.8
  78.9 54.7 %copy-start.23 = (f32[64]{0:T(128)S(1)}, f32[64]{0:T(128)}, u32[]{:S(2)}) copy-start(f32[64]{0:T(128)} %param.9) | copy-start | bytes 772
  172.3 5.9 %copy-start.11 = (bf16[512,8,128]{2,1,0:T(8,128)(2,1)S(1)}, bf16[512,8,128]{2,1,0:T(8,128)(2,1)}, u32[]{:S(2)}) copy-start(bf16[512,8,128]{2,1,0:T(8,128)(2,1)} %copy-done.10) | copy-start | bytes 3145732
  173.5 5.8 %copy-start.9 = (bf16[512,8,128]{2,1,0:T(8,128)(2,1)S(1)}, bf16[512,8,128]{2,1,0:T(8,128)(2,1)}, u32[]{:S(2)}) copy-start(bf16[512,8,128]{2,1,0:T(8,128)(2,1)} %copy-done.8) | copy-start | bytes 3145732
  181.5 8.1 %copy-start.19 = (bf16[8,8,8,128]{3,2,1,0:T(8,128)(2,1)S(1)}, bf16[8,8,8,128]{3,2,1,0:T(8,128)(2,1)}, u32[]{:S(2)}) copy-start(bf16[8,8,8,128]{3,2,1,0:T(8,128)(2,1)} %get-tuple-element.40) | copy-start | bytes 393220
  181.6 9.0 %copy-start.20 = (bf16[1,64,512]{2,1,0:T(8,128)(2,1)S(1)}, bf16[1,64,512]{2,1,0:T(8,128)(2,1)}, u32[]{:S(2)}) copy-start(bf16[1,64,512]{2,1,0:T(8,128)(2,1)} %fusion.67) | copy-start | bytes 196612
  181.6 9.0 %copy-start.21 = (bf16[1,64,512]{2,1,0:T(8,128)(2,1)S(1)}, bf16[1,64,512]{2,1,0:T(8,128)(2,1)}, u32[]{:S(2)}) copy-start(bf16[1,64,512]{2,1,0:T(8,128)(2,1)} %fusion.66) | copy-start | bytes 196612
  181.6 9.0 %copy-start.22 = (bf16[1,64,512]{2,1,0:T(8,128)(2,1)S(1)}, bf16[1,64,512]{2,1,0:T(8,128)(2,1)}, u32[]{:S(2)}) copy-start(bf16[1,64,512]{2,1,0:T(8,128)(2,1)} %fusion.65) | copy-start | bytes 196612
  184.0 7.6 %collective-permute-start.5 = (bf16[64,1,128]{2,1,0:T(2,128)(2,1)}, bf16[64,1,128]{2,1,0:T(2,128)(2,1)S(1)}, u32[]{:S(2)}, u32[]{:S(2)}) collective-permute-start(bf16[64,1,128]{2,1,0:T(2,128)(2,1)} %get-tuple-element.43), channel_id=1, source_target_pairs={{8,0},{16,8},{24,16},{32,24},{40,32},{48,40},{56,48},{64,56},{72,6... | collective-permute-start | bytes 49160 | tf_op jit(solution)/shard_map/ppermute | solution.py:21
  187.5 4.1 collective-permute-start.4
  190.3 180.6 %all-reduce.9.cloned.1.call-start = ((), (), s32[]{:S(2)}) async-start(), calls=%async_computation.6 | async-start | bytes 2359296 | tf_op jit(solution)/shard_map/psum | solution.py:138
  231.6 11.5 %copy-start.3 = (bf16[512,8,128]{2,0,1:T(8,128)(2,1)S(1)}, bf16[512,8,128]{2,0,1:T(8,128)(2,1)}, u32[]{:S(2)}) copy-start(bf16[512,8,128]{2,0,1:T(8,128)(2,1)} %all-gather.5.cloned.1.call-done) | copy-start | bytes 3145732
  232.7 7.8 %collective-permute-start.6 = (bf16[512,1,128]{2,0,1:T(8,128)(2,1)S(1)}, bf16[512,1,128]{2,0,1:T(8,128)(2,1)S(1)}, u32[]{:S(2)}, u32[]{:S(2)}) collective-permute-start(bf16[512,1,128]{2,0,1:T(8,128)(2,1)S(1)} %get-tuple-element.22), channel_id=1, source_target_pairs={{0,8},{8,16},{16,24},{24,32},{32,40},{40,48},{48,56},{56,64},{64,7... | collective-permute-start | bytes 393224 | tf_op jit(solution)/shard_map/ppermute | solution.py:20
  236.9 6.3 %collective-permute-start.7 = (bf16[512,1,128]{2,0,1:T(8,128)(2,1)S(1)}, bf16[512,1,128]{2,0,1:T(8,128)(2,1)S(1)}, u32[]{:S(2)}, u32[]{:S(2)}) collective-permute-start(bf16[512,1,128]{2,0,1:T(8,128)(2,1)S(1)} %get-tuple-element.23), channel_id=1, source_target_pairs={{8,0},{16,8},{24,16},{32,24},{40,32},{48,40},{56,48},{64,56},{72,6... | collective-permute-start | bytes 393224 | tf_op jit(solution)/shard_map/ppermute | solution.py:21
  249.9 196.1 %reduce-scatter.5.cloned.1.call-start = ((), (), s32[]{:S(2)}) async-start(), calls=%async_computation.4 | async-start | bytes 1179648 | tf_op jit(solution)/shard_map/reduce_scatter | solution.py:88
  (13 other events, 26.2 us)
Sparse Core Ops, SparseCore 0:
  10.4 48.0 all-gather.2
  62.6 69.9 reduce-scatter.2
  190.4 41.1 all-gather.4
  250.0 120.8 all-reduce.8
  375.3 70.5 reduce-scatter.4
where the time goes:
time: 454 us; the launch traced here: 452 us
  waiting for transfers between devices  276 us (61%)
  blocking collectives  58.3 us (13%)
  matrix products  39.1 us (9%)
  starting transfers between devices  24.8 us (5%)
  other arithmetic  23.5 us (5%)
  local copies, waits for them, and re-layouts  16.9 us (4%)
  between operations  14.4 us (3%)
    psum x1, waiting for transfers between devices, body(): lax.psum(first_grad.astype(jnp.bfloat16), 'rows').astype(jnp.float32)  113 us
    reduce_scatter x2, waiting for transfers between devices, input_grad(): lax.psum_scatter(transpose_local(weight, padded, strip_rows, strip_cols)....  94.1 us
    all_gather x2, waiting for transfers between devices, widen(): gathered = lax.all_gather(values, 'ch', axis=0, tiled=True)  64.9 us
    psum x1, blocking collectives, body(): lax.psum((jnp.sum(pre_grad * normed, axis=1), jnp.sum(pre_grad, axis=1)),...  29.7 us
    psum x1, blocking collectives, body(): lax.psum((jnp.sum(grouped, axis=1), jnp.sum(grouped * grouped, axis=1)),...  28.6 us
    dot_general x18, matrix products, transpose_local(): lax.dot_general(weight[row_tap, col_tap], slab, (((0,), (0,)), ((), ())),...  21 us
    dot_general x18, matrix products, filter_local(): lax.dot_general(gradient, slab, (((1,), (1,)), ((), ())), preferred_eleme...  14 us
    ppermute x4, starting transfers between devices, with_halo(): after = lax.ppermute(initial, axis, down)  12.7 us
  transfers between devices with their start and end apart: 13, of which 6 were waited for; matrix products, arithmetic and copies ran while one was open for 11% of the time, Pallas kernels for 0%

commit v1 on v0

v1 whole, which is shorter than its diff:
```python
import functools

import jax
import jax.numpy as jnp
from jax import lax
from jax.experimental import pallas as pl
from jax.experimental.pallas import tpu as pltpu
from jax.sharding import PartitionSpec as P

C = 512
G = 32
EPS = 1e-06
ROWS = 8
W = 128
OWN = 64
TAPS = 9
STACK = TAPS * OWN
PIECE = 144
BF = jnp.bfloat16
F32 = jnp.float32

VMEM = pl.BlockSpec(memory_space=pltpu.VMEM)
SMEM = pl.BlockSpec(memory_space=pltpu.SMEM)

CH_SHIFTS = ((0, 0), (1, 0), (0, 1), (0, 3), (0, 2), (1, 1), (1, 3), (1, 2))


def ch_pairs(dx, dy):
    return [(i, ((i // 4 + dx) % 2) * 4 + (i % 4 + dy) % 4) for i in range(8)]


def row_pairs(dz, dx, dc):
    pairs = []
    for i in range(16):
        z, x, c = i // 4, (i // 2) % 2, i % 2
        pairs.append((i, ((z + dz) % 4) * 4 + ((x + dx) % 2) * 2 + (c + dc) % 2))
    return pairs


def call(kernel, out, *args, flops=0, name=None):
    moved = sum(a.size * a.dtype.itemsize for a in args)
    shapes = [jax.ShapeDtypeStruct(s, d) for s, d in out["shapes"]]
    moved += sum(s.size * s.dtype.itemsize for s in shapes)
    return pl.pallas_call(
        kernel,
        out_shape=shapes,
        in_specs=[SMEM if a.dtype == jnp.int32 else VMEM for a in args],
        out_specs=[VMEM] * len(shapes),
        scratch_shapes=out.get("scratch", ()),
        compiler_params=pltpu.CompilerParams(vmem_limit_bytes=40 * 1024 * 1024),
        cost_estimate=pl.CostEstimate(flops=flops, bytes_accessed=moved, transcendentals=0),
        name=name,
    )(*args)


def shifted_cols(v, by):
    lane = lax.broadcasted_iota(jnp.int32, v.shape, 1)
    rolled = pltpu.roll(v, by % W, 1)
    return jnp.where(lane == (0 if by == 1 else W - 1), 0.0, rolled)


def source_of(at, shift):
    dx, dy = shift
    return lax.rem(at[0] + dx, 2) * 4 + lax.rem(at[1] + 4 - dy, 4)


def target_of(at, shift):
    dx, dy = shift
    return lax.rem(at[0] + dx, 2) * 4 + lax.rem(at[1] + dy, 4)


def assemble(at, pieces, full):
    for shift, piece in zip(CH_SHIFTS, pieces):
        place = pl.multiple_of(source_of(at, shift) * OWN, OWN)
        full[:, pl.ds(place, OWN), :] = piece[...]


def conv_kernel(at, *refs):
    pieces, (w, hid, top, bottom, full, acc) = refs[:8], refs[8:]
    assemble(at, pieces, full)
    acc[...] = jnp.zeros_like(acc)
    for j in range(ROWS // 2):
        pair = jnp.concatenate([full[2 * j], full[2 * j + 1]], axis=1)
        v = jnp.dot(w[...], pair, preferred_element_type=F32)
        for a in range(3):
            for b in range(3):
                for k in range(2):
                    o = (a * 3 + b) * OWN
                    acc[b, 2 * j + k - a + 2] += v[o : o + OWN, k * W : (k + 1) * W]
    for r in range(ROWS + 2):
        row = acc[1, r] + shifted_cols(acc[0, r], 1) + shifted_cols(acc[2, r], -1)
        if r == 0:
            top[...] = row
        elif r == ROWS + 1:
            bottom[...] = row
        else:
            hid[r - 1] = row


def stats_kernel(hid, above, below, out, stats):
    total = jnp.zeros((OWN, W), F32)
    square = jnp.zeros((OWN, W), F32)
    for r in range(ROWS):
        row = hid[r]
        if r == 0:
            row = row + above[...]
        if r == ROWS - 1:
            row = row + below[...]
        out[r] = row
        total = total + row
        square = square + row * row
    both = jnp.concatenate([total, square], axis=0)
    sums = jnp.sum(jnp.sum(both.reshape(8, OWN // 4, W), axis=1), axis=1, keepdims=True)
    stats[...] = jnp.broadcast_to(sums, (8, W))


def per_channel(groups):
    return jnp.broadcast_to(groups[:, None, :], (4, OWN // 4, W)).reshape(OWN, W)


def norm_of(stats, cells):
    mean = stats[0:4] / cells
    var = stats[4:8] / cells - mean * mean
    return per_channel(mean), per_channel(lax.rsqrt(var + EPS))


def act_kernel(cells, hid, stats, gain, shift, act):
    mean, scale = norm_of(stats[...], cells)
    for r in range(ROWS):
        normed = (hid[r] - mean) * scale
        s = normed * gain[...] + shift[...]
        act[r] = (s * jax.nn.sigmoid(s)).astype(BF)


def pre_kernel(cells, hid, stats, gain, shift, p0, p1, p2, p3, p4, pre, sums):
    mean, scale = norm_of(stats[...], cells)
    by_normed = jnp.zeros((OWN, W), F32)
    plain = jnp.zeros((OWN, W), F32)
    for r in range(ROWS):
        normed = (hid[r] - mean) * scale
        s = normed * gain[...] + shift[...]
        q = jax.nn.sigmoid(s)
        act_grad = p0[r].astype(F32)
        for p in (p1, p2, p3, p4):
            act_grad = act_grad + p[r].astype(F32)
        value = act_grad * q * (1.0 + s * (1.0 - q))
        pre[r] = value
        by_normed = by_normed + value * normed
        plain = plain + value
    both = jnp.concatenate([by_normed, plain], axis=0).T
    sums[...] = jnp.broadcast_to(jnp.sum(both, axis=0, keepdims=True), (8, W))


def hidden_grad_kernel(cells, hid, stats, gain, pre, sums, out):
    mean, scale = norm_of(stats[...], cells)
    spread = jnp.broadcast_to(sums[0:1, :], (W, W)).T
    by_normed, plain = spread[:OWN], spread[OWN:]

    def group_mean(v):
        return per_channel(jnp.sum((gain[...] * v).reshape(4, OWN // 4, W), axis=1) / cells)

    first, second = group_mean(plain), group_mean(by_normed)
    for r in range(ROWS):
        normed = (hid[r] - mean) * scale
        out[r] = (scale * (pre[r] * gain[...] - first - normed * second)).astype(BF)


def input_grad_kernel(at, grad, above, below, wt, stack, *rest):
    pieces, (cols, full) = rest[:8], rest[8:]
    for r in range(ROWS + 2):
        row = above[...] if r == 0 else below[...] if r == ROWS + 1 else grad[r - 1]
        wide = row.astype(F32)
        cols[0, r] = shifted_cols(wide, -1).astype(BF)
        cols[1, r] = row
        cols[2, r] = shifted_cols(wide, 1).astype(BF)
    for j in range(ROWS // 2):
        for a in range(3):
            for b in range(3):
                o = (a * 3 + b) * OWN
                for k in range(2):
                    y = 2 * j + k
                    stack[o : o + OWN, y * W : (y + 1) * W] = cols[b, y - a + 2]
        part = jnp.dot(
            wt[...], stack[:, 2 * j * W : (2 * j + 2) * W], preferred_element_type=F32
        ).astype(BF)
        full[2 * j] = part[:, :W]
        full[2 * j + 1] = part[:, W:]
    for shift, piece in zip(CH_SHIFTS, pieces):
        place = pl.multiple_of(target_of(at, shift) * OWN, OWN)
        piece[...] = full[:, pl.ds(place, OWN), :]


def filter_products(at, stack, full, keep, send):
    core = at[4]
    for q in range(4):
        cells = jnp.concatenate(
            [full[r, q * W : (q + 1) * W, :] for r in range(ROWS)], axis=1
        )
        part = lax.dot_general(
            stack[...], cells, (((1,), (1,)), ((), ())), preferred_element_type=F32
        ).astype(BF)
        mine = core == q // 2

        @pl.when(mine)
        def _():
            keep[(q % 2) * STACK : (q % 2 + 1) * STACK, :] = part

        @pl.when(jnp.logical_not(mine))
        def _():
            send[(q % 2) * STACK : (q % 2 + 1) * STACK, :] = part


def filter_kernel(at, stack, full, keep, send):
    filter_products(at, stack, full, keep, send)


def gathered_filter_kernel(at, stack, *refs):
    pieces, (keep, send, full) = refs[:8], refs[8:]
    assemble(at, pieces, full)
    filter_products(at, stack, full, keep, send)


def core_sum_kernel(at, k1, r1, k2, r2, near, far):
    for n, (k, r) in enumerate(((k1, r1), (k2, r2))):
        for dx, out in ((0, near), (1, far)):
            for dz in range(4):
                p = lax.rem(at[3] + dx, 2) * 4 + lax.rem(at[2] + dz, 4)
                at_row = pl.ds(pl.multiple_of(p * PIECE, PIECE), PIECE)
                out[dz, n] = (k[at_row, :].astype(F32) + r[at_row, :].astype(F32)).astype(BF)


def pair_sum_kernel(near, far, z0, z1, z2, z3):
    for dz, out in enumerate((z0, z1, z2, z3)):
        out[...] = (near[dz].astype(F32) + far[dz].astype(F32)).astype(BF)


def four_sum_kernel(a, b, c, d, out):
    total = a[...].astype(F32) + b[...].astype(F32) + c[...].astype(F32) + d[...].astype(F32)
    out[...] = total.astype(BF)


def sum_four(a, b, c, d, name):
    return call(four_sum_kernel, dict(shapes=[(a.shape, BF)]), a, b, c, d, name=name)[0]


def place_kernel(at, mine, other, first, second):
    for half, src in ((0, mine), (1, other)):
        core = lax.rem(at[4] + half, 2)
        for k, (dz, dx) in enumerate(AG_ORDER):
            z, x = lax.rem(at[2] + 4 - dz, 4), lax.rem(at[3] + dx, 2)
            rows = pl.ds(pl.multiple_of(z * PIECE, PIECE), PIECE)
            lanes = pl.ds(pl.multiple_of((core * 2 + x) * W, W), W)
            first[rows, lanes] = src[k, 0].astype(F32)
            second[rows, lanes] = src[k, 1].astype(F32)


AG_ORDER = ((0, 0), (0, 1), (2, 0), (1, 0), (3, 0), (2, 1), (1, 1), (3, 1))


def gather_ch(value):
    other = lax.ppermute(value, "ch", ch_pairs(1, 0))
    near = [lax.ppermute(value, "ch", ch_pairs(0, k)) for k in (1, 3, 2)]
    far = [lax.ppermute(other, "ch", ch_pairs(0, k)) for k in (1, 3, 2)]
    return [value, other, *near, *far]


def scatter_ch(pieces, name):
    far = [lax.ppermute(p, "ch", ch_pairs(0, k)) for k, p in zip((1, 3, 2), pieces[5:8])]
    near = [lax.ppermute(p, "ch", ch_pairs(0, k)) for k, p in zip((1, 3, 2), pieces[2:5])]
    total = sum_four(pieces[1], *far, name=name)
    other = lax.ppermute(total, "ch", ch_pairs(1, 0))
    return [pieces[0], *near, other]


def neighbours(first, last):
    up = [(i, i + 1) for i in range(15)]
    down = [(i + 1, i) for i in range(15)]
    return lax.ppermute(last, "rows", up), lax.ppermute(first, "rows", down)


def sum_rows(value):
    for dz, dx, dc in ((0, 0, 1), (0, 1, 0)):
        value = value + lax.ppermute(value, "rows", row_pairs(dz, dx, dc))
    for bit in (4, 8):
        value = value + lax.ppermute(value, "rows", [(i, i ^ bit) for i in range(16)])
    return value


def final_kernel(p0, p1, p2, p3, p4, out):
    for r in range(ROWS):
        total = p0[r].astype(F32)
        for p in (p1, p2, p3, p4):
            total = total + p[r].astype(F32)
        out[r] = total.astype(BF)


def input_grad(at, grad, wt, name):
    above, below = neighbours(grad[0], grad[ROWS - 1])
    outs = call(
        input_grad_kernel,
        dict(
            shapes=[((STACK, ROWS * W), BF)] + [((ROWS, OWN, W), BF)] * 8,
            scratch=[pltpu.VMEM((3, ROWS + 2, OWN, W), BF), pltpu.VMEM((ROWS, C, W), BF)],
        ),
        at, grad, above, below, wt,
        flops=2 * STACK * C * ROWS * W,
        name=name,
    )
    return outs[0], outs[1:]


def body(x_band, first_filter, second_filter, norm_gain, norm_shift, out_cotangent):
    cells = float((C // G) * ROWS * lax.axis_size("rows") * W)
    ch, rows = lax.axis_index("ch"), lax.axis_index("rows")
    at = jnp.stack([ch // 4, ch % 4, rows // 4, (rows // 2) % 2, rows % 2]).astype(jnp.int32)
    x_rows = jnp.transpose(x_band, (1, 0, 2))
    cot_rows = jnp.transpose(out_cotangent, (1, 0, 2))
    w1 = first_filter.reshape(STACK, C)
    w1t, w2t = w1.T, second_filter.reshape(STACK, C).T
    gain = jnp.broadcast_to(norm_gain[:, None], (OWN, W))
    shift = jnp.broadcast_to(norm_shift[:, None], (OWN, W))
    strip = (ROWS, OWN, W)

    x_pieces = gather_ch(x_rows)
    cot_stack, act_pieces = input_grad(at, cot_rows, w2t, "act_grad")
    hid, top, bottom, x_full = call(
        conv_kernel,
        dict(
            shapes=[(strip, F32), ((OWN, W), F32), ((OWN, W), F32), ((ROWS, C, W), BF)],
            scratch=[pltpu.VMEM((3, ROWS + 2, OWN, W), F32)],
        ),
        at, *x_pieces, w1,
        flops=2 * STACK * C * ROWS * W,
        name="hidden",
    )
    above, below = neighbours(top, bottom)
    hid, stats = call(
        stats_kernel, dict(shapes=[(strip, F32), ((8, W), F32)]), hid, above, below, name="stats"
    )
    act_parts = scatter_ch(act_pieces, "act_grad_sum")
    stats = sum_rows(stats)
    (act,) = call(
        functools.partial(act_kernel, cells), dict(shapes=[(strip, BF)]),
        hid, stats, gain, shift, name="activation",
    )
    pre, sums = call(
        functools.partial(pre_kernel, cells), dict(shapes=[(strip, F32), ((8, W), F32)]),
        hid, stats, gain, shift, *act_parts, name="pre_grad",
    )
    sums = sum_rows(sums)
    act_all = gather_ch(act)
    (hidden_grad,) = call(
        functools.partial(hidden_grad_kernel, cells), dict(shapes=[(strip, BF)]),
        hid, stats, gain, pre, sums, name="hidden_grad",
    )
    half = ((2 * STACK, W), BF)
    keep2, send2 = call(
        gathered_filter_kernel,
        dict(shapes=[half, half], scratch=[pltpu.VMEM((ROWS, C, W), BF)]),
        at, cot_stack, *act_all,
        flops=2 * STACK * C * ROWS * W,
        name="second_grad",
    )
    recv2 = lax.ppermute(send2, "rows", row_pairs(0, 0, 1))
    hg_stack, band_pieces = input_grad(at, hidden_grad, w1t, "band_grad")
    band_parts = scatter_ch(band_pieces, "band_grad_sum")
    keep1, send1 = call(
        filter_kernel, dict(shapes=[half, half]), at, hg_stack, x_full,
        flops=2 * STACK * C * ROWS * W, name="first_grad",
    )
    recv1 = lax.ppermute(send1, "rows", row_pairs(0, 0, 1))
    share = (2, PIECE, W)
    near, far = call(
        core_sum_kernel, dict(shapes=[((4, *share), BF)] * 2), at, keep1, recv1, keep2, recv2, name="core_sum"
    )
    far = lax.ppermute(far, "rows", row_pairs(0, 1, 0))
    zs = call(pair_sum_kernel, dict(shapes=[(share, BF)] * 4), near, far, name="pair_sum")
    got = [lax.ppermute(zs[k], "rows", row_pairs(k, 0, 0)) for k in (2, 1, 3)]
    done = sum_four(zs[0], *got, name="filter_sum")
    other = lax.ppermute(done, "rows", row_pairs(0, 1, 0))
    got = [lax.ppermute(done, "rows", row_pairs(k, 0, 0)) for k in (2, 1, 3)]
    got += [lax.ppermute(other, "rows", row_pairs(k, 0, 0)) for k in (2, 1, 3)]
    mine = jnp.stack([done, other, *got])
    theirs = lax.ppermute(mine, "rows", row_pairs(0, 0, 1))
    first_grad, second_grad = call(
        place_kernel, dict(shapes=[((STACK, C), F32)] * 2), at, mine, theirs, name="filter_grads"
    )
    (band,) = call(final_kernel, dict(shapes=[(strip, BF)]), *band_parts, name="band_grad_total")
    shape = (3, 3, OWN, C)
    return (
        jnp.transpose(band, (1, 0, 2)),
        first_grad.reshape(shape),
        second_grad.reshape(shape),
        sums[0, :OWN],
        sums[0, OWN:],
    )


def solution(mesh):
    filters = P(None, None, "ch", None)
    strip = P("ch", "rows", None)
    return jax.shard_map(
        body,
        mesh=mesh,
        in_specs=(strip, filters, filters, P("ch"), P("ch"), strip),
        out_specs=(strip, filters, filters, P("ch"), P("ch")),
        check_vma=False,
    )
```

time: 454 us -> 161 us (0.35)
  waiting for transfers between devices: 276 us -> 34.3 us
  starting transfers between devices: 24.8 us -> 101 us
  blocking collectives: 58.3 us -> 0 us
  matrix products: 39.1 us -> 0 us
  other arithmetic: 23.5 us -> 0.03 us
  Pallas kernels: 0 us -> 16.2 us
  between operations: 14.4 us -> 1.04 us
  local copies, waits for them, and re-layouts: 16.9 us -> 6.19 us
    psum x1 -> x0, waiting for transfers between devices: 113 us -> none  [body(): lax.psum(first_grad.astype(jnp.bfloat16), 'rows').astype(jnp.float32)]
    reduce_scatter x2 -> x0, waiting for transfers between devices: 94.1 us -> none  [input_grad(): lax.psum_scatter(transpose_local(weight, padded, strip_rows, strip_cols)....]
    ppermute x8 -> x56, starting transfers between devices: 24.3 us -> 101 us  [the longest x6 20.9 us: neighbours(): return (lax.ppermute(last, 'rows', up), lax.ppermute(first, 'rows', down))]
    all_gather x2 -> x0, waiting for transfers between devices: 64.9 us -> none  [widen(): gathered = lax.all_gather(values, 'ch', axis=0, tiled=True)]
    psum x2 -> x0, blocking collectives: 58.3 us -> none  [the longest x1 29.7 us: body(): lax.psum((jnp.sum(pre_grad * normed, axis=1), jnp.sum(pre_grad, axis=1)),...]
    dot_general x45 -> x0, matrix products: 39.1 us -> none  [the longest x18 21 us: transpose_local(): lax.dot_general(weight[row_tap, col_tap], slab, (((0,), (0,)), ((), ())),...]
    ppermute x8 -> x56, waiting for transfers between devices: 2.7 us -> 34.3 us  [the longest x1 7.08 us: body(): far = lax.ppermute(far, 'rows', row_pairs(0, 1, 0))]
    pallas_call x0 -> x16, Pallas kernels: none -> 16.2 us  [call(): pl.pallas_call(kernel, out_shape=shapes, in_specs=[SMEM if a.dtype == jnp...]
  transfers between devices with their start and end apart: 13 -> 56, of which waited for: 6 -> 21; matrix products, arithmetic and copies ran while one was open for 11% -> 3% of each run, Pallas kernels for 0% -> 8%
where the time goes in v1:
time: 161 us; the launch traced here: 159 us
  starting transfers between devices  101 us (63%)
  waiting for transfers between devices  34.3 us (21%)
  Pallas kernels  16.2 us (10%)
  local copies, waits for them, and re-layouts  6.19 us (4%)
    ppermute x6, starting transfers between devices, neighbours(): return (lax.ppermute(last, 'rows', up), lax.ppermute(first, 'rows', down))  20.9 us
    ppermute x12, starting transfers between devices, scatter_ch(): lax.ppermute(p, 'ch', ch_pairs(0, k))  16.9 us
    pallas_call x16, Pallas kernels, call(): pl.pallas_call(kernel, out_shape=shapes, in_specs=[SMEM if a.dtype == jnp...  16.2 us
    ppermute x6, starting transfers between devices, gather_ch(): far = [lax.ppermute(other, 'ch', ch_pairs(0, k)) for k in (1, 3, 2)]  9.61 us
    ppermute x4, starting transfers between devices, sum_rows(): value = value + lax.ppermute(value, 'rows', row_pairs(dz, dx, dc))  9.54 us
    ppermute x6, starting transfers between devices, gather_ch(): near = [lax.ppermute(value, 'ch', ch_pairs(0, k)) for k in (1, 3, 2)]  8.76 us
    ppermute x4, starting transfers between devices, sum_rows(): lax.ppermute(value, 'rows', [(i, i ^ bit) for i in range(16)])  7.6 us
    ppermute x1, waiting for transfers between devices, body(): far = lax.ppermute(far, 'rows', row_pairs(0, 1, 0))  7.08 us
  transfers between devices with their start and end apart: 56, of which 21 were waited for; matrix products, arithmetic and copies ran while one was open for 3% of the time, Pallas kernels for 8%

profile of v1, /device:TPU:1, one launch (start us, length us, event | category | flops | bytes accessed | tf_op | source)
XLA Modules:
  0.0 159.1 jit_solution(17401007102217365028)
XLA Ops:
  1.6 4.5 %collective-permute-start.13 = (bf16[64,128]{1,0:T(8,128)(2,1)S(1)}, bf16[64,128]{1,0:T(8,128)(2,1)S(1)}, u32[]{:S(2)}, u32[]{:S(2)}) collective-permute-start(bf16[64,128]{1,0:T(8,128)(2,1)S(1)} %get-tuple-element.94), channel_id=1, source_target_pairs={{0,8},{8,16},{16,24},{24,32},{32,40},{40,48},{48,56},{56,64},{64,7... | collective-permute-start | bytes 49160 | tf_op jit(solution)/shard_map/ppermute | solution.py:278
  8.9 2.5 %collective-permute-start = (bf16[8,64,128]{2,1,0:T(8,128)(2,1)S(1)}, bf16[8,64,128]{2,1,0:T(8,128)(2,1)S(1)}, u32[]{:S(2)}, u32[]{:S(2)}) collective-permute-start(bf16[8,64,128]{2,1,0:T(8,128)(2,1)S(1)} %bitcast.53), channel_id=1, source_target_pairs={{0,4},{1,5},{2,6},{3,7},{4,0},{5,1},{6,2},{7,3},{8,12},{9,13},{10,... | collective-permute-start | bytes 393224 | tf_op jit(solution)/shard_map/ppermute | solution.py:261
  23.6 5.3 %collective-permute-start.5 = (bf16[8,64,128]{2,1,0:T(8,128)(2,1)S(1)}, bf16[8,64,128]{2,1,0:T(8,128)(2,1)S(1)}, u32[]{:S(2)}, u32[]{:S(2)}) collective-permute-start(bf16[8,64,128]{2,1,0:T(8,128)(2,1)S(1)} %collective-permute-done.refs_1_), channel_id=1, source_target_pairs={{0,3},{1,0},{2,1},{3,2},{4,7},{5,4},{6,5},{7,6},{8,11},{9,8},{10,9... | collective-permute-start | bytes 393224 | tf_op jit(solution)/shard_map/ppermute | solution.py:263
  29.6 3.7 %collective-permute-start.15 = (bf16[8,64,128]{2,1,0:T(8,128)(2,1)S(1)}, bf16[8,64,128]{2,1,0:T(8,128)(2,1)S(1)}, u32[]{:S(2)}, u32[]{:S(2)}) collective-permute-start(bf16[8,64,128]{2,1,0:T(8,128)(2,1)S(1)} %get-tuple-element.49), channel_id=1, source_target_pairs={{0,1},{1,2},{2,3},{3,0},{4,5},{5,6},{6,7},{7,4},{8,9},{9,10},{10,1... | collective-permute-start | bytes 393224 | tf_op jit(solution)/shard_map/ppermute | solution.py:269
  37.5 5.9 %collective-permute-start.7 = (f32[64,128]{1,0:T(8,128)S(1)}, f32[64,128]{1,0:T(8,128)S(1)}, u32[]{:S(2)}, u32[]{:S(2)}) collective-permute-start(f32[64,128]{1,0:T(8,128)S(1)} %get-tuple-element.44), channel_id=1, source_target_pairs={{0,8},{8,16},{16,24},{24,32},{32,40},{40,48},{48,56},{56,64},{64,7... | collective-permute-start | bytes 98312 | tf_op jit(solution)/shard_map/ppermute | solution.py:278
  46.3 3.9 %collective-permute-done.8.below = f32[64,128]{1,0:T(8,128)S(1)} collective-permute-done((f32[64,128]{1,0:T(8,128)S(1)}, f32[64,128]{1,0:T(8,128)S(1)}, u32[]{:S(2)}, u32[]{:S(2)}) %collective-permute-start.8) | collective-permute-done | bytes 32800 | tf_op jit(solution)/shard_map/ppermute | solution.py:278
  51.5 4.4 %collective-permute-start.10 = (f32[8,128]{1,0:T(8,128)S(1)}, f32[8,128]{1,0:T(8,128)S(1)}, u32[]{:S(2)}, u32[]{:S(2)}) collective-permute-start(f32[8,128]{1,0:T(8,128)S(1)} %add.40), channel_id=1, source_target_pairs={{0,16},{8,24},{16,0},{24,8},{32,48},{40,56},{48,32},{56,40},{64,80... | collective-permute-start | bytes 12296 | tf_op jit(solution)/shard_map/ppermute | solution.py:283
  59.3 2.7 %collective-permute-start.12 = (f32[8,128]{1,0:T(8,128)S(1)}, f32[8,128]{1,0:T(8,128)S(1)}, u32[]{:S(2)}, u32[]{:S(2)}) collective-permute-start(f32[8,128]{1,0:T(8,128)S(1)} %add.42), channel_id=1, source_target_pairs={{0,64},{8,72},{16,80},{24,88},{32,96},{40,104},{48,112},{56,120},{... | collective-permute-start | bytes 12296 | tf_op jit(solution)/shard_map/ppermute | solution.py:285
  63.8 3.4 %collective-permute-start.22 = (f32[8,128]{1,0:T(8,128)S(1)}, f32[8,128]{1,0:T(8,128)S(1)}, u32[]{:S(2)}, u32[]{:S(2)}) collective-permute-start(f32[8,128]{1,0:T(8,128)S(1)} %get-tuple-element.57), channel_id=1, source_target_pairs={{0,8},{8,0},{16,24},{24,16},{32,40},{40,32},{48,56},{56,48},{64,72... | collective-permute-start | bytes 12296 | tf_op jit(solution)/shard_map/ppermute | solution.py:283
  73.2 2.7 %collective-permute-start.25 = (f32[8,128]{1,0:T(8,128)S(1)}, f32[8,128]{1,0:T(8,128)S(1)}, u32[]{:S(2)}, u32[]{:S(2)}) collective-permute-start(f32[8,128]{1,0:T(8,128)S(1)} %add.46), channel_id=1, source_target_pairs={{0,64},{8,72},{16,80},{24,88},{32,96},{40,104},{48,112},{56,120},{... | collective-permute-start | bytes 12296 | tf_op jit(solution)/shard_map/ppermute | solution.py:285
  80.2 4.8 %collective-permute-start.26 = (bf16[64,128]{1,0:T(8,128)(2,1)S(1)}, bf16[64,128]{1,0:T(8,128)(2,1)S(1)}, u32[]{:S(2)}, u32[]{:S(2)}) collective-permute-start(bf16[64,128]{1,0:T(8,128)(2,1)S(1)} %get-tuple-element.92), channel_id=1, source_target_pairs={{0,8},{8,16},{16,24},{24,32},{32,40},{40,48},{48,56},{56,64},{64,7... | collective-permute-start | bytes 49160 | tf_op jit(solution)/shard_map/ppermute | solution.py:278
  86.9 2.6 %collective-permute-start.38 = (bf16[8,64,128]{2,1,0:T(8,128)(2,1)S(1)}, bf16[8,64,128]{2,1,0:T(8,128)(2,1)S(1)}, u32[]{:S(2)}, u32[]{:S(2)}) collective-permute-start(bf16[8,64,128]{2,1,0:T(8,128)(2,1)S(1)} %activation.1.refs_0_), channel_id=1, source_target_pairs={{0,3},{1,0},{2,1},{3,2},{4,7},{5,4},{6,5},{7,6},{8,11},{9,8},{10,9... | collective-permute-start | bytes 393224 | tf_op jit(solution)/shard_map/ppermute | solution.py:262
  90.9 2.7 %collective-permute-start.41 = (bf16[8,64,128]{2,1,0:T(8,128)(2,1)S(1)}, bf16[8,64,128]{2,1,0:T(8,128)(2,1)S(1)}, u32[]{:S(2)}, u32[]{:S(2)}) collective-permute-start(bf16[8,64,128]{2,1,0:T(8,128)(2,1)S(1)} %collective-permute-done.36.refs_1_), channel_id=1, source_target_pairs={{0,3},{1,0},{2,1},{3,2},{4,7},{5,4},{6,5},{7,6},{8,11},{9,8},{10,9... | collective-permute-start | bytes 393224 | tf_op jit(solution)/shard_map/ppermute | solution.py:263
  96.1 3.6 %first_grad.1 = (bf16[1152,128]{1,0:T(8,128)(2,1)S(1)}, bf16[1152,128]{1,0:T(8,128)(2,1)S(1)}) custom-call(s32[5]{0:T(128)S(1)} %stack.50.at, bf16[576,1024]{1,0:T(8,128)(2,1)S(1)} %get-tuple-element.66.stack, bf16[8,512,128]{2,1,0:T(8,128)(2,1)S(1)} %get-tuple-element.67.full), custom_call_target="tpu_custom_call" | custom-call | flops 603979776 | bytes 2818068 | tf_op jit(solution)/shard_map/first_grad/pallas_call | solution.py:44
  100.3 3.7 %second_grad.1 = (bf16[1152,128]{1,0:T(8,128)(2,1)S(1)}, bf16[1152,128]{1,0:T(8,128)(2,1)S(1)}) custom-call(s32[5]{0:T(128)S(1)} %stack.50.at, bf16[576,1024]{1,0:T(8,128)(2,1)S(1)} %copy-done.2, bf16[8,64,128]{2,1,0:T(8,128)(2,1)S(1)} %activation.1.refs_0_, bf16[8,64,128]{2,1,0:T(8,128)(2,1)S(1)} %collective-permute-done.36.refs_1_, ...), custom_call_target="tpu_custom_call" | custom-call | flops 603979776 | bytes 2818068 | tf_op jit(solution)/shard_map/second_grad/pallas_call | solution.py:44
  106.4 2.9 %collective-permute-start.44 = (bf16[4,2,144,128]{3,2,1,0:T(8,128)(2,1)S(1)}, bf16[4,2,144,128]{3,2,1,0:T(8,128)(2,1)S(1)}, u32[]{:S(2)}, u32[]{:S(2)}) collective-permute-start(bf16[4,2,144,128]{3,2,1,0:T(8,128)(2,1)S(1)} %get-tuple-element.74), channel_id=1, source_target_pairs={{0,16},{8,24},{16,0},{24,8},{32,48},{40,56},{48,32},{56,40},{64,80... | collective-permute-start | bytes 884744 | tf_op jit(solution)/shard_map/ppermute | solution.py:376
  109.3 7.1 %collective-permute-done.44.far = bf16[4,2,144,128]{3,2,1,0:T(8,128)(2,1)S(1)} collective-permute-done((bf16[4,2,144,128]{3,2,1,0:T(8,128)(2,1)S(1)}, bf16[4,2,144,128]{3,2,1,0:T(8,128)(2,1)S(1)}, u32[]{:S(2)}, u32[]{:S(2)}) %collective-permute-start.44) | collective-permute-done | bytes 294944 | tf_op jit(solution)/shard_map/ppermute | solution.py:376
  116.4 3.5 %collective-permute-start.45 = (bf16[2,144,128]{2,1,0:T(8,128)(2,1)S(1)}, bf16[2,144,128]{2,1,0:T(8,128)(2,1)S(1)}, u32[]{:S(2)}, u32[]{:S(2)}) collective-permute-start(bf16[2,144,128]{2,1,0:T(8,128)(2,1)S(1)} %get-tuple-element.76), channel_id=1, source_target_pairs={{0,64},{8,72},{16,80},{24,88},{32,96},{40,104},{48,112},{56,120},{... | collective-permute-start | bytes 221192 | tf_op jit(solution)/shard_map/ppermute | solution.py:378
  120.1 2.5 %collective-permute-start.47 = (bf16[2,144,128]{2,1,0:T(8,128)(2,1)S(1)}, bf16[2,144,128]{2,1,0:T(8,128)(2,1)S(1)}, u32[]{:S(2)}, u32[]{:S(2)}) collective-permute-start(bf16[2,144,128]{2,1,0:T(8,128)(2,1)S(1)} %get-tuple-element.78), channel_id=1, source_target_pairs={{0,96},{8,104},{16,112},{24,120},{32,0},{40,8},{48,16},{56,24},{64... | collective-permute-start | bytes 221192 | tf_op jit(solution)/shard_map/ppermute | solution.py:378
  131.0 2.4 %collective-permute-start.54 = (bf16[2,144,128]{2,1,0:T(8,128)(2,1)S(1)}, bf16[2,144,128]{2,1,0:T(8,128)(2,1)S(1)}, u32[]{:S(2)}, u32[]{:S(2)}) collective-permute-start(bf16[2,144,128]{2,1,0:T(8,128)(2,1)S(1)} %collective-permute-done.48), channel_id=1, source_target_pairs={{0,96},{8,104},{16,112},{24,120},{32,0},{40,8},{48,16},{56,24},{64... | collective-permute-start | bytes 221192 | tf_op jit(solution)/shard_map/ppermute | solution.py:382
  136.2 3.9 %collective-permute-start.55 = (bf16[8,2,144,128]{3,2,1,0:T(8,128)(2,1)S(1)}, bf16[8,2,144,128]{3,2,1,0:T(8,128)(2,1)S(1)}, u32[]{:S(2)}, u32[]{:S(2)}) collective-permute-start(bf16[8,2,144,128]{3,2,1,0:T(8,128)(2,1)S(1)} %bitcast_dynamic-update-slice_fusion.mine), channel_id=1, source_target_pairs={{0,8},{8,0},{16,24},{24,16},{32,40},{40,32},{48,56},{56,48},{64,72... | collective-permute-start | bytes 1769480 | tf_op jit(solution)/shard_map/ppermute | solution.py:384
  140.5 2.3 %collective-permute-start.32 = (bf16[8,64,128]{2,1,0:T(8,128)(2,1)S(1)}, bf16[8,64,128]{2,1,0:T(8,128)(2,1)S(1)}, u32[]{:S(2)}, u32[]{:S(2)}) collective-permute-start(bf16[8,64,128]{2,1,0:T(8,128)(2,1)S(1)} %get-tuple-element.64), channel_id=1, source_target_pairs={{0,3},{1,0},{2,1},{3,2},{4,7},{5,4},{6,5},{7,6},{8,11},{9,8},{10,9... | collective-permute-start | bytes 393224 | tf_op jit(solution)/shard_map/ppermute | solution.py:268
  152.7 2.3 %collective-permute-done.30.p3 = bf16[8,64,128]{2,1,0:T(8,128)(2,1)S(1)} collective-permute-done((bf16[8,64,128]{2,1,0:T(8,128)(2,1)S(1)}, bf16[8,64,128]{2,1,0:T(8,128)(2,1)S(1)}, u32[]{:S(2)}, u32[]{:S(2)}) %collective-permute-start.30) | collective-permute-done | bytes 131104 | tf_op jit(solution)/shard_map/ppermute | solution.py:269
  156.8 2.3 %filter_grads.1 = (f32[576,512]{1,0:T(8,128)}, f32[576,512]{1,0:T(8,128)}) custom-call(s32[5]{0:T(128)S(1)} %stack.50.at, bf16[8,2,144,128]{3,2,1,0:T(8,128)(2,1)S(1)} %bitcast_dynamic-update-slice_fusion.mine, bf16[8,2,144,128]{3,2,1,0:T(8,128)(2,1)S(1)} %collective-permute-done.55.other), custom_call_target="tpu_custom_call" | custom-call | bytes 3538964 | tf_op jit(solution)/shard_map/filter_grads/pallas_call | solution.py:44
  (141 shorter events, 72.6 us)
Async XLA Ops:
  1.6 12.7 %collective-permute-start.13 = (bf16[64,128]{1,0:T(8,128)(2,1)S(1)}, bf16[64,128]{1,0:T(8,128)(2,1)S(1)}, u32[]{:S(2)}, u32[]{:S(2)}) collective-permute-start(bf16[64,128]{1,0:T(8,128)(2,1)S(1)} %get-tuple-element.94), channel_id=1, source_target_pairs={{0,8},{8,16},{16,24},{24,32},{32,40},{40,48},{48,56},{56,64},{64,7... | collective-permute-start | bytes 49160 | tf_op jit(solution)/shard_map/ppermute | solution.py:278
  6.1 8.2 %collective-permute-start.14 = (bf16[64,128]{1,0:T(8,128)(2,1)S(1)}, bf16[64,128]{1,0:T(8,128)(2,1)S(1)}, u32[]{:S(2)}, u32[]{:S(2)}) collective-permute-start(bf16[64,128]{1,0:T(8,128)(2,1)S(1)} %get-tuple-element.93), channel_id=1, source_target_pairs={{8,0},{16,8},{24,16},{32,24},{40,32},{48,40},{56,48},{64,56},{72,6... | collective-permute-start | bytes 49160 | tf_op jit(solution)/shard_map/ppermute | solution.py:278
  8.9 12.2 %collective-permute-start = (bf16[8,64,128]{2,1,0:T(8,128)(2,1)S(1)}, bf16[8,64,128]{2,1,0:T(8,128)(2,1)S(1)}, u32[]{:S(2)}, u32[]{:S(2)}) collective-permute-start(bf16[8,64,128]{2,1,0:T(8,128)(2,1)S(1)} %bitcast.53), channel_id=1, source_target_pairs={{0,4},{1,5},{2,6},{3,7},{4,0},{5,1},{6,2},{7,3},{8,12},{9,13},{10,... | collective-permute-start | bytes 393224 | tf_op jit(solution)/shard_map/ppermute | solution.py:261
  11.5 10.7 %collective-permute-start.1 = (bf16[8,64,128]{2,1,0:T(8,128)(2,1)S(1)}, bf16[8,64,128]{2,1,0:T(8,128)(2,1)S(1)}, u32[]{:S(2)}, u32[]{:S(2)}) collective-permute-start(bf16[8,64,128]{2,1,0:T(8,128)(2,1)S(1)} %bitcast.54), channel_id=1, source_target_pairs={{0,1},{1,2},{2,3},{3,0},{4,5},{5,6},{6,7},{7,4},{8,9},{9,10},{10,1... | collective-permute-start | bytes 393224 | tf_op jit(solution)/shard_map/ppermute | solution.py:262
  19.7 9.1 %collective-permute-start.20 = (bf16[8,64,128]{2,1,0:T(8,128)(2,1)S(1)}, bf16[8,64,128]{2,1,0:T(8,128)(2,1)S(1)}, u32[]{:S(2)}, u32[]{:S(2)}) collective-permute-start(bf16[8,64,128]{2,1,0:T(8,128)(2,1)S(1)} %get-tuple-element.55), channel_id=1, source_target_pairs={{0,2},{1,3},{2,0},{3,1},{4,6},{5,7},{6,4},{7,5},{8,10},{9,11},{10,... | collective-permute-start | bytes 393224 | tf_op jit(solution)/shard_map/ppermute | solution.py:268
  21.2 8.4 %collective-permute-start.2 = (bf16[8,64,128]{2,1,0:T(8,128)(2,1)S(1)}, bf16[8,64,128]{2,1,0:T(8,128)(2,1)S(1)}, u32[]{:S(2)}, u32[]{:S(2)}) collective-permute-start(bf16[8,64,128]{2,1,0:T(8,128)(2,1)S(1)} %bitcast.55), channel_id=1, source_target_pairs={{0,3},{1,0},{2,1},{3,2},{4,7},{5,4},{6,5},{7,6},{8,11},{9,8},{10,9... | collective-permute-start | bytes 393224 | tf_op jit(solution)/shard_map/ppermute | solution.py:262
  22.2 11.1 %collective-permute-start.3 = (bf16[8,64,128]{2,1,0:T(8,128)(2,1)S(1)}, bf16[8,64,128]{2,1,0:T(8,128)(2,1)S(1)}, u32[]{:S(2)}, u32[]{:S(2)}) collective-permute-start(bf16[8,64,128]{2,1,0:T(8,128)(2,1)S(1)} %bitcast.56), channel_id=1, source_target_pairs={{0,2},{1,3},{2,0},{3,1},{4,6},{5,7},{6,4},{7,5},{8,10},{9,11},{10,... | collective-permute-start | bytes 393224 | tf_op jit(solution)/shard_map/ppermute | solution.py:262
  22.9 11.6 %collective-permute-start.4 = (bf16[8,64,128]{2,1,0:T(8,128)(2,1)S(1)}, bf16[8,64,128]{2,1,0:T(8,128)(2,1)S(1)}, u32[]{:S(2)}, u32[]{:S(2)}) collective-permute-start(bf16[8,64,128]{2,1,0:T(8,128)(2,1)S(1)} %collective-permute-done.refs_1_), channel_id=1, source_target_pairs={{0,1},{1,2},{2,3},{3,0},{4,5},{5,6},{6,7},{7,4},{8,9},{9,10},{10,1... | collective-permute-start | bytes 393224 | tf_op jit(solution)/shard_map/ppermute | solution.py:263
  23.6 12.1 %collective-permute-start.5 = (bf16[8,64,128]{2,1,0:T(8,128)(2,1)S(1)}, bf16[8,64,128]{2,1,0:T(8,128)(2,1)S(1)}, u32[]{:S(2)}, u32[]{:S(2)}) collective-permute-start(bf16[8,64,128]{2,1,0:T(8,128)(2,1)S(1)} %collective-permute-done.refs_1_), channel_id=1, source_target_pairs={{0,3},{1,0},{2,1},{3,2},{4,7},{5,4},{6,5},{7,6},{8,11},{9,8},{10,9... | collective-permute-start | bytes 393224 | tf_op jit(solution)/shard_map/ppermute | solution.py:263
  29.6 33.7 %collective-permute-start.15 = (bf16[8,64,128]{2,1,0:T(8,128)(2,1)S(1)}, bf16[8,64,128]{2,1,0:T(8,128)(2,1)S(1)}, u32[]{:S(2)}, u32[]{:S(2)}) collective-permute-start(bf16[8,64,128]{2,1,0:T(8,128)(2,1)S(1)} %get-tuple-element.49), channel_id=1, source_target_pairs={{0,1},{1,2},{2,3},{3,0},{4,5},{5,6},{6,7},{7,4},{8,9},{9,10},{10,1... | collective-permute-start | bytes 393224 | tf_op jit(solution)/shard_map/ppermute | solution.py:269
  33.3 30.0 %collective-permute-start.16 = (bf16[8,64,128]{2,1,0:T(8,128)(2,1)S(1)}, bf16[8,64,128]{2,1,0:T(8,128)(2,1)S(1)}, u32[]{:S(2)}, u32[]{:S(2)}) collective-permute-start(bf16[8,64,128]{2,1,0:T(8,128)(2,1)S(1)} %get-tuple-element.50), channel_id=1, source_target_pairs={{0,3},{1,0},{2,1},{3,2},{4,7},{5,4},{6,5},{7,6},{8,11},{9,8},{10,9... | collective-permute-start | bytes 393224 | tf_op jit(solution)/shard_map/ppermute | solution.py:269
  34.5 28.8 %collective-permute-start.17 = (bf16[8,64,128]{2,1,0:T(8,128)(2,1)S(1)}, bf16[8,64,128]{2,1,0:T(8,128)(2,1)S(1)}, u32[]{:S(2)}, u32[]{:S(2)}) collective-permute-start(bf16[8,64,128]{2,1,0:T(8,128)(2,1)S(1)} %get-tuple-element.51), channel_id=1, source_target_pairs={{0,2},{1,3},{2,0},{3,1},{4,6},{5,7},{6,4},{7,5},{8,10},{9,11},{10,... | collective-permute-start | bytes 393224 | tf_op jit(solution)/shard_map/ppermute | solution.py:269
  35.7 27.6 %collective-permute-start.21 = (bf16[8,64,128]{2,1,0:T(8,128)(2,1)S(1)}, bf16[8,64,128]{2,1,0:T(8,128)(2,1)S(1)}, u32[]{:S(2)}, u32[]{:S(2)}) collective-permute-start(bf16[8,64,128]{2,1,0:T(8,128)(2,1)S(1)} %act_grad_sum.1), channel_id=1, source_target_pairs={{0,4},{1,5},{2,6},{3,7},{4,0},{5,1},{6,2},{7,3},{8,12},{9,13},{10,... | collective-permute-start | bytes 393224 | tf_op jit(solution)/shard_map/ppermute | solution.py:271
  76.1 14.9 %collective-permute-start.36 = (bf16[8,64,128]{2,1,0:T(8,128)(2,1)S(1)}, bf16[8,64,128]{2,1,0:T(8,128)(2,1)S(1)}, u32[]{:S(2)}, u32[]{:S(2)}) collective-permute-start(bf16[8,64,128]{2,1,0:T(8,128)(2,1)S(1)} %activation.1.refs_0_), channel_id=1, source_target_pairs={{0,4},{1,5},{2,6},{3,7},{4,0},{5,1},{6,2},{7,3},{8,12},{9,13},{10,... | collective-permute-start | bytes 393224 | tf_op jit(solution)/shard_map/ppermute | solution.py:261
  78.2 15.4 %collective-permute-start.37 = (bf16[8,64,128]{2,1,0:T(8,128)(2,1)S(1)}, bf16[8,64,128]{2,1,0:T(8,128)(2,1)S(1)}, u32[]{:S(2)}, u32[]{:S(2)}) collective-permute-start(bf16[8,64,128]{2,1,0:T(8,128)(2,1)S(1)} %activation.1.refs_0_), channel_id=1, source_target_pairs={{0,1},{1,2},{2,3},{3,0},{4,5},{5,6},{6,7},{7,4},{8,9},{9,10},{10,1... | collective-permute-start | bytes 393224 | tf_op jit(solution)/shard_map/ppermute | solution.py:262
  80.2 9.3 %collective-permute-start.26 = (bf16[64,128]{1,0:T(8,128)(2,1)S(1)}, bf16[64,128]{1,0:T(8,128)(2,1)S(1)}, u32[]{:S(2)}, u32[]{:S(2)}) collective-permute-start(bf16[64,128]{1,0:T(8,128)(2,1)S(1)} %get-tuple-element.92), channel_id=1, source_target_pairs={{0,8},{8,16},{16,24},{24,32},{32,40},{40,48},{48,56},{56,64},{64,7... | collective-permute-start | bytes 49160 | tf_op jit(solution)/shard_map/ppermute | solution.py:278
  86.9 12.8 %collective-permute-start.38 = (bf16[8,64,128]{2,1,0:T(8,128)(2,1)S(1)}, bf16[8,64,128]{2,1,0:T(8,128)(2,1)S(1)}, u32[]{:S(2)}, u32[]{:S(2)}) collective-permute-start(bf16[8,64,128]{2,1,0:T(8,128)(2,1)S(1)} %activation.1.refs_0_), channel_id=1, source_target_pairs={{0,3},{1,0},{2,1},{3,2},{4,7},{5,4},{6,5},{7,6},{8,11},{9,8},{10,9... | collective-permute-start | bytes 393224 | tf_op jit(solution)/shard_map/ppermute | solution.py:262
  89.5 10.3 %collective-permute-start.39 = (bf16[8,64,128]{2,1,0:T(8,128)(2,1)S(1)}, bf16[8,64,128]{2,1,0:T(8,128)(2,1)S(1)}, u32[]{:S(2)}, u32[]{:S(2)}) collective-permute-start(bf16[8,64,128]{2,1,0:T(8,128)(2,1)S(1)} %activation.1.refs_0_), channel_id=1, source_target_pairs={{0,2},{1,3},{2,0},{3,1},{4,6},{5,7},{6,4},{7,5},{8,10},{9,11},{10,... | collective-permute-start | bytes 393224 | tf_op jit(solution)/shard_map/ppermute | solution.py:262
  90.9 8.9 %collective-permute-start.40 = (bf16[8,64,128]{2,1,0:T(8,128)(2,1)S(1)}, bf16[8,64,128]{2,1,0:T(8,128)(2,1)S(1)}, u32[]{:S(2)}, u32[]{:S(2)}) collective-permute-start(bf16[8,64,128]{2,1,0:T(8,128)(2,1)S(1)} %collective-permute-done.36.refs_1_), channel_id=1, source_target_pairs={{0,1},{1,2},{2,3},{3,0},{4,5},{5,6},{6,7},{7,4},{8,9},{9,10},{10,1... | collective-permute-start | bytes 393224 | tf_op jit(solution)/shard_map/ppermute | solution.py:263
  90.9 8.9 %collective-permute-start.41 = (bf16[8,64,128]{2,1,0:T(8,128)(2,1)S(1)}, bf16[8,64,128]{2,1,0:T(8,128)(2,1)S(1)}, u32[]{:S(2)}, u32[]{:S(2)}) collective-permute-start(bf16[8,64,128]{2,1,0:T(8,128)(2,1)S(1)} %collective-permute-done.36.refs_1_), channel_id=1, source_target_pairs={{0,3},{1,0},{2,1},{3,2},{4,7},{5,4},{6,5},{7,6},{8,11},{9,8},{10,9... | collective-permute-start | bytes 393224 | tf_op jit(solution)/shard_map/ppermute | solution.py:263
  106.4 10.0 %collective-permute-start.44 = (bf16[4,2,144,128]{3,2,1,0:T(8,128)(2,1)S(1)}, bf16[4,2,144,128]{3,2,1,0:T(8,128)(2,1)S(1)}, u32[]{:S(2)}, u32[]{:S(2)}) collective-permute-start(bf16[4,2,144,128]{3,2,1,0:T(8,128)(2,1)S(1)} %get-tuple-element.74), channel_id=1, source_target_pairs={{0,16},{8,24},{16,0},{24,8},{32,48},{40,56},{48,32},{56,40},{64,80... | collective-permute-start | bytes 884744 | tf_op jit(solution)/shard_map/ppermute | solution.py:376
  136.2 20.6 %collective-permute-start.55 = (bf16[8,2,144,128]{3,2,1,0:T(8,128)(2,1)S(1)}, bf16[8,2,144,128]{3,2,1,0:T(8,128)(2,1)S(1)}, u32[]{:S(2)}, u32[]{:S(2)}) collective-permute-start(bf16[8,2,144,128]{3,2,1,0:T(8,128)(2,1)S(1)} %bitcast_dynamic-update-slice_fusion.mine), channel_id=1, source_target_pairs={{0,8},{8,0},{16,24},{24,16},{32,40},{40,32},{48,56},{56,48},{64,72... | collective-permute-start | bytes 1769480 | tf_op jit(solution)/shard_map/ppermute | solution.py:384
  142.8 7.4 %collective-permute-start.33 = (bf16[8,64,128]{2,1,0:T(8,128)(2,1)S(1)}, bf16[8,64,128]{2,1,0:T(8,128)(2,1)S(1)}, u32[]{:S(2)}, u32[]{:S(2)}) collective-permute-start(bf16[8,64,128]{2,1,0:T(8,128)(2,1)S(1)} %get-tuple-element.65), channel_id=1, source_target_pairs={{0,2},{1,3},{2,0},{3,1},{4,6},{5,7},{6,4},{7,5},{8,10},{9,11},{10,... | collective-permute-start | bytes 393224 | tf_op jit(solution)/shard_map/ppermute | solution.py:268
  143.8 9.0 %collective-permute-start.28 = (bf16[8,64,128]{2,1,0:T(8,128)(2,1)S(1)}, bf16[8,64,128]{2,1,0:T(8,128)(2,1)S(1)}, u32[]{:S(2)}, u32[]{:S(2)}) collective-permute-start(bf16[8,64,128]{2,1,0:T(8,128)(2,1)S(1)} %get-tuple-element.59), channel_id=1, source_target_pairs={{0,1},{1,2},{2,3},{3,0},{4,5},{5,6},{6,7},{7,4},{8,9},{9,10},{10,1... | collective-permute-start | bytes 393224 | tf_op jit(solution)/shard_map/ppermute | solution.py:269
  (37 other events, 246.4 us)

commit v2 on v1

v2 whole, which is shorter than its diff:
```python
import functools

import jax
import jax.numpy as jnp
from jax import lax
from jax.experimental import pallas as pl
from jax.experimental.pallas import tpu as pltpu
from jax.sharding import PartitionSpec as P

C = 512
G = 32
EPS = 1e-06
ROWS = 8
W = 128
OWN = 64
TAPS = 9
STACK = TAPS * OWN
PIECE = 288
BF = jnp.bfloat16
F32 = jnp.float32

VMEM = pl.BlockSpec(memory_space=pltpu.VMEM)
SMEM = pl.BlockSpec(memory_space=pltpu.SMEM)

CH_SHIFTS = ((0, 0), (1, 0), (0, 1), (0, 3), (0, 2), (1, 1), (1, 3), (1, 2))


def after(value, other):
    return lax.optimization_barrier((value, other))[0]


def ch_pairs(dx, dy):
    return [(i, ((i // 4 + dx) % 2) * 4 + (i % 4 + dy) % 4) for i in range(8)]


def row_pairs(dz, dx, dc):
    pairs = []
    for i in range(16):
        z, x, c = i // 4, (i // 2) % 2, i % 2
        pairs.append((i, ((z + dz) % 4) * 4 + ((x + dx) % 2) * 2 + (c + dc) % 2))
    return pairs


GATES = (1, 0, 0, 4, 0, 0)
NG = (3, 0, 0, 0)
HINT = {'act_grad': 21, 'hidden': 26, 'act_grad_sum': 0, 'activation': 0, 'pre_grad': 0, 'second_grad': 0, 'band_grad': 0, 'first_grad': 0, 'band_grad_sum': 0, 'core_sum': 0, 'filter_sum': 0, 'pair_sum': 0, 'own_half': 10, 'other_half': 0, 'band_grad_total': 0}


def hint(name):
    return pl.CostEstimate(flops=int(HINT[name] * 1.15e9), bytes_accessed=0, transcendentals=0)


def call(kernel, out, *args, name=None):
    shapes = [jax.ShapeDtypeStruct(s, d) for s, d in out["shapes"]]
    return pl.pallas_call(
        kernel,
        out_shape=shapes,
        in_specs=[SMEM if a.dtype == jnp.int32 else VMEM for a in args],
        out_specs=[VMEM] * len(shapes),
        scratch_shapes=out.get("scratch", ()),
        compiler_params=pltpu.CompilerParams(vmem_limit_bytes=10 * 1024 * 1024),
        cost_estimate=hint(name),
        name=name,
    )(*args)


def shifted_cols(v, by):
    lane = lax.broadcasted_iota(jnp.int32, v.shape, 1)
    rolled = pltpu.roll(v, by % W, 1)
    return jnp.where(lane == (0 if by == 1 else W - 1), 0.0, rolled)


def source_of(at, shift):
    dx, dy = shift
    return lax.rem(at[0] + dx, 2) * 4 + lax.rem(at[1] + 4 - dy, 4)


def target_of(at, shift):
    dx, dy = shift
    return lax.rem(at[0] + dx, 2) * 4 + lax.rem(at[1] + dy, 4)


def assemble(at, pieces, full):
    for shift, piece in zip(CH_SHIFTS, pieces):
        place = pl.multiple_of(source_of(at, shift) * OWN, OWN)
        full[:, pl.ds(place, OWN), :] = piece[...]


def conv_kernel(at, *refs):
    pieces, (w, hid, stats, full, acc) = refs[:8], refs[8:]
    assemble(at, pieces, full)
    acc[...] = jnp.zeros_like(acc)
    for j in range(ROWS // 2 + 1):
        pair = jnp.concatenate([full[2 * j], full[2 * j + 1]], axis=1)
        v = jnp.dot(w[...], pair, preferred_element_type=F32)
        for a in range(3):
            for b in range(3):
                for k in range(2):
                    o = (a * 3 + b) * OWN
                    y = 2 * j + k - a
                    if 0 <= y < ROWS:
                        acc[b, y] += v[o : o + OWN, k * W : (k + 1) * W]
    total = jnp.zeros((OWN, W), F32)
    square = jnp.zeros((OWN, W), F32)
    for r in range(ROWS):
        row = acc[1, r] + shifted_cols(acc[0, r], 1) + shifted_cols(acc[2, r], -1)
        hid[r] = row
        total = total + row
        square = square + row * row
    both = jnp.concatenate([total, square], axis=0)
    sums = jnp.sum(jnp.sum(both.reshape(8, OWN // 4, W), axis=1), axis=1, keepdims=True)
    stats[...] = jnp.broadcast_to(sums, (8, W))


def per_channel(groups):
    return jnp.broadcast_to(groups[:, None, :], (4, OWN // 4, W)).reshape(OWN, W)


def norm_of(stats, cells):
    mean = stats[0:4] / cells
    var = stats[4:8] / cells - mean * mean
    return per_channel(mean), per_channel(lax.rsqrt(var + EPS))


def act_kernel(cells, hid, stats, gain, shift, act):
    mean, scale = norm_of(stats[...], cells)
    for r in range(ROWS):
        normed = (hid[r] - mean) * scale
        s = normed * gain[...] + shift[...]
        act[r] = (s * jax.nn.sigmoid(s)).astype(BF)


def pre_kernel(cells, hid, stats, gain, shift, near, far, pre, sums):
    mean, scale = norm_of(stats[...], cells)
    by_normed = jnp.zeros((OWN, W), F32)
    plain = jnp.zeros((OWN, W), F32)
    for r in range(ROWS):
        normed = (hid[r] - mean) * scale
        s = normed * gain[...] + shift[...]
        q = jax.nn.sigmoid(s)
        act_grad = near[r] + far[r].astype(F32)
        value = act_grad * q * (1.0 + s * (1.0 - q))
        pre[r] = value
        by_normed = by_normed + value * normed
        plain = plain + value
    both = jnp.concatenate([by_normed, plain], axis=0).T
    sums[...] = jnp.broadcast_to(jnp.sum(both, axis=0, keepdims=True), (8, W))


def shift_columns(r, row, cols):
    wide = row.astype(F32)
    cols[0, r] = shifted_cols(wide, -1).astype(BF)
    cols[1, r] = row
    cols[2, r] = shifted_cols(wide, 1).astype(BF)


def transposed_conv(at, w, stack, pieces, cols, full):
    for j in range(ROWS // 2):
        for a in range(3):
            for b in range(3):
                o = (a * 3 + b) * OWN
                for k in range(2):
                    y = 2 * j + k
                    stack[o : o + OWN, y * W : (y + 1) * W] = cols[b, y - a + 2]
        part = lax.dot_general(
            w[...],
            stack[:, 2 * j * W : (2 * j + 2) * W],
            (((0,), (0,)), ((), ())),
            preferred_element_type=F32,
        ).astype(BF)
        full[2 * j] = part[:, :W]
        full[2 * j + 1] = part[:, W:]
    for k, (near, far) in zip((0, 1, 3, 2), pieces):
        for n, out in enumerate((near, far)):
            place = pl.multiple_of(target_of(at, (n, k)) * OWN, OWN)
            out[...] = full[:, pl.ds(place, OWN), :]


def piece_refs(refs):
    return [(ref.at[0], ref.at[1]) for ref in refs]


def act_grad_kernel(at, grad, above, below, w, stack, *rest):
    pieces, (cols, full) = rest[:4], rest[4:]
    for r in range(ROWS + 2):
        row = above[OWN:] if r == 0 else below[OWN:] if r == ROWS + 1 else grad[r - 1]
        shift_columns(r, row, cols)
    transposed_conv(at, w, stack, piece_refs(pieces), cols, full)


def band_grad_kernel(cells, at, hid, stats, gain, pre, sums, above, below, w, stack, *rest):
    pieces, (cols, full) = rest[:4], rest[4:]
    mean, scale = norm_of(stats[...], cells)
    spread = jnp.broadcast_to(sums[0:1, :], (W, W)).T
    by_normed, plain = spread[:OWN], spread[OWN:]

    def group_mean(v):
        return per_channel(jnp.sum((gain[...] * v).reshape(4, OWN // 4, W), axis=1) / cells)

    first, second = group_mean(plain), group_mean(by_normed)

    def hidden_grad(p, h):
        normed = (h - mean) * scale
        return scale * (p * gain[...] - first - normed * second)

    for r in range(ROWS + 2):
        if r == 0:
            row = jnp.where(at[5] > 0, hidden_grad(above[0], above[1]), 0.0)
        elif r == ROWS + 1:
            row = jnp.where(at[5] < 15, hidden_grad(below[0], below[1]), 0.0)
        else:
            row = hidden_grad(pre[r - 1], hid[r - 1])
        shift_columns(r, row.astype(BF), cols)
    transposed_conv(at, w, stack, piece_refs(pieces), cols, full)


def filter_products(at, stack, full, rows, keep, send):
    for slot, out in enumerate((keep, send)):
        half = lax.rem(at[4] + slot, 2)
        place = pl.ds(pl.multiple_of(half * 2 * W, 2 * W), 2 * W)
        cells = jnp.concatenate([full[r, place, :] for r in rows], axis=1)
        part = lax.dot_general(
            stack[...], cells, (((1,), (1,)), ((), ())), preferred_element_type=F32
        ).astype(BF)
        out[:STACK, :] = part[:, :W]
        out[STACK:, :] = part[:, W:]


def filter_kernel(at, stack, full, keep, send):
    filter_products(at, stack, full, range(1, ROWS + 1), keep, send)


def gathered_filter_kernel(at, stack, *refs):
    pieces, (keep, send, full) = refs[:4], refs[4:]
    for k, piece in zip((0, 1, 3, 2), pieces):
        for n in range(2):
            place = pl.multiple_of(source_of(at, (n, k)) * OWN, OWN)
            full[:, pl.ds(place, OWN), :] = piece[n]
    filter_products(at, stack, full, range(ROWS), keep, send)


def core_sum_kernel(at, k1, r1, k2, r2, *outs):
    for n, (k, r) in enumerate(((k1, r1), (k2, r2))):
        for dz, out in enumerate(outs):
            p = lax.rem(at[2] + dz, 4)
            rows = pl.ds(pl.multiple_of(p * PIECE, PIECE), PIECE)
            out[n] = (k[rows, :].astype(F32) + r[rows, :].astype(F32)).astype(BF)


def two_sum_kernel(a, b, out):
    out[...] = (a[...].astype(F32) + b[...].astype(F32)).astype(BF)


def four_sum_kernel(a, b, c, d, out):
    total = a[...].astype(F32) + b[...].astype(F32) + c[...].astype(F32) + d[...].astype(F32)
    out[...] = total.astype(BF)


def sum_four(a, b, c, d, name):
    return call(four_sum_kernel, dict(shapes=[(a.shape, BF)]), a, b, c, d, name=name)[0]


Z_ORDER = (0, 1, 3, 2)


def place_kernel(half, at, *refs):
    pieces, (first, second, wide, sems) = refs[:4], refs[-4:]
    core = lax.rem(at[4] + half, 2)
    copies = []
    for k, dz in enumerate(Z_ORDER):
        z = lax.rem(at[2] + 4 - dz, 4)
        rows = pl.ds(pl.multiple_of(lax.rem(z, 2) * PIECE, PIECE), PIECE)
        lanes = pl.ds(pl.multiple_of((core * 2 + lax.div(z, 2)) * W, W), W)
        for n, out in enumerate((first, second)):
            wide[k, n] = pieces[k][n].astype(F32)
            copies.append(
                pltpu.make_async_copy(wide.at[k, n], out.at[rows, lanes], sems.at[k, n])
            )
            copies[-1].start()
    for copy in copies:
        copy.wait()


def place(half, at, pieces, outs, name):
    whole = jax.ShapeDtypeStruct((STACK, C), F32)
    anywhere = pl.BlockSpec(memory_space=pl.ANY)
    return pl.pallas_call(
        functools.partial(place_kernel, half),
        out_shape=[whole] * 2,
        in_specs=[SMEM] + [VMEM] * 4 + [anywhere] * len(outs),
        out_specs=[anywhere] * 2,
        input_output_aliases={5 + n: n for n in range(len(outs))},
        scratch_shapes=[pltpu.VMEM((4, 2, PIECE, W), F32), pltpu.SemaphoreType.DMA((4, 2))],
        compiler_params=pltpu.CompilerParams(vmem_limit_bytes=10 * 1024 * 1024),
        cost_estimate=hint(name),
        name=name,
    )(at, *pieces, *outs)


def gather_ch(value):
    other = lax.ppermute(value, "ch", ch_pairs(1, 0))
    near = [lax.ppermute(value, "ch", ch_pairs(0, k)) for k in (1, 3, 2)]
    far = [lax.ppermute(other, "ch", ch_pairs(0, k)) for k in (1, 3, 2)]
    return [value, other, *near, *far]


def gather_ch_pairs(value):
    both = jnp.stack([value, lax.ppermute(value, "ch", ch_pairs(1, 0))])
    return [both] + [lax.ppermute(both, "ch", ch_pairs(0, k)) for k in (1, 3, 2)]


def scatter_sum_kernel(own, a, b, c, near, far):
    for n, out in enumerate((near, far)):
        total = own[n].astype(F32) + a[n].astype(F32) + b[n].astype(F32) + c[n].astype(F32)
        out[...] = total.astype(out.dtype)


def scatter_ch(pieces, name, gate=None):
    got = [lax.ppermute(p, "ch", ch_pairs(0, k)) for k, p in zip((1, 3, 2), pieces[1:])]
    own = pieces[0] if gate is None else after(pieces[0], gate)
    near, far = call(
        scatter_sum_kernel, dict(shapes=[((ROWS, OWN, W), F32), ((ROWS, OWN, W), BF)]),
        own, *got, name=name,
    )
    return near, lax.ppermute(far, "ch", ch_pairs(1, 0)), got


def neighbours(first, last):
    up = [(i, i + 1) for i in range(15)]
    down = [(i + 1, i) for i in range(15)]
    return lax.ppermute(last, "rows", up), lax.ppermute(first, "rows", down)


def sum_rows_near(value):
    for dz, dx, dc in ((0, 0, 1), (0, 1, 0)):
        value = value + lax.ppermute(value, "rows", row_pairs(dz, dx, dc))
    return value


def sum_rows_far(value, gate=None):
    for mask in (4, 8):
        if mask == 8 and gate is not None:
            value = after(value, gate)
        value = value + lax.ppermute(value, "rows", [(i, i ^ mask) for i in range(16)])
    return value


def final_kernel(near, far, out):
    for r in range(ROWS):
        out[r] = (near[r] + far[r].astype(F32)).astype(BF)


def input_grad(kernel, w, *args, name):
    outs = call(
        kernel,
        dict(
            shapes=[((STACK, ROWS * W), BF)] + [((2, ROWS, OWN, W), BF)] * 4,
            scratch=[pltpu.VMEM((3, ROWS + 2, OWN, W), BF), pltpu.VMEM((ROWS, C, W), BF)],
        ),
        *args, w,
        name=name,
    )
    return outs[0], outs[1:]


def body(x_band, first_filter, second_filter, norm_gain, norm_shift, out_cotangent):
    cells = float((C // G) * ROWS * lax.axis_size("rows") * W)
    ch, rows = lax.axis_index("ch"), lax.axis_index("rows")
    at = jnp.stack([ch // 4, ch % 4, rows // 4, (rows // 2) % 2, rows % 2, rows]).astype(jnp.int32)
    x_band, out_cotangent, at = lax.optimization_barrier((x_band, out_cotangent, at))
    x_above, x_below = neighbours(
        *(jnp.concatenate([x_band[:, r], out_cotangent[:, r]]) for r in (0, ROWS - 1))
    )
    cot_rows = jnp.transpose(out_cotangent, (1, 0, 2))
    x_rows = jnp.concatenate(
        [x_above[None, :OWN], jnp.transpose(x_band, (1, 0, 2)), x_below[None, :OWN]]
    )
    w1 = first_filter.reshape(STACK, C)
    w2 = second_filter.reshape(STACK, C)
    gain = jnp.broadcast_to(norm_gain[:, None], (OWN, W))
    shift = jnp.broadcast_to(norm_shift[:, None], (OWN, W))
    strip = (ROWS, OWN, W)

    x_pieces = gather_ch(x_rows)
    cot_stack, act_pieces = input_grad(
        act_grad_kernel, w2, at, after(cot_rows, x_pieces[GATES[3]]), x_above, x_below, name="act_grad"
    )
    hid, stats, x_full = call(
        conv_kernel,
        dict(
            shapes=[(strip, F32), ((8, W), F32), ((ROWS + 2, C, W), BF)],
            scratch=[pltpu.VMEM((3, ROWS, OWN, W), F32)],
        ),
        at, *x_pieces, w1,
        name="hidden",
    )
    stats = sum_rows_near(stats)
    *act_parts, _ = scatter_ch([after(p, x_pieces[GATES[5]]) if GATES[5] else p for p in act_pieces], "act_grad_sum", stats)
    stats = sum_rows_far(stats, act_parts[0] if GATES[0] else None)
    (act,) = call(
        functools.partial(act_kernel, cells), dict(shapes=[(strip, BF)]),
        hid, stats, gain, shift, name="activation",
    )
    pre, sums = call(
        functools.partial(pre_kernel, cells), dict(shapes=[(strip, F32), ((8, W), F32)]),
        hid, stats, gain, shift, *act_parts, name="pre_grad",
    )
    act_all = gather_ch_pairs(act)
    sums = sum_rows_near(sums)
    if GATES[1] == 2:
        sums = after(sums, act_all[0])
    sums = sum_rows_far(sums, act_all[0] if GATES[1] == 1 else None)
    above, below = neighbours(
        jnp.stack([pre[0], hid[0]]), jnp.stack([pre[ROWS - 1], hid[ROWS - 1]])
    )
    half = ((2 * STACK, W), BF)
    hg_stack, band_pieces = input_grad(
        functools.partial(band_grad_kernel, cells), w1,
        at, hid, stats, gain, pre, after(sums, act_all[1 : 1 + NG[0]]) if NG[0] else sums, above, below,
        name="band_grad",
    )
    *band_parts, band_got = scatter_ch(band_pieces, "band_grad_sum")
    keep1, send1 = call(
        filter_kernel, dict(shapes=[half, half]), at, hg_stack, x_full,
        name="first_grad",
    )
    recv1 = lax.ppermute(send1, "rows", row_pairs(0, 0, 1))
    keep2, send2 = call(
        gathered_filter_kernel,
        dict(shapes=[half, half], scratch=[pltpu.VMEM((ROWS, C, W), BF)]),
        at, cot_stack if GATES[4] == 0 else after(cot_stack, hg_stack if GATES[4] == 1 else keep1), *act_all,
        name="second_grad",
    )
    recv2 = lax.ppermute(send2, "rows", row_pairs(0, 0, 1))
    share = ((2, PIECE, W), BF)
    parts = call(
        core_sum_kernel, dict(shapes=[share] * 4), at, after(keep1, band_got[0]) if NG[1] else keep1, recv1, keep2, recv2, name="core_sum"
    )
    got = [lax.ppermute(parts[k], "rows", row_pairs(k, 0, 0)) for k in (1, 3, 2)]
    gain_grad, shift_grad = sums[0, :OWN], sums[0, OWN:]
    part = sum_four(after(parts[0], (gain_grad, shift_grad, *band_parts[: NG[2]])), *got, name="filter_sum")
    part = call(
        two_sum_kernel, dict(shapes=[share]),
        part, lax.ppermute(after(part, band_parts[0]) if GATES[2] == 1 else part, "rows", row_pairs(0, 1, 0)), name="pair_sum",
    )[0]
    if NG[3]:
        part = after(part, band_parts[1])
    mine = [part] + [lax.ppermute(part, "rows", row_pairs(k, 0, 0)) for k in Z_ORDER[1:]]
    theirs = [lax.ppermute(p, "rows", row_pairs(0, 0, 1)) for p in mine]
    grads = place(0, at, mine, (), "own_half")
    first_grad, second_grad = place(1, at, theirs, grads, "other_half")
    (band,) = call(final_kernel, dict(shapes=[(strip, BF)]), *band_parts, name="band_grad_total")
    shape = (3, 3, OWN, C)
    return (
        jnp.transpose(band, (1, 0, 2)),
        first_grad.reshape(shape),
        second_grad.reshape(shape),
        gain_grad,
        shift_grad,
    )


def solution(mesh):
    filters = P(None, None, "ch", None)
    strip = P("ch", "rows", None)
    return jax.shard_map(
        body,
        mesh=mesh,
        in_specs=(strip, filters, filters, P("ch"), P("ch"), strip),
        out_specs=(strip, filters, filters, P("ch"), P("ch")),
        check_vma=False,
    )
```

time: 161 us -> 117 us (0.73)
  starting transfers between devices: 101 us -> 70.1 us
  waiting for transfers between devices: 34.3 us -> 29.3 us
  local copies, waits for them, and re-layouts: 6.19 us -> 2.7 us
  Pallas kernels: 16.2 us -> 13 us
    ppermute x12 -> x6, starting transfers between devices: 16.9 us -> 8.05 us  [scatter_ch(): lax.ppermute(p, 'ch', ch_pairs(0, k))]
    ppermute x6 -> x4, starting transfers between devices: 20.9 us -> 13.8 us  [neighbours(): return (lax.ppermute(last, 'rows', up), lax.ppermute(first, 'rows', down))]
    ppermute x12 -> x6, waiting for transfers between devices: 6.92 us -> 0.02 us  [scatter_ch(): lax.ppermute(p, 'ch', ch_pairs(0, k))]
    ppermute x6 -> x3, starting transfers between devices: 9.61 us -> 2.79 us  [gather_ch(): far = [lax.ppermute(other, 'ch', ch_pairs(0, k)) for k in (1, 3, 2)]]
    pallas_call x16 -> x13, Pallas kernels: 16.2 us -> 9.77 us  [call(): pl.pallas_call(kernel, out_shape=shapes, in_specs=[SMEM if a.dtype == jnp...]
    ppermute x6 -> x3, starting transfers between devices: 8.76 us -> 4.46 us  [gather_ch(): near = [lax.ppermute(value, 'ch', ch_pairs(0, k)) for k in (1, 3, 2)]]
    ppermute x6 -> x4, waiting for transfers between devices: 4.9 us -> 0.99 us  [neighbours(): return (lax.ppermute(last, 'rows', up), lax.ppermute(first, 'rows', down))]
    pallas_call x0 -> x2, Pallas kernels: none -> 3.25 us  [place(): pl.pallas_call(functools.partial(place_kernel, half), out_shape=[whole] *...]
  transfers between devices with their start and end apart: 56 -> 44, of which waited for: 21 -> 18; matrix products, arithmetic and copies ran while one was open for 3% -> 1% of each run, Pallas kernels for 8% -> 9%
where the time goes in v2:
time: 117 us; the launch traced here: 116 us
  starting transfers between devices  70.1 us (60%)
  waiting for transfers between devices  29.3 us (25%)
  Pallas kernels  13 us (11%)
  local copies, waits for them, and re-layouts  2.7 us (2%)
  between operations  1.19 us (1%)
    ppermute x4, starting transfers between devices, neighbours(): return (lax.ppermute(last, 'rows', up), lax.ppermute(first, 'rows', down))  13.8 us
    pallas_call x13, Pallas kernels, call(): pl.pallas_call(kernel, out_shape=shapes, in_specs=[SMEM if a.dtype == jnp...  9.77 us
    ppermute x4, starting transfers between devices, sum_rows_far(): lax.ppermute(value, 'rows', [(i, i ^ mask) for i in range(16)])  8.64 us
    ppermute x4, starting transfers between devices, sum_rows_near(): value = value + lax.ppermute(value, 'rows', row_pairs(dz, dx, dc))  8.33 us
    ppermute x6, starting transfers between devices, scatter_ch(): lax.ppermute(p, 'ch', ch_pairs(0, k))  8.05 us
    ppermute x2, waiting for transfers between devices, scatter_ch(): return (near, lax.ppermute(far, 'ch', ch_pairs(1, 0)), got)  6 us
    ppermute x4, starting transfers between devices, body(): theirs = [lax.ppermute(p, 'rows', row_pairs(0, 0, 1)) for p in mine]  4.89 us
    ppermute x3, starting transfers between devices, gather_ch(): near = [lax.ppermute(value, 'ch', ch_pairs(0, k)) for k in (1, 3, 2)]  4.46 us
  transfers between devices with their start and end apart: 44, of which 18 were waited for; matrix products, arithmetic and copies ran while one was open for 1% of the time, Pallas kernels for 9%

profile of v2, /device:TPU:1, one launch (start us, length us, event | category | flops | bytes accessed | tf_op | source)
XLA Modules:
  0.0 116.4 jit_solution(10933254640537340132)
XLA Ops:
  1.9 3.3 %collective-permute-start.1 = (bf16[128,128]{1,0:T(8,128)(2,1)S(1)}, bf16[128,128]{1,0:T(8,128)(2,1)S(1)}, u32[]{:S(2)}, u32[]{:S(2)}) collective-permute-start(bf16[128,128]{1,0:T(8,128)(2,1)S(1)} %pad_maximum_fusion.5), channel_id=1, source_target_pairs={{8,0},{16,8},{24,16},{32,24},{40,32},{48,40},{56,48},{64,56},{72,6... | collective-permute-start | bytes 98312 | tf_op jit(solution)/shard_map/ppermute | solution.py:331
  5.3 3.1 %collective-permute-start = (bf16[128,128]{1,0:T(8,128)(2,1)S(1)}, bf16[128,128]{1,0:T(8,128)(2,1)S(1)}, u32[]{:S(2)}, u32[]{:S(2)}) collective-permute-start(bf16[128,128]{1,0:T(8,128)(2,1)S(1)} %pad_maximum_fusion.4), channel_id=1, source_target_pairs={{0,8},{8,16},{16,24},{24,32},{32,40},{40,48},{48,56},{56,64},{64,7... | collective-permute-start | bytes 98312 | tf_op jit(solution)/shard_map/ppermute | solution.py:331
  9.4 3.0 %collective-permute-start.5 = (bf16[10,64,128]{2,1,0:T(8,128)(2,1)S(1)}, bf16[10,64,128]{2,1,0:T(8,128)(2,1)S(1)}, u32[]{:S(2)}, u32[]{:S(2)}) collective-permute-start(bf16[10,64,128]{2,1,0:T(8,128)(2,1)S(1)} %pad_maximum_fusion.1.refs_0_), channel_id=1, source_target_pairs={{0,2},{1,3},{2,0},{3,1},{4,6},{5,7},{6,4},{7,5},{8,10},{9,11},{10,... | collective-permute-start | bytes 491528 | tf_op jit(solution)/shard_map/ppermute | solution.py:302
  12.4 2.7 %collective-permute-start.2 = (bf16[10,64,128]{2,1,0:T(8,128)(2,1)S(1)}, bf16[10,64,128]{2,1,0:T(8,128)(2,1)S(1)}, u32[]{:S(2)}, u32[]{:S(2)}) collective-permute-start(bf16[10,64,128]{2,1,0:T(8,128)(2,1)S(1)} %pad_maximum_fusion.1.refs_0_), channel_id=1, source_target_pairs={{0,4},{1,5},{2,6},{3,7},{4,0},{5,1},{6,2},{7,3},{8,12},{9,13},{10,... | collective-permute-start | bytes 491528 | tf_op jit(solution)/shard_map/ppermute | solution.py:301
  16.8 3.2 %collective-permute-done.2.refs_1_ = bf16[10,64,128]{2,1,0:T(8,128)(2,1)S(1)} collective-permute-done((bf16[10,64,128]{2,1,0:T(8,128)(2,1)S(1)}, bf16[10,64,128]{2,1,0:T(8,128)(2,1)S(1)}, u32[]{:S(2)}, u32[]{:S(2)}) %collective-permute-start.2) | collective-permute-done | bytes 163872 | tf_op jit(solution)/shard_map/ppermute | solution.py:301
  20.1 2.8 %collective-permute-start.7 = (bf16[10,64,128]{2,1,0:T(8,128)(2,1)S(1)}, bf16[10,64,128]{2,1,0:T(8,128)(2,1)S(1)}, u32[]{:S(2)}, u32[]{:S(2)}) collective-permute-start(bf16[10,64,128]{2,1,0:T(8,128)(2,1)S(1)} %collective-permute-done.2.refs_1_), channel_id=1, source_target_pairs={{0,3},{1,0},{2,1},{3,2},{4,7},{5,4},{6,5},{7,6},{8,11},{9,8},{10,9... | collective-permute-start | bytes 491528 | tf_op jit(solution)/shard_map/ppermute | solution.py:303
  22.9 1.8 %act_grad.1 = (bf16[576,1024]{1,0:T(8,128)(2,1)S(1)}, bf16[2,8,64,128]{3,2,1,0:T(8,128)(2,1)S(1)}, bf16[2,8,64,128]{3,2,1,0:T(8,128)(2,1)S(1)}, bf16[2,8,64,128]...) custom-call(s32[6]{0:T(128)S(1)} %stack.42.at, bf16[8,64,128]{2,1,0:T(8,128)(2,1)S(1)} %get-tuple-element.49.grad, ...), custom_call_target="tpu_custom_call" | custom-call | flops 24149999616 | tf_op jit(solution)/shard_map/act_grad/pallas_call | solution.py:55
  24.9 2.7 %collective-permute-start.13 = (bf16[2,8,64,128]{3,2,1,0:T(8,128)(2,1)S(1)}, bf16[2,8,64,128]{3,2,1,0:T(8,128)(2,1)S(1)}, u32[]{:S(2)}, u32[]{:S(2)}) collective-permute-start(bf16[2,8,64,128]{3,2,1,0:T(8,128)(2,1)S(1)} %get-tuple-element.53), channel_id=1, source_target_pairs={{0,3},{1,0},{2,1},{3,2},{4,7},{5,4},{6,5},{7,6},{8,11},{9,8},{10,9... | collective-permute-start | bytes 786440 | tf_op jit(solution)/shard_map/ppermute | solution.py:319
  35.0 2.2 %collective-permute-start.10 = (f32[8,128]{1,0:T(8,128)S(1)}, f32[8,128]{1,0:T(8,128)S(1)}, u32[]{:S(2)}, u32[]{:S(2)}) collective-permute-start(f32[8,128]{1,0:T(8,128)S(1)} %add.40), channel_id=1, source_target_pairs={{0,16},{8,24},{16,0},{24,8},{32,48},{40,56},{48,32},{56,40},{64,80... | collective-permute-start | bytes 12296 | tf_op jit(solution)/shard_map/ppermute | solution.py:336
  38.5 2.3 %collective-permute-start.11 = (f32[8,128]{1,0:T(8,128)S(1)}, f32[8,128]{1,0:T(8,128)S(1)}, u32[]{:S(2)}, u32[]{:S(2)}) collective-permute-start(f32[8,128]{1,0:T(8,128)S(1)} %add.41), channel_id=1, source_target_pairs={{0,32},{8,40},{16,48},{24,56},{32,0},{40,8},{48,16},{56,24},{64,96... | collective-permute-start | bytes 12296 | tf_op jit(solution)/shard_map/ppermute | solution.py:344
  42.3 4.2 %collective-permute-start.15 = (f32[8,128]{1,0:T(8,128)S(1)}, f32[8,128]{1,0:T(8,128)S(1)}, u32[]{:S(2)}, u32[]{:S(2)}) collective-permute-start(f32[8,128]{1,0:T(8,128)S(1)} %add.42), channel_id=1, source_target_pairs={{0,64},{8,72},{16,80},{24,88},{32,96},{40,104},{48,112},{56,120},{... | collective-permute-start | bytes 12296 | tf_op jit(solution)/shard_map/ppermute | solution.py:344
  49.9 2.0 %collective-permute-done.16.far = bf16[8,64,128]{2,1,0:T(8,128)(2,1)S(1)} collective-permute-done((bf16[8,64,128]{2,1,0:T(8,128)(2,1)S(1)}, bf16[8,64,128]{2,1,0:T(8,128)(2,1)S(1)}, u32[]{:S(2)}, u32[]{:S(2)}) %collective-permute-start.16) | collective-permute-done | bytes 131104 | tf_op jit(solution)/shard_map/ppermute | solution.py:325
  52.1 4.4 %collective-permute-start.17 = (f32[8,128]{1,0:T(8,128)S(1)}, f32[8,128]{1,0:T(8,128)S(1)}, u32[]{:S(2)}, u32[]{:S(2)}) collective-permute-start(f32[8,128]{1,0:T(8,128)S(1)} %get-tuple-element.59), channel_id=1, source_target_pairs={{0,8},{8,0},{16,24},{24,16},{32,40},{40,32},{48,56},{56,48},{64,72... | collective-permute-start | bytes 12296 | tf_op jit(solution)/shard_map/ppermute | solution.py:336
  60.3 4.7 %collective-permute-start.25 = (f32[2,64,128]{2,1,0:T(8,128)S(1)}, f32[2,64,128]{2,1,0:T(8,128)S(1)}, u32[]{:S(2)}, u32[]{:S(2)}) collective-permute-start(f32[2,64,128]{2,1,0:T(8,128)S(1)} %pad_maximum_fusion.2), channel_id=1, source_target_pairs={{0,8},{8,16},{16,24},{24,32},{32,40},{40,48},{48,56},{56,64},{64,7... | collective-permute-start | bytes 196616 | tf_op jit(solution)/shard_map/ppermute | solution.py:331
  66.6 2.6 %collective-permute-done.20 = f32[8,128]{1,0:T(8,128)S(1)} collective-permute-done((f32[8,128]{1,0:T(8,128)S(1)}, f32[8,128]{1,0:T(8,128)S(1)}, u32[]{:S(2)}, u32[]{:S(2)}) %collective-permute-start.20) | collective-permute-done | bytes 4128 | tf_op jit(solution)/shard_map/ppermute | solution.py:344
  69.1 2.7 %collective-permute-start.26 = (f32[2,64,128]{2,1,0:T(8,128)S(1)}, f32[2,64,128]{2,1,0:T(8,128)S(1)}, u32[]{:S(2)}, u32[]{:S(2)}) collective-permute-start(f32[2,64,128]{2,1,0:T(8,128)S(1)} %pad_maximum_fusion.3), channel_id=1, source_target_pairs={{8,0},{16,8},{24,16},{32,24},{40,32},{48,40},{56,48},{64,56},{72,6... | collective-permute-start | bytes 196616 | tf_op jit(solution)/shard_map/ppermute | solution.py:331
  74.9 2.0 %band_grad.1 = (bf16[576,1024]{1,0:T(8,128)(2,1)S(1)}, bf16[2,8,64,128]{3,2,1,0:T(8,128)(2,1)S(1)}, bf16[2,8,64,128]{3,2,1,0:T(8,128)(2,1)S(1)}, bf16[2,8,64,128...) custom-call(s32[6]{0:T(128)S(1)} %stack.42.at, f32[8,64,128]{2,1,0:T(8,128)S(1)} %get-tuple-element.47.hid, ...), custom_call_target="tpu_custom_call" | custom-call | tf_op jit(solution)/shard_map/band_grad/pallas_call | solution.py:55
  81.6 2.5 %collective-permute-start.28 = (bf16[2,8,64,128]{3,2,1,0:T(8,128)(2,1)S(1)}, bf16[2,8,64,128]{3,2,1,0:T(8,128)(2,1)S(1)}, u32[]{:S(2)}, u32[]{:S(2)}) collective-permute-start(bf16[2,8,64,128]{3,2,1,0:T(8,128)(2,1)S(1)} %get-tuple-element.63), channel_id=1, source_target_pairs={{0,3},{1,0},{2,1},{3,2},{4,7},{5,4},{6,5},{7,6},{8,11},{9,8},{10,9... | collective-permute-start | bytes 786440 | tf_op jit(solution)/shard_map/ppermute | solution.py:319
  85.3 2.2 %collective-permute-start.34 = (bf16[2,288,128]{2,1,0:T(8,128)(2,1)S(1)}, bf16[2,288,128]{2,1,0:T(8,128)(2,1)S(1)}, u32[]{:S(2)}, u32[]{:S(2)}) collective-permute-start(bf16[2,288,128]{2,1,0:T(8,128)(2,1)S(1)} %get-tuple-element.77), channel_id=1, source_target_pairs={{0,96},{8,104},{16,112},{24,120},{32,0},{40,8},{48,16},{56,24},{64... | collective-permute-start | bytes 442376 | tf_op jit(solution)/shard_map/ppermute | solution.py:439
  90.2 3.2 %collective-permute-done.35.d = bf16[2,288,128]{2,1,0:T(8,128)(2,1)S(1)} collective-permute-done((bf16[2,288,128]{2,1,0:T(8,128)(2,1)S(1)}, bf16[2,288,128]{2,1,0:T(8,128)(2,1)S(1)}, u32[]{:S(2)}, u32[]{:S(2)}) %collective-permute-start.35) | collective-permute-done | bytes 147488 | tf_op jit(solution)/shard_map/ppermute | solution.py:439
  94.4 3.4 %collective-permute-done.36.b = bf16[2,288,128]{2,1,0:T(8,128)(2,1)S(1)} collective-permute-done((bf16[2,288,128]{2,1,0:T(8,128)(2,1)S(1)}, bf16[2,288,128]{2,1,0:T(8,128)(2,1)S(1)}, u32[]{:S(2)}, u32[]{:S(2)}) %collective-permute-start.36) | collective-permute-done | bytes 147488 | tf_op jit(solution)/shard_map/ppermute | solution.py:444
  99.0 2.3 %collective-permute-start.40 = (bf16[2,288,128]{2,1,0:T(8,128)(2,1)S(1)}, bf16[2,288,128]{2,1,0:T(8,128)(2,1)S(1)}, u32[]{:S(2)}, u32[]{:S(2)}) collective-permute-start(bf16[2,288,128]{2,1,0:T(8,128)(2,1)S(1)} %pair_sum.1.refs_0_), channel_id=1, source_target_pairs={{0,96},{8,104},{16,112},{24,120},{32,0},{40,8},{48,16},{56,24},{64... | collective-permute-start | bytes 442376 | tf_op jit(solution)/shard_map/ppermute | solution.py:448
  103.3 4.0 %collective-permute-done.30.far = bf16[8,64,128]{2,1,0:T(8,128)(2,1)S(1)} collective-permute-done((bf16[8,64,128]{2,1,0:T(8,128)(2,1)S(1)}, bf16[8,64,128]{2,1,0:T(8,128)(2,1)S(1)}, u32[]{:S(2)}, u32[]{:S(2)}) %collective-permute-start.30) | collective-permute-done | bytes 131104 | tf_op jit(solution)/shard_map/ppermute | solution.py:325
  108.1 4.3 %collective-permute-start.37 = (bf16[2,288,128]{2,1,0:T(8,128)(2,1)S(1)}, bf16[2,288,128]{2,1,0:T(8,128)(2,1)S(1)}, u32[]{:S(2)}, u32[]{:S(2)}) collective-permute-start(bf16[2,288,128]{2,1,0:T(8,128)(2,1)S(1)} %pair_sum.1.refs_0_), channel_id=1, source_target_pairs={{0,8},{8,0},{16,24},{24,16},{32,40},{40,32},{48,56},{56,48},{64,72... | collective-permute-start | bytes 442376 | tf_op jit(solution)/shard_map/ppermute | solution.py:449
  (113 shorter events, 43.5 us)
Async XLA Ops:
  1.9 6.5 %collective-permute-start.1 = (bf16[128,128]{1,0:T(8,128)(2,1)S(1)}, bf16[128,128]{1,0:T(8,128)(2,1)S(1)}, u32[]{:S(2)}, u32[]{:S(2)}) collective-permute-start(bf16[128,128]{1,0:T(8,128)(2,1)S(1)} %pad_maximum_fusion.5), channel_id=1, source_target_pairs={{8,0},{16,8},{24,16},{32,24},{40,32},{48,40},{56,48},{64,56},{72,6... | collective-permute-start | bytes 98312 | tf_op jit(solution)/shard_map/ppermute | solution.py:331
  9.4 7.4 %collective-permute-start.5 = (bf16[10,64,128]{2,1,0:T(8,128)(2,1)S(1)}, bf16[10,64,128]{2,1,0:T(8,128)(2,1)S(1)}, u32[]{:S(2)}, u32[]{:S(2)}) collective-permute-start(bf16[10,64,128]{2,1,0:T(8,128)(2,1)S(1)} %pad_maximum_fusion.1.refs_0_), channel_id=1, source_target_pairs={{0,2},{1,3},{2,0},{3,1},{4,6},{5,7},{6,4},{7,5},{8,10},{9,11},{10,... | collective-permute-start | bytes 491528 | tf_op jit(solution)/shard_map/ppermute | solution.py:302
  12.4 7.7 %collective-permute-start.2 = (bf16[10,64,128]{2,1,0:T(8,128)(2,1)S(1)}, bf16[10,64,128]{2,1,0:T(8,128)(2,1)S(1)}, u32[]{:S(2)}, u32[]{:S(2)}) collective-permute-start(bf16[10,64,128]{2,1,0:T(8,128)(2,1)S(1)} %pad_maximum_fusion.1.refs_0_), channel_id=1, source_target_pairs={{0,4},{1,5},{2,6},{3,7},{4,0},{5,1},{6,2},{7,3},{8,12},{9,13},{10,... | collective-permute-start | bytes 491528 | tf_op jit(solution)/shard_map/ppermute | solution.py:301
  15.1 9.6 %collective-permute-start.4 = (bf16[10,64,128]{2,1,0:T(8,128)(2,1)S(1)}, bf16[10,64,128]{2,1,0:T(8,128)(2,1)S(1)}, u32[]{:S(2)}, u32[]{:S(2)}) collective-permute-start(bf16[10,64,128]{2,1,0:T(8,128)(2,1)S(1)} %pad_maximum_fusion.1.refs_0_), channel_id=1, source_target_pairs={{0,3},{1,0},{2,1},{3,2},{4,7},{5,4},{6,5},{7,6},{8,11},{9,8},{10,9... | collective-permute-start | bytes 491528 | tf_op jit(solution)/shard_map/ppermute | solution.py:302
  15.9 9.0 %collective-permute-start.3 = (bf16[10,64,128]{2,1,0:T(8,128)(2,1)S(1)}, bf16[10,64,128]{2,1,0:T(8,128)(2,1)S(1)}, u32[]{:S(2)}, u32[]{:S(2)}) collective-permute-start(bf16[10,64,128]{2,1,0:T(8,128)(2,1)S(1)} %pad_maximum_fusion.1.refs_0_), channel_id=1, source_target_pairs={{0,1},{1,2},{2,3},{3,0},{4,5},{5,6},{6,7},{7,4},{8,9},{9,10},{10,1... | collective-permute-start | bytes 491528 | tf_op jit(solution)/shard_map/ppermute | solution.py:302
  20.1 7.5 %collective-permute-start.8 = (bf16[10,64,128]{2,1,0:T(8,128)(2,1)S(1)}, bf16[10,64,128]{2,1,0:T(8,128)(2,1)S(1)}, u32[]{:S(2)}, u32[]{:S(2)}) collective-permute-start(bf16[10,64,128]{2,1,0:T(8,128)(2,1)S(1)} %collective-permute-done.2.refs_1_), channel_id=1, source_target_pairs={{0,2},{1,3},{2,0},{3,1},{4,6},{5,7},{6,4},{7,5},{8,10},{9,11},{10,... | collective-permute-start | bytes 491528 | tf_op jit(solution)/shard_map/ppermute | solution.py:303
  20.1 8.8 %collective-permute-start.7 = (bf16[10,64,128]{2,1,0:T(8,128)(2,1)S(1)}, bf16[10,64,128]{2,1,0:T(8,128)(2,1)S(1)}, u32[]{:S(2)}, u32[]{:S(2)}) collective-permute-start(bf16[10,64,128]{2,1,0:T(8,128)(2,1)S(1)} %collective-permute-done.2.refs_1_), channel_id=1, source_target_pairs={{0,3},{1,0},{2,1},{3,2},{4,7},{5,4},{6,5},{7,6},{8,11},{9,8},{10,9... | collective-permute-start | bytes 491528 | tf_op jit(solution)/shard_map/ppermute | solution.py:303
  22.9 7.8 %collective-permute-start.6 = (bf16[10,64,128]{2,1,0:T(8,128)(2,1)S(1)}, bf16[10,64,128]{2,1,0:T(8,128)(2,1)S(1)}, u32[]{:S(2)}, u32[]{:S(2)}) collective-permute-start(bf16[10,64,128]{2,1,0:T(8,128)(2,1)S(1)} %collective-permute-done.2.refs_1_), channel_id=1, source_target_pairs={{0,1},{1,2},{2,3},{3,0},{4,5},{5,6},{6,7},{7,4},{8,9},{9,10},{10,1... | collective-permute-start | bytes 491528 | tf_op jit(solution)/shard_map/ppermute | solution.py:303
  24.8 17.4 %collective-permute-start.12 = (bf16[2,8,64,128]{3,2,1,0:T(8,128)(2,1)S(1)}, bf16[2,8,64,128]{3,2,1,0:T(8,128)(2,1)S(1)}, u32[]{:S(2)}, u32[]{:S(2)}) collective-permute-start(bf16[2,8,64,128]{3,2,1,0:T(8,128)(2,1)S(1)} %get-tuple-element.52), channel_id=1, source_target_pairs={{0,1},{1,2},{2,3},{3,0},{4,5},{5,6},{6,7},{7,4},{8,9},{9,10},{10,1... | collective-permute-start | bytes 786440 | tf_op jit(solution)/shard_map/ppermute | solution.py:319
  24.9 17.3 %collective-permute-start.13 = (bf16[2,8,64,128]{3,2,1,0:T(8,128)(2,1)S(1)}, bf16[2,8,64,128]{3,2,1,0:T(8,128)(2,1)S(1)}, u32[]{:S(2)}, u32[]{:S(2)}) collective-permute-start(bf16[2,8,64,128]{3,2,1,0:T(8,128)(2,1)S(1)} %get-tuple-element.53), channel_id=1, source_target_pairs={{0,3},{1,0},{2,1},{3,2},{4,7},{5,4},{6,5},{7,6},{8,11},{9,8},{10,9... | collective-permute-start | bytes 786440 | tf_op jit(solution)/shard_map/ppermute | solution.py:319
  27.6 14.6 %collective-permute-start.14 = (bf16[2,8,64,128]{3,2,1,0:T(8,128)(2,1)S(1)}, bf16[2,8,64,128]{3,2,1,0:T(8,128)(2,1)S(1)}, u32[]{:S(2)}, u32[]{:S(2)}) collective-permute-start(bf16[2,8,64,128]{3,2,1,0:T(8,128)(2,1)S(1)} %get-tuple-element.54), channel_id=1, source_target_pairs={{0,2},{1,3},{2,0},{3,1},{4,6},{5,7},{6,4},{7,5},{8,10},{9,11},{10,... | collective-permute-start | bytes 786440 | tf_op jit(solution)/shard_map/ppermute | solution.py:319
  48.6 8.6 %collective-permute-start.21 = (bf16[8,64,128]{2,1,0:T(8,128)(2,1)S(1)}, bf16[8,64,128]{2,1,0:T(8,128)(2,1)S(1)}, u32[]{:S(2)}, u32[]{:S(2)}) collective-permute-start(bf16[8,64,128]{2,1,0:T(8,128)(2,1)S(1)} %activation.1), channel_id=1, source_target_pairs={{0,4},{1,5},{2,6},{3,7},{4,0},{5,1},{6,2},{7,3},{8,12},{9,13},{10,... | collective-permute-start | bytes 393224 | tf_op jit(solution)/shard_map/ppermute | solution.py:308
  57.3 14.6 %collective-permute-start.24 = (bf16[2,8,64,128]{3,2,1,0:T(8,128)(2,1)S(1)}, bf16[2,8,64,128]{3,2,1,0:T(8,128)(2,1)S(1)}, u32[]{:S(2)}, u32[]{:S(2)}) collective-permute-start(bf16[2,8,64,128]{3,2,1,0:T(8,128)(2,1)S(1)} %pad_maximum_fusion.refs_0_), channel_id=1, source_target_pairs={{0,2},{1,3},{2,0},{3,1},{4,6},{5,7},{6,4},{7,5},{8,10},{9,11},{10,... | collective-permute-start | bytes 786440 | tf_op jit(solution)/shard_map/ppermute | solution.py:309
  57.6 14.2 %collective-permute-start.23 = (bf16[2,8,64,128]{3,2,1,0:T(8,128)(2,1)S(1)}, bf16[2,8,64,128]{3,2,1,0:T(8,128)(2,1)S(1)}, u32[]{:S(2)}, u32[]{:S(2)}) collective-permute-start(bf16[2,8,64,128]{3,2,1,0:T(8,128)(2,1)S(1)} %pad_maximum_fusion.refs_0_), channel_id=1, source_target_pairs={{0,3},{1,0},{2,1},{3,2},{4,7},{5,4},{6,5},{7,6},{8,11},{9,8},{10,9... | collective-permute-start | bytes 786440 | tf_op jit(solution)/shard_map/ppermute | solution.py:309
  59.3 13.4 %collective-permute-start.22 = (bf16[2,8,64,128]{3,2,1,0:T(8,128)(2,1)S(1)}, bf16[2,8,64,128]{3,2,1,0:T(8,128)(2,1)S(1)}, u32[]{:S(2)}, u32[]{:S(2)}) collective-permute-start(bf16[2,8,64,128]{3,2,1,0:T(8,128)(2,1)S(1)} %pad_maximum_fusion.refs_0_), channel_id=1, source_target_pairs={{0,1},{1,2},{2,3},{3,0},{4,5},{5,6},{6,7},{7,4},{8,9},{9,10},{10,1... | collective-permute-start | bytes 786440 | tf_op jit(solution)/shard_map/ppermute | solution.py:309
  60.3 14.7 %collective-permute-start.25 = (f32[2,64,128]{2,1,0:T(8,128)S(1)}, f32[2,64,128]{2,1,0:T(8,128)S(1)}, u32[]{:S(2)}, u32[]{:S(2)}) collective-permute-start(f32[2,64,128]{2,1,0:T(8,128)S(1)} %pad_maximum_fusion.2), channel_id=1, source_target_pairs={{0,8},{8,16},{16,24},{24,32},{32,40},{40,48},{48,56},{56,64},{64,7... | collective-permute-start | bytes 196616 | tf_op jit(solution)/shard_map/ppermute | solution.py:331
  80.6 6.9 %collective-permute-start.33 = (bf16[2,288,128]{2,1,0:T(8,128)(2,1)S(1)}, bf16[2,288,128]{2,1,0:T(8,128)(2,1)S(1)}, u32[]{:S(2)}, u32[]{:S(2)}) collective-permute-start(bf16[2,288,128]{2,1,0:T(8,128)(2,1)S(1)} %get-tuple-element.76), channel_id=1, source_target_pairs={{0,32},{8,40},{16,48},{24,56},{32,64},{40,72},{48,80},{56,88},{64,... | collective-permute-start | bytes 442376 | tf_op jit(solution)/shard_map/ppermute | solution.py:439
  81.3 20.1 %collective-permute-start.27 = (bf16[2,8,64,128]{3,2,1,0:T(8,128)(2,1)S(1)}, bf16[2,8,64,128]{3,2,1,0:T(8,128)(2,1)S(1)}, u32[]{:S(2)}, u32[]{:S(2)}) collective-permute-start(bf16[2,8,64,128]{3,2,1,0:T(8,128)(2,1)S(1)} %get-tuple-element.62), channel_id=1, source_target_pairs={{0,1},{1,2},{2,3},{3,0},{4,5},{5,6},{6,7},{7,4},{8,9},{9,10},{10,1... | collective-permute-start | bytes 786440 | tf_op jit(solution)/shard_map/ppermute | solution.py:319
  81.6 19.8 %collective-permute-start.28 = (bf16[2,8,64,128]{3,2,1,0:T(8,128)(2,1)S(1)}, bf16[2,8,64,128]{3,2,1,0:T(8,128)(2,1)S(1)}, u32[]{:S(2)}, u32[]{:S(2)}) collective-permute-start(bf16[2,8,64,128]{3,2,1,0:T(8,128)(2,1)S(1)} %get-tuple-element.63), channel_id=1, source_target_pairs={{0,3},{1,0},{2,1},{3,2},{4,7},{5,4},{6,5},{7,6},{8,11},{9,8},{10,9... | collective-permute-start | bytes 786440 | tf_op jit(solution)/shard_map/ppermute | solution.py:319
  84.1 17.3 %collective-permute-start.29 = (bf16[2,8,64,128]{3,2,1,0:T(8,128)(2,1)S(1)}, bf16[2,8,64,128]{3,2,1,0:T(8,128)(2,1)S(1)}, u32[]{:S(2)}, u32[]{:S(2)}) collective-permute-start(bf16[2,8,64,128]{3,2,1,0:T(8,128)(2,1)S(1)} %get-tuple-element.64), channel_id=1, source_target_pairs={{0,2},{1,3},{2,0},{3,1},{4,6},{5,7},{6,4},{7,5},{8,10},{9,11},{10,... | collective-permute-start | bytes 786440 | tf_op jit(solution)/shard_map/ppermute | solution.py:319
  97.8 14.5 %collective-permute-start.42 = (bf16[2,288,128]{2,1,0:T(8,128)(2,1)S(1)}, bf16[2,288,128]{2,1,0:T(8,128)(2,1)S(1)}, u32[]{:S(2)}, u32[]{:S(2)}) collective-permute-start(bf16[2,288,128]{2,1,0:T(8,128)(2,1)S(1)} %pair_sum.1.refs_0_), channel_id=1, source_target_pairs={{0,64},{8,72},{16,80},{24,88},{32,96},{40,104},{48,112},{56,120},{... | collective-permute-start | bytes 442376 | tf_op jit(solution)/shard_map/ppermute | solution.py:448
  99.0 13.4 %collective-permute-start.40 = (bf16[2,288,128]{2,1,0:T(8,128)(2,1)S(1)}, bf16[2,288,128]{2,1,0:T(8,128)(2,1)S(1)}, u32[]{:S(2)}, u32[]{:S(2)}) collective-permute-start(bf16[2,288,128]{2,1,0:T(8,128)(2,1)S(1)} %pair_sum.1.refs_0_), channel_id=1, source_target_pairs={{0,96},{8,104},{16,112},{24,120},{32,0},{40,8},{48,16},{56,24},{64... | collective-permute-start | bytes 442376 | tf_op jit(solution)/shard_map/ppermute | solution.py:448
  101.3 11.5 %collective-permute-start.38 = (bf16[2,288,128]{2,1,0:T(8,128)(2,1)S(1)}, bf16[2,288,128]{2,1,0:T(8,128)(2,1)S(1)}, u32[]{:S(2)}, u32[]{:S(2)}) collective-permute-start(bf16[2,288,128]{2,1,0:T(8,128)(2,1)S(1)} %pair_sum.1.refs_0_), channel_id=1, source_target_pairs={{0,32},{8,40},{16,48},{24,56},{32,64},{40,72},{48,80},{56,88},{64,... | collective-permute-start | bytes 442376 | tf_op jit(solution)/shard_map/ppermute | solution.py:448
  108.1 6.5 %collective-permute-start.37 = (bf16[2,288,128]{2,1,0:T(8,128)(2,1)S(1)}, bf16[2,288,128]{2,1,0:T(8,128)(2,1)S(1)}, u32[]{:S(2)}, u32[]{:S(2)}) collective-permute-start(bf16[2,288,128]{2,1,0:T(8,128)(2,1)S(1)} %pair_sum.1.refs_0_), channel_id=1, source_target_pairs={{0,8},{8,0},{16,24},{24,16},{32,40},{40,32},{48,56},{56,48},{64,72... | collective-permute-start | bytes 442376 | tf_op jit(solution)/shard_map/ppermute | solution.py:449
  (24 other events, 142.9 us)

commit v3 on v2

--- a/solution.py
+++ b/solution.py
@@ -41,9 +41,7 @@
     return pairs
 
 
-GATES = (1, 0, 0, 4, 0, 0)
-NG = (3, 0, 0, 0)
-HINT = {'act_grad': 21, 'hidden': 26, 'act_grad_sum': 0, 'activation': 0, 'pre_grad': 0, 'second_grad': 0, 'band_grad': 0, 'first_grad': 0, 'band_grad_sum': 0, 'core_sum': 0, 'filter_sum': 0, 'pair_sum': 0, 'own_half': 10, 'other_half': 0, 'band_grad_total': 0}
+HINT = {'act_grad': 0, 'hidden': 26, 'act_grad_sum': 0, 'activation': 0, 'pre_grad': 0, 'second_grad': 0, 'band_grad': 0, 'first_grad': 0, 'band_grad_sum': 0, 'core_sum': 0, 'filter_sum': 25, 'pair_sum': 0, 'own_half': 10, 'other_half': 0, 'band_grad_total': 0}
 
 
 def hint(name):
@@ -383,7 +381,7 @@
 
     x_pieces = gather_ch(x_rows)
     cot_stack, act_pieces = input_grad(
-        act_grad_kernel, w2, at, after(cot_rows, x_pieces[GATES[3]]), x_above, x_below, name="act_grad"
+        act_grad_kernel, w2, at, after(cot_rows, x_pieces[4]), x_above, x_below, name="act_grad"
     )
     hid, stats, x_full = call(
         conv_kernel,
@@ -395,8 +393,8 @@
         name="hidden",
     )
     stats = sum_rows_near(stats)
-    *act_parts, _ = scatter_ch([after(p, x_pieces[GATES[5]]) if GATES[5] else p for p in act_pieces], "act_grad_sum", stats)
-    stats = sum_rows_far(stats, act_parts[0] if GATES[0] else None)
+    *act_parts, _ = scatter_ch(act_pieces, "act_grad_sum", stats)
+    stats = sum_rows_far(stats, act_parts[0])
     (act,) = call(
         functools.partial(act_kernel, cells), dict(shapes=[(strip, BF)]),
         hid, stats, gain, shift, name="activation",
@@ -407,19 +405,17 @@
     )
     act_all = gather_ch_pairs(act)
     sums = sum_rows_near(sums)
-    if GATES[1] == 2:
-        sums = after(sums, act_all[0])
-    sums = sum_rows_far(sums, act_all[0] if GATES[1] == 1 else None)
+    sums = after(sums, act_all[0])
+    sums = sum_rows_far(sums)
     above, below = neighbours(
         jnp.stack([pre[0], hid[0]]), jnp.stack([pre[ROWS - 1], hid[ROWS - 1]])
     )
     half = ((2 * STACK, W), BF)
     hg_stack, band_pieces = input_grad(
         functools.partial(band_grad_kernel, cells), w1,
-        at, hid, stats, gain, pre, after(sums, act_all[1 : 1 + NG[0]]) if NG[0] else sums, above, below,
+        at, hid, stats, gain, pre, after(sums, act_all[1:3]), above, below,
         name="band_grad",
     )
-    *band_parts, band_got = scatter_ch(band_pieces, "band_grad_sum")
     keep1, send1 = call(
         filter_kernel, dict(shapes=[half, half]), at, hg_stack, x_full,
         name="first_grad",
@@ -428,23 +424,22 @@
     keep2, send2 = call(
         gathered_filter_kernel,
         dict(shapes=[half, half], scratch=[pltpu.VMEM((ROWS, C, W), BF)]),
-        at, cot_stack if GATES[4] == 0 else after(cot_stack, hg_stack if GATES[4] == 1 else keep1), *act_all,
+        at, cot_stack, *act_all,
         name="second_grad",
     )
     recv2 = lax.ppermute(send2, "rows", row_pairs(0, 0, 1))
     share = ((2, PIECE, W), BF)
     parts = call(
-        core_sum_kernel, dict(shapes=[share] * 4), at, after(keep1, band_got[0]) if NG[1] else keep1, recv1, keep2, recv2, name="core_sum"
+        core_sum_kernel, dict(shapes=[share] * 4), at, keep1, recv1, keep2, recv2, name="core_sum"
     )
     got = [lax.ppermute(parts[k], "rows", row_pairs(k, 0, 0)) for k in (1, 3, 2)]
+    *band_parts, band_got = scatter_ch([after(p, parts[0]) for p in band_pieces], "band_grad_sum")
     gain_grad, shift_grad = sums[0, :OWN], sums[0, OWN:]
-    part = sum_four(after(parts[0], (gain_grad, shift_grad, *band_parts[: NG[2]])), *got, name="filter_sum")
+    part = sum_four(after(parts[0], (gain_grad, shift_grad)), *got, name="filter_sum")
     part = call(
         two_sum_kernel, dict(shapes=[share]),
-        part, lax.ppermute(after(part, band_parts[0]) if GATES[2] == 1 else part, "rows", row_pairs(0, 1, 0)), name="pair_sum",
+        part, lax.ppermute(part, "rows", row_pairs(0, 1, 0)), name="pair_sum",
     )[0]
-    if NG[3]:
-        part = after(part, band_parts[1])
     mine = [part] + [lax.ppermute(part, "rows", row_pairs(k, 0, 0)) for k in Z_ORDER[1:]]
     theirs = [lax.ppermute(p, "rows", row_pairs(0, 0, 1)) for p in mine]
     grads = place(0, at, mine, (), "own_half")

time: 117 us -> 115 us (0.983)
  waiting for transfers between devices: 29.3 us -> 25 us
  starting transfers between devices: 70.1 us -> 72.9 us
    ppermute x2, starting transfers between devices: 3.5 us -> 0.31 us  [scatter_ch(): return (near, lax.ppermute(far, 'ch', ch_pairs(1, 0)), got)]
    ppermute x1, waiting for transfers between devices: 3.25 us -> 0.25 us  [gather_ch(): other = lax.ppermute(value, 'ch', ch_pairs(1, 0))]
    ppermute x3, waiting for transfers between devices: 3.98 us -> 1.33 us  [body(): lax.ppermute(parts[k], 'rows', row_pairs(k, 0, 0))]
    ppermute x3, starting transfers between devices: 2.79 us -> 4.41 us  [gather_ch(): far = [lax.ppermute(other, 'ch', ch_pairs(0, k)) for k in (1, 3, 2)]]
    ppermute x6, waiting for transfers between devices: 0.02 us -> 1.56 us  [scatter_ch(): lax.ppermute(p, 'ch', ch_pairs(0, k))]
    ppermute x4, starting transfers between devices: 8.64 us -> 10.1 us  [sum_rows_far(): lax.ppermute(value, 'rows', [(i, i ^ mask) for i in range(16)])]
    ppermute x6, starting transfers between devices: 8.05 us -> 9.4 us  [scatter_ch(): lax.ppermute(p, 'ch', ch_pairs(0, k))]
    ppermute x3, starting transfers between devices: 2.04 us -> 3.39 us  [gather_ch_pairs(): lax.ppermute(both, 'ch', ch_pairs(0, k))]
where the time goes in v3:
time: 115 us
  starting transfers between devices  72.9 us (63%)
  waiting for transfers between devices  25 us (22%)
  Pallas kernels  13 us (11%)
  local copies, waits for them, and re-layouts  2.75 us (2%)
  between operations  1.19 us (1%)
    ppermute x4, starting transfers between devices, neighbours(): return (lax.ppermute(last, 'rows', up), lax.ppermute(first, 'rows', down))  13.4 us
    ppermute x4, starting transfers between devices, sum_rows_far(): lax.ppermute(value, 'rows', [(i, i ^ mask) for i in range(16)])  10.1 us
    pallas_call x13, Pallas kernels, call(): pl.pallas_call(kernel, out_shape=shapes, in_specs=[SMEM if a.dtype == jnp...  9.79 us
    ppermute x6, starting transfers between devices, scatter_ch(): lax.ppermute(p, 'ch', ch_pairs(0, k))  9.4 us
    ppermute x4, starting transfers between devices, sum_rows_near(): value = value + lax.ppermute(value, 'rows', row_pairs(dz, dx, dc))  7.51 us
    ppermute x4, starting transfers between devices, body(): theirs = [lax.ppermute(p, 'rows', row_pairs(0, 0, 1)) for p in mine]  5.65 us
    ppermute x2, waiting for transfers between devices, scatter_ch(): return (near, lax.ppermute(far, 'ch', ch_pairs(1, 0)), got)  5.22 us
    ppermute x3, starting transfers between devices, body(): lax.ppermute(parts[k], 'rows', row_pairs(k, 0, 0))  5 us
  transfers between devices with their start and end apart: 44, of which 18 were waited for; matrix products, arithmetic and copies ran while one was open for 1% of the time, Pallas kernels for 9%

profile of v3, /device:TPU:1, one launch (start us, length us, event | category | flops | bytes accessed | tf_op | source)
XLA Modules:
  0.0 115.1 jit_solution(9097867353034781727)
XLA Ops:
  2.0 3.3 %collective-permute-start.1 = (bf16[128,128]{1,0:T(8,128)(2,1)S(1)}, bf16[128,128]{1,0:T(8,128)(2,1)S(1)}, u32[]{:S(2)}, u32[]{:S(2)}) collective-permute-start(bf16[128,128]{1,0:T(8,128)(2,1)S(1)} %pad_maximum_fusion.5), channel_id=1, source_target_pairs={{8,0},{16,8},{24,16},{32,24},{40,32},{48,40},{56,48},{64,56},{72,6... | collective-permute-start | bytes 98312 | tf_op jit(solution)/shard_map/ppermute | solution.py:329
  5.3 3.1 %collective-permute-start = (bf16[128,128]{1,0:T(8,128)(2,1)S(1)}, bf16[128,128]{1,0:T(8,128)(2,1)S(1)}, u32[]{:S(2)}, u32[]{:S(2)}) collective-permute-start(bf16[128,128]{1,0:T(8,128)(2,1)S(1)} %pad_maximum_fusion.4), channel_id=1, source_target_pairs={{0,8},{8,16},{16,24},{24,32},{32,40},{40,48},{48,56},{56,64},{64,7... | collective-permute-start | bytes 98312 | tf_op jit(solution)/shard_map/ppermute | solution.py:329
  9.5 2.8 %collective-permute-start.2 = (bf16[10,64,128]{2,1,0:T(8,128)(2,1)S(1)}, bf16[10,64,128]{2,1,0:T(8,128)(2,1)S(1)}, u32[]{:S(2)}, u32[]{:S(2)}) collective-permute-start(bf16[10,64,128]{2,1,0:T(8,128)(2,1)S(1)} %pad_maximum_fusion.1.refs_0_), channel_id=1, source_target_pairs={{0,4},{1,5},{2,6},{3,7},{4,0},{5,1},{6,2},{7,3},{8,12},{9,13},{10,... | collective-permute-start | bytes 491528 | tf_op jit(solution)/shard_map/ppermute | solution.py:299
  12.3 2.9 %collective-permute-start.5 = (bf16[10,64,128]{2,1,0:T(8,128)(2,1)S(1)}, bf16[10,64,128]{2,1,0:T(8,128)(2,1)S(1)}, u32[]{:S(2)}, u32[]{:S(2)}) collective-permute-start(bf16[10,64,128]{2,1,0:T(8,128)(2,1)S(1)} %pad_maximum_fusion.1.refs_0_), channel_id=1, source_target_pairs={{0,2},{1,3},{2,0},{3,1},{4,6},{5,7},{6,4},{7,5},{8,10},{9,11},{10,... | collective-permute-start | bytes 491528 | tf_op jit(solution)/shard_map/ppermute | solution.py:300
  16.9 2.7 %collective-permute-start.8 = (bf16[10,64,128]{2,1,0:T(8,128)(2,1)S(1)}, bf16[10,64,128]{2,1,0:T(8,128)(2,1)S(1)}, u32[]{:S(2)}, u32[]{:S(2)}) collective-permute-start(bf16[10,64,128]{2,1,0:T(8,128)(2,1)S(1)} %collective-permute-done.2.refs_1_), channel_id=1, source_target_pairs={{0,2},{1,3},{2,0},{3,1},{4,6},{5,7},{6,4},{7,5},{8,10},{9,11},{10,... | collective-permute-start | bytes 491528 | tf_op jit(solution)/shard_map/ppermute | solution.py:301
  27.0 3.0 %collective-permute-start.14 = (bf16[2,8,64,128]{3,2,1,0:T(8,128)(2,1)S(1)}, bf16[2,8,64,128]{3,2,1,0:T(8,128)(2,1)S(1)}, u32[]{:S(2)}, u32[]{:S(2)}) collective-permute-start(bf16[2,8,64,128]{3,2,1,0:T(8,128)(2,1)S(1)} %get-tuple-element.59), channel_id=1, source_target_pairs={{0,2},{1,3},{2,0},{3,1},{4,6},{5,7},{6,4},{7,5},{8,10},{9,11},{10,... | collective-permute-start | bytes 786440 | tf_op jit(solution)/shard_map/ppermute | solution.py:317
  34.0 2.5 %collective-permute-start.10 = (f32[8,128]{1,0:T(8,128)S(1)}, f32[8,128]{1,0:T(8,128)S(1)}, u32[]{:S(2)}, u32[]{:S(2)}) collective-permute-start(f32[8,128]{1,0:T(8,128)S(1)} %add.40), channel_id=1, source_target_pairs={{0,16},{8,24},{16,0},{24,8},{32,48},{40,56},{48,32},{56,40},{64,80... | collective-permute-start | bytes 12296 | tf_op jit(solution)/shard_map/ppermute | solution.py:334
  37.8 3.0 %collective-permute-start.11 = (f32[8,128]{1,0:T(8,128)S(1)}, f32[8,128]{1,0:T(8,128)S(1)}, u32[]{:S(2)}, u32[]{:S(2)}) collective-permute-start(f32[8,128]{1,0:T(8,128)S(1)} %add.41), channel_id=1, source_target_pairs={{0,32},{8,40},{16,48},{24,56},{32,0},{40,8},{48,16},{56,24},{64,96... | collective-permute-start | bytes 12296 | tf_op jit(solution)/shard_map/ppermute | solution.py:342
  42.0 4.0 %collective-permute-start.15 = (f32[8,128]{1,0:T(8,128)S(1)}, f32[8,128]{1,0:T(8,128)S(1)}, u32[]{:S(2)}, u32[]{:S(2)}) collective-permute-start(f32[8,128]{1,0:T(8,128)S(1)} %add.42), channel_id=1, source_target_pairs={{0,64},{8,72},{16,80},{24,88},{32,96},{40,104},{48,112},{56,120},{... | collective-permute-start | bytes 12296 | tf_op jit(solution)/shard_map/ppermute | solution.py:342
  47.2 2.1 %collective-permute-start.19 = (bf16[8,64,128]{2,1,0:T(8,128)(2,1)S(1)}, bf16[8,64,128]{2,1,0:T(8,128)(2,1)S(1)}, u32[]{:S(2)}, u32[]{:S(2)}) collective-permute-start(bf16[8,64,128]{2,1,0:T(8,128)(2,1)S(1)} %activation.1), channel_id=1, source_target_pairs={{0,4},{1,5},{2,6},{3,7},{4,0},{5,1},{6,2},{7,3},{8,12},{9,13},{10,... | collective-permute-start | bytes 393224 | tf_op jit(solution)/shard_map/ppermute | solution.py:306
  49.3 2.0 %collective-permute-done.16.far = bf16[8,64,128]{2,1,0:T(8,128)(2,1)S(1)} collective-permute-done((bf16[8,64,128]{2,1,0:T(8,128)(2,1)S(1)}, bf16[8,64,128]{2,1,0:T(8,128)(2,1)S(1)}, u32[]{:S(2)}, u32[]{:S(2)}) %collective-permute-start.16) | collective-permute-done | bytes 131104 | tf_op jit(solution)/shard_map/ppermute | solution.py:323
  51.5 3.6 %collective-permute-start.17 = (f32[8,128]{1,0:T(8,128)S(1)}, f32[8,128]{1,0:T(8,128)S(1)}, u32[]{:S(2)}, u32[]{:S(2)}) collective-permute-start(f32[8,128]{1,0:T(8,128)S(1)} %get-tuple-element.64), channel_id=1, source_target_pairs={{0,8},{8,0},{16,24},{24,16},{32,40},{40,32},{48,56},{56,48},{64,72... | collective-permute-start | bytes 12296 | tf_op jit(solution)/shard_map/ppermute | solution.py:334
  61.1 4.7 %collective-permute-start.24 = (f32[2,64,128]{2,1,0:T(8,128)S(1)}, f32[2,64,128]{2,1,0:T(8,128)S(1)}, u32[]{:S(2)}, u32[]{:S(2)}) collective-permute-start(f32[2,64,128]{2,1,0:T(8,128)S(1)} %pad_maximum_fusion.2), channel_id=1, source_target_pairs={{0,8},{8,16},{16,24},{24,32},{32,40},{40,48},{48,56},{56,64},{64,7... | collective-permute-start | bytes 196616 | tf_op jit(solution)/shard_map/ppermute | solution.py:329
  65.8 2.3 %collective-permute-start.21 = (f32[8,128]{1,0:T(8,128)S(1)}, f32[8,128]{1,0:T(8,128)S(1)}, u32[]{:S(2)}, u32[]{:S(2)}) collective-permute-start(f32[8,128]{1,0:T(8,128)S(1)} %add.46), channel_id=1, source_target_pairs={{0,64},{8,72},{16,80},{24,88},{32,96},{40,104},{48,112},{56,120},{... | collective-permute-start | bytes 12296 | tf_op jit(solution)/shard_map/ppermute | solution.py:342
  68.1 2.0 %collective-permute-done.21 = f32[8,128]{1,0:T(8,128)S(1)} collective-permute-done((f32[8,128]{1,0:T(8,128)S(1)}, f32[8,128]{1,0:T(8,128)S(1)}, u32[]{:S(2)}, u32[]{:S(2)}) %collective-permute-start.21) | collective-permute-done | bytes 4128 | tf_op jit(solution)/shard_map/ppermute | solution.py:342
  70.1 2.3 %collective-permute-start.25 = (f32[2,64,128]{2,1,0:T(8,128)S(1)}, f32[2,64,128]{2,1,0:T(8,128)S(1)}, u32[]{:S(2)}, u32[]{:S(2)}) collective-permute-start(f32[2,64,128]{2,1,0:T(8,128)S(1)} %pad_maximum_fusion.3), channel_id=1, source_target_pairs={{8,0},{16,8},{24,16},{32,24},{40,32},{48,40},{56,48},{64,56},{72,6... | collective-permute-start | bytes 196616 | tf_op jit(solution)/shard_map/ppermute | solution.py:329
  75.7 2.0 %band_grad.1 = (bf16[576,1024]{1,0:T(8,128)(2,1)S(1)}, bf16[2,8,64,128]{3,2,1,0:T(8,128)(2,1)S(1)}, bf16[2,8,64,128]{3,2,1,0:T(8,128)(2,1)S(1)}, bf16[2,8,64,128...) custom-call(s32[6]{0:T(128)S(1)} %stack.42.at, f32[8,64,128]{2,1,0:T(8,128)S(1)} %get-tuple-element.52.hid, ...), custom_call_target="tpu_custom_call" | custom-call | tf_op jit(solution)/shard_map/band_grad/pallas_call | solution.py:53
  81.9 2.2 %collective-permute-start.34 = (bf16[2,288,128]{2,1,0:T(8,128)(2,1)S(1)}, bf16[2,288,128]{2,1,0:T(8,128)(2,1)S(1)}, u32[]{:S(2)}, u32[]{:S(2)}) collective-permute-start(bf16[2,288,128]{2,1,0:T(8,128)(2,1)S(1)} %get-tuple-element.87), channel_id=1, source_target_pairs={{0,96},{8,104},{16,112},{24,120},{32,0},{40,8},{48,16},{56,24},{64... | collective-permute-start | bytes 442376 | tf_op jit(solution)/shard_map/ppermute | solution.py:435
  84.1 2.3 %collective-permute-start.35 = (bf16[2,288,128]{2,1,0:T(8,128)(2,1)S(1)}, bf16[2,288,128]{2,1,0:T(8,128)(2,1)S(1)}, u32[]{:S(2)}, u32[]{:S(2)}) collective-permute-start(bf16[2,288,128]{2,1,0:T(8,128)(2,1)S(1)} %get-tuple-element.88), channel_id=1, source_target_pairs={{0,64},{8,72},{16,80},{24,88},{32,96},{40,104},{48,112},{56,120},{... | collective-permute-start | bytes 442376 | tf_op jit(solution)/shard_map/ppermute | solution.py:435
  87.0 2.7 %collective-permute-start.30 = (bf16[2,8,64,128]{3,2,1,0:T(8,128)(2,1)S(1)}, bf16[2,8,64,128]{3,2,1,0:T(8,128)(2,1)S(1)}, u32[]{:S(2)}, u32[]{:S(2)}) collective-permute-start(bf16[2,8,64,128]{3,2,1,0:T(8,128)(2,1)S(1)} %get-tuple-element.80), channel_id=1, source_target_pairs={{0,3},{1,0},{2,1},{3,2},{4,7},{5,4},{6,5},{7,6},{8,11},{9,8},{10,9... | collective-permute-start | bytes 786440 | tf_op jit(solution)/shard_map/ppermute | solution.py:317
  92.6 4.2 %collective-permute-done.36.b = bf16[2,288,128]{2,1,0:T(8,128)(2,1)S(1)} collective-permute-done((bf16[2,288,128]{2,1,0:T(8,128)(2,1)S(1)}, bf16[2,288,128]{2,1,0:T(8,128)(2,1)S(1)}, u32[]{:S(2)}, u32[]{:S(2)}) %collective-permute-start.36) | collective-permute-done | bytes 147488 | tf_op jit(solution)/shard_map/ppermute | solution.py:441
  101.9 2.1 %collective-permute-start.37 = (bf16[2,288,128]{2,1,0:T(8,128)(2,1)S(1)}, bf16[2,288,128]{2,1,0:T(8,128)(2,1)S(1)}, u32[]{:S(2)}, u32[]{:S(2)}) collective-permute-start(bf16[2,288,128]{2,1,0:T(8,128)(2,1)S(1)} %pair_sum.1.refs_0_), channel_id=1, source_target_pairs={{0,8},{8,0},{16,24},{24,16},{32,40},{40,32},{48,56},{56,48},{64,72... | collective-permute-start | bytes 442376 | tf_op jit(solution)/shard_map/ppermute | solution.py:444
  104.0 3.2 %collective-permute-done.32.far = bf16[8,64,128]{2,1,0:T(8,128)(2,1)S(1)} collective-permute-done((bf16[8,64,128]{2,1,0:T(8,128)(2,1)S(1)}, bf16[8,64,128]{2,1,0:T(8,128)(2,1)S(1)}, u32[]{:S(2)}, u32[]{:S(2)}) %collective-permute-start.32) | collective-permute-done | bytes 131104 | tf_op jit(solution)/shard_map/ppermute | solution.py:323
  108.0 3.1 %collective-permute-start.43 = (bf16[2,288,128]{2,1,0:T(8,128)(2,1)S(1)}, bf16[2,288,128]{2,1,0:T(8,128)(2,1)S(1)}, u32[]{:S(2)}, u32[]{:S(2)}) collective-permute-start(bf16[2,288,128]{2,1,0:T(8,128)(2,1)S(1)} %collective-permute-done.42.refs_3_), channel_id=1, source_target_pairs={{0,8},{8,0},{16,24},{24,16},{32,40},{40,32},{48,56},{56,48},{64,72... | collective-permute-start | bytes 442376 | tf_op jit(solution)/shard_map/ppermute | solution.py:444
  (113 shorter events, 46.0 us)
Async XLA Ops:
  12.3 8.1 %collective-permute-start.5 = (bf16[10,64,128]{2,1,0:T(8,128)(2,1)S(1)}, bf16[10,64,128]{2,1,0:T(8,128)(2,1)S(1)}, u32[]{:S(2)}, u32[]{:S(2)}) collective-permute-start(bf16[10,64,128]{2,1,0:T(8,128)(2,1)S(1)} %pad_maximum_fusion.1.refs_0_), channel_id=1, source_target_pairs={{0,2},{1,3},{2,0},{3,1},{4,6},{5,7},{6,4},{7,5},{8,10},{9,11},{10,... | collective-permute-start | bytes 491528 | tf_op jit(solution)/shard_map/ppermute | solution.py:300
  15.2 8.7 %collective-permute-start.4 = (bf16[10,64,128]{2,1,0:T(8,128)(2,1)S(1)}, bf16[10,64,128]{2,1,0:T(8,128)(2,1)S(1)}, u32[]{:S(2)}, u32[]{:S(2)}) collective-permute-start(bf16[10,64,128]{2,1,0:T(8,128)(2,1)S(1)} %pad_maximum_fusion.1.refs_0_), channel_id=1, source_target_pairs={{0,3},{1,0},{2,1},{3,2},{4,7},{5,4},{6,5},{7,6},{8,11},{9,8},{10,9... | collective-permute-start | bytes 491528 | tf_op jit(solution)/shard_map/ppermute | solution.py:300
  16.0 8.8 %collective-permute-start.3 = (bf16[10,64,128]{2,1,0:T(8,128)(2,1)S(1)}, bf16[10,64,128]{2,1,0:T(8,128)(2,1)S(1)}, u32[]{:S(2)}, u32[]{:S(2)}) collective-permute-start(bf16[10,64,128]{2,1,0:T(8,128)(2,1)S(1)} %pad_maximum_fusion.1.refs_0_), channel_id=1, source_target_pairs={{0,1},{1,2},{2,3},{3,0},{4,5},{5,6},{6,7},{7,4},{8,9},{9,10},{10,1... | collective-permute-start | bytes 491528 | tf_op jit(solution)/shard_map/ppermute | solution.py:300
  16.9 10.1 %collective-permute-start.8 = (bf16[10,64,128]{2,1,0:T(8,128)(2,1)S(1)}, bf16[10,64,128]{2,1,0:T(8,128)(2,1)S(1)}, u32[]{:S(2)}, u32[]{:S(2)}) collective-permute-start(bf16[10,64,128]{2,1,0:T(8,128)(2,1)S(1)} %collective-permute-done.2.refs_1_), channel_id=1, source_target_pairs={{0,2},{1,3},{2,0},{3,1},{4,6},{5,7},{6,4},{7,5},{8,10},{9,11},{10,... | collective-permute-start | bytes 491528 | tf_op jit(solution)/shard_map/ppermute | solution.py:301
  19.6 11.3 %collective-permute-start.7 = (bf16[10,64,128]{2,1,0:T(8,128)(2,1)S(1)}, bf16[10,64,128]{2,1,0:T(8,128)(2,1)S(1)}, u32[]{:S(2)}, u32[]{:S(2)}) collective-permute-start(bf16[10,64,128]{2,1,0:T(8,128)(2,1)S(1)} %collective-permute-done.2.refs_1_), channel_id=1, source_target_pairs={{0,3},{1,0},{2,1},{3,2},{4,7},{5,4},{6,5},{7,6},{8,11},{9,8},{10,9... | collective-permute-start | bytes 491528 | tf_op jit(solution)/shard_map/ppermute | solution.py:301
  20.4 10.6 %collective-permute-start.6 = (bf16[10,64,128]{2,1,0:T(8,128)(2,1)S(1)}, bf16[10,64,128]{2,1,0:T(8,128)(2,1)S(1)}, u32[]{:S(2)}, u32[]{:S(2)}) collective-permute-start(bf16[10,64,128]{2,1,0:T(8,128)(2,1)S(1)} %collective-permute-done.2.refs_1_), channel_id=1, source_target_pairs={{0,1},{1,2},{2,3},{3,0},{4,5},{5,6},{6,7},{7,4},{8,9},{9,10},{10,1... | collective-permute-start | bytes 491528 | tf_op jit(solution)/shard_map/ppermute | solution.py:301
  23.9 17.9 %collective-permute-start.12 = (bf16[2,8,64,128]{3,2,1,0:T(8,128)(2,1)S(1)}, bf16[2,8,64,128]{3,2,1,0:T(8,128)(2,1)S(1)}, u32[]{:S(2)}, u32[]{:S(2)}) collective-permute-start(bf16[2,8,64,128]{3,2,1,0:T(8,128)(2,1)S(1)} %get-tuple-element.57), channel_id=1, source_target_pairs={{0,1},{1,2},{2,3},{3,0},{4,5},{5,6},{6,7},{7,4},{8,9},{9,10},{10,1... | collective-permute-start | bytes 786440 | tf_op jit(solution)/shard_map/ppermute | solution.py:317
  24.8 17.0 %collective-permute-start.13 = (bf16[2,8,64,128]{3,2,1,0:T(8,128)(2,1)S(1)}, bf16[2,8,64,128]{3,2,1,0:T(8,128)(2,1)S(1)}, u32[]{:S(2)}, u32[]{:S(2)}) collective-permute-start(bf16[2,8,64,128]{3,2,1,0:T(8,128)(2,1)S(1)} %get-tuple-element.58), channel_id=1, source_target_pairs={{0,3},{1,0},{2,1},{3,2},{4,7},{5,4},{6,5},{7,6},{8,11},{9,8},{10,9... | collective-permute-start | bytes 786440 | tf_op jit(solution)/shard_map/ppermute | solution.py:317
  27.0 14.8 %collective-permute-start.14 = (bf16[2,8,64,128]{3,2,1,0:T(8,128)(2,1)S(1)}, bf16[2,8,64,128]{3,2,1,0:T(8,128)(2,1)S(1)}, u32[]{:S(2)}, u32[]{:S(2)}) collective-permute-start(bf16[2,8,64,128]{3,2,1,0:T(8,128)(2,1)S(1)} %get-tuple-element.59), channel_id=1, source_target_pairs={{0,2},{1,3},{2,0},{3,1},{4,6},{5,7},{6,4},{7,5},{8,10},{9,11},{10,... | collective-permute-start | bytes 786440 | tf_op jit(solution)/shard_map/ppermute | solution.py:317
  47.2 9.7 %collective-permute-start.19 = (bf16[8,64,128]{2,1,0:T(8,128)(2,1)S(1)}, bf16[8,64,128]{2,1,0:T(8,128)(2,1)S(1)}, u32[]{:S(2)}, u32[]{:S(2)}) collective-permute-start(bf16[8,64,128]{2,1,0:T(8,128)(2,1)S(1)} %activation.1), channel_id=1, source_target_pairs={{0,4},{1,5},{2,6},{3,7},{4,0},{5,1},{6,2},{7,3},{8,12},{9,13},{10,... | collective-permute-start | bytes 393224 | tf_op jit(solution)/shard_map/ppermute | solution.py:306
  56.9 15.5 %collective-permute-start.27 = (bf16[2,8,64,128]{3,2,1,0:T(8,128)(2,1)S(1)}, bf16[2,8,64,128]{3,2,1,0:T(8,128)(2,1)S(1)}, u32[]{:S(2)}, u32[]{:S(2)}) collective-permute-start(bf16[2,8,64,128]{3,2,1,0:T(8,128)(2,1)S(1)} %pad_maximum_fusion.refs_0_), channel_id=1, source_target_pairs={{0,2},{1,3},{2,0},{3,1},{4,6},{5,7},{6,4},{7,5},{8,10},{9,11},{10,... | collective-permute-start | bytes 786440 | tf_op jit(solution)/shard_map/ppermute | solution.py:307
  58.8 13.6 %collective-permute-start.23 = (bf16[2,8,64,128]{3,2,1,0:T(8,128)(2,1)S(1)}, bf16[2,8,64,128]{3,2,1,0:T(8,128)(2,1)S(1)}, u32[]{:S(2)}, u32[]{:S(2)}) collective-permute-start(bf16[2,8,64,128]{3,2,1,0:T(8,128)(2,1)S(1)} %pad_maximum_fusion.refs_0_), channel_id=1, source_target_pairs={{0,3},{1,0},{2,1},{3,2},{4,7},{5,4},{6,5},{7,6},{8,11},{9,8},{10,9... | collective-permute-start | bytes 786440 | tf_op jit(solution)/shard_map/ppermute | solution.py:307
  60.1 12.3 %collective-permute-start.22 = (bf16[2,8,64,128]{3,2,1,0:T(8,128)(2,1)S(1)}, bf16[2,8,64,128]{3,2,1,0:T(8,128)(2,1)S(1)}, u32[]{:S(2)}, u32[]{:S(2)}) collective-permute-start(bf16[2,8,64,128]{3,2,1,0:T(8,128)(2,1)S(1)} %pad_maximum_fusion.refs_0_), channel_id=1, source_target_pairs={{0,1},{1,2},{2,3},{3,0},{4,5},{5,6},{6,7},{7,4},{8,9},{9,10},{10,1... | collective-permute-start | bytes 786440 | tf_op jit(solution)/shard_map/ppermute | solution.py:307
  61.1 13.5 %collective-permute-start.24 = (f32[2,64,128]{2,1,0:T(8,128)S(1)}, f32[2,64,128]{2,1,0:T(8,128)S(1)}, u32[]{:S(2)}, u32[]{:S(2)}) collective-permute-start(f32[2,64,128]{2,1,0:T(8,128)S(1)} %pad_maximum_fusion.2), channel_id=1, source_target_pairs={{0,8},{8,16},{16,24},{24,32},{32,40},{40,48},{48,56},{56,64},{64,7... | collective-permute-start | bytes 196616 | tf_op jit(solution)/shard_map/ppermute | solution.py:329
  81.4 8.3 %collective-permute-start.33 = (bf16[2,288,128]{2,1,0:T(8,128)(2,1)S(1)}, bf16[2,288,128]{2,1,0:T(8,128)(2,1)S(1)}, u32[]{:S(2)}, u32[]{:S(2)}) collective-permute-start(bf16[2,288,128]{2,1,0:T(8,128)(2,1)S(1)} %get-tuple-element.86), channel_id=1, source_target_pairs={{0,32},{8,40},{16,48},{24,56},{32,64},{40,72},{48,80},{56,88},{64,... | collective-permute-start | bytes 442376 | tf_op jit(solution)/shard_map/ppermute | solution.py:435
  81.9 8.8 %collective-permute-start.34 = (bf16[2,288,128]{2,1,0:T(8,128)(2,1)S(1)}, bf16[2,288,128]{2,1,0:T(8,128)(2,1)S(1)}, u32[]{:S(2)}, u32[]{:S(2)}) collective-permute-start(bf16[2,288,128]{2,1,0:T(8,128)(2,1)S(1)} %get-tuple-element.87), channel_id=1, source_target_pairs={{0,96},{8,104},{16,112},{24,120},{32,0},{40,8},{48,16},{56,24},{64... | collective-permute-start | bytes 442376 | tf_op jit(solution)/shard_map/ppermute | solution.py:435
  84.1 7.9 %collective-permute-start.35 = (bf16[2,288,128]{2,1,0:T(8,128)(2,1)S(1)}, bf16[2,288,128]{2,1,0:T(8,128)(2,1)S(1)}, u32[]{:S(2)}, u32[]{:S(2)}) collective-permute-start(bf16[2,288,128]{2,1,0:T(8,128)(2,1)S(1)} %get-tuple-element.88), channel_id=1, source_target_pairs={{0,64},{8,72},{16,80},{24,88},{32,96},{40,104},{48,112},{56,120},{... | collective-permute-start | bytes 442376 | tf_op jit(solution)/shard_map/ppermute | solution.py:435
  87.0 12.7 %collective-permute-start.29 = (bf16[2,8,64,128]{3,2,1,0:T(8,128)(2,1)S(1)}, bf16[2,8,64,128]{3,2,1,0:T(8,128)(2,1)S(1)}, u32[]{:S(2)}, u32[]{:S(2)}) collective-permute-start(bf16[2,8,64,128]{3,2,1,0:T(8,128)(2,1)S(1)} %get-tuple-element.78), channel_id=1, source_target_pairs={{0,1},{1,2},{2,3},{3,0},{4,5},{5,6},{6,7},{7,4},{8,9},{9,10},{10,1... | collective-permute-start | bytes 786440 | tf_op jit(solution)/shard_map/ppermute | solution.py:317
  87.0 13.2 %collective-permute-start.30 = (bf16[2,8,64,128]{3,2,1,0:T(8,128)(2,1)S(1)}, bf16[2,8,64,128]{3,2,1,0:T(8,128)(2,1)S(1)}, u32[]{:S(2)}, u32[]{:S(2)}) collective-permute-start(bf16[2,8,64,128]{3,2,1,0:T(8,128)(2,1)S(1)} %get-tuple-element.80), channel_id=1, source_target_pairs={{0,3},{1,0},{2,1},{3,2},{4,7},{5,4},{6,5},{7,6},{8,11},{9,8},{10,9... | collective-permute-start | bytes 786440 | tf_op jit(solution)/shard_map/ppermute | solution.py:317
  89.7 12.0 %collective-permute-start.31 = (bf16[2,8,64,128]{3,2,1,0:T(8,128)(2,1)S(1)}, bf16[2,8,64,128]{3,2,1,0:T(8,128)(2,1)S(1)}, u32[]{:S(2)}, u32[]{:S(2)}) collective-permute-start(bf16[2,8,64,128]{3,2,1,0:T(8,128)(2,1)S(1)} %get-tuple-element.82), channel_id=1, source_target_pairs={{0,2},{1,3},{2,0},{3,1},{4,6},{5,7},{6,4},{7,5},{8,10},{9,11},{10,... | collective-permute-start | bytes 786440 | tf_op jit(solution)/shard_map/ppermute | solution.py:317
  96.8 11.2 %collective-permute-start.42 = (bf16[2,288,128]{2,1,0:T(8,128)(2,1)S(1)}, bf16[2,288,128]{2,1,0:T(8,128)(2,1)S(1)}, u32[]{:S(2)}, u32[]{:S(2)}) collective-permute-start(bf16[2,288,128]{2,1,0:T(8,128)(2,1)S(1)} %pair_sum.1.refs_0_), channel_id=1, source_target_pairs={{0,64},{8,72},{16,80},{24,88},{32,96},{40,104},{48,112},{56,120},{... | collective-permute-start | bytes 442376 | tf_op jit(solution)/shard_map/ppermute | solution.py:443
  98.6 12.5 %collective-permute-start.40 = (bf16[2,288,128]{2,1,0:T(8,128)(2,1)S(1)}, bf16[2,288,128]{2,1,0:T(8,128)(2,1)S(1)}, u32[]{:S(2)}, u32[]{:S(2)}) collective-permute-start(bf16[2,288,128]{2,1,0:T(8,128)(2,1)S(1)} %pair_sum.1.refs_0_), channel_id=1, source_target_pairs={{0,96},{8,104},{16,112},{24,120},{32,0},{40,8},{48,16},{56,24},{64... | collective-permute-start | bytes 442376 | tf_op jit(solution)/shard_map/ppermute | solution.py:443
  99.6 11.5 %collective-permute-start.38 = (bf16[2,288,128]{2,1,0:T(8,128)(2,1)S(1)}, bf16[2,288,128]{2,1,0:T(8,128)(2,1)S(1)}, u32[]{:S(2)}, u32[]{:S(2)}) collective-permute-start(bf16[2,288,128]{2,1,0:T(8,128)(2,1)S(1)} %pair_sum.1.refs_0_), channel_id=1, source_target_pairs={{0,32},{8,40},{16,48},{24,56},{32,64},{40,72},{48,80},{56,88},{64,... | collective-permute-start | bytes 442376 | tf_op jit(solution)/shard_map/ppermute | solution.py:443
  101.9 11.3 %collective-permute-start.37 = (bf16[2,288,128]{2,1,0:T(8,128)(2,1)S(1)}, bf16[2,288,128]{2,1,0:T(8,128)(2,1)S(1)}, u32[]{:S(2)}, u32[]{:S(2)}) collective-permute-start(bf16[2,288,128]{2,1,0:T(8,128)(2,1)S(1)} %pair_sum.1.refs_0_), channel_id=1, source_target_pairs={{0,8},{8,0},{16,24},{24,16},{32,40},{40,32},{48,56},{56,48},{64,72... | collective-permute-start | bytes 442376 | tf_op jit(solution)/shard_map/ppermute | solution.py:444
  (24 other events, 167.5 us)

commit v4 on v3

--- a/solution.py
+++ b/solution.py
@@ -344,8 +344,7 @@
 
 
 def final_kernel(near, far, out):
-    for r in range(ROWS):
-        out[r] = (near[r] + far[r].astype(F32)).astype(BF)
+    out[...] = jnp.swapaxes(near[...] + far[...].astype(F32), 0, 1).astype(BF)
 
 
 def input_grad(kernel, w, *args, name):
@@ -444,10 +443,10 @@
     theirs = [lax.ppermute(p, "rows", row_pairs(0, 0, 1)) for p in mine]
     grads = place(0, at, mine, (), "own_half")
     first_grad, second_grad = place(1, at, theirs, grads, "other_half")
-    (band,) = call(final_kernel, dict(shapes=[(strip, BF)]), *band_parts, name="band_grad_total")
+    (band,) = call(final_kernel, dict(shapes=[((OWN, ROWS, W), BF)]), *band_parts, name="band_grad_total")
     shape = (3, 3, OWN, C)
     return (
-        jnp.transpose(band, (1, 0, 2)),
+        band,
         first_grad.reshape(shape),
         second_grad.reshape(shape),
         gain_grad,

time: 115 us -> 115 us (level)
  transfers between devices with their start and end apart: 44 -> 44, of which waited for: 18 -> 18; matrix products, arithmetic and copies ran while one was open for 1% -> 1% of each run, Pallas kernels for 9% -> 10%
where the time goes in v4:
time: 115 us
  starting transfers between devices  72.9 us (63%)
  waiting for transfers between devices  25 us (22%)
  Pallas kernels  13.7 us (12%)
  local copies, waits for them, and re-layouts  2 us (2%)
  between operations  1.19 us (1%)
    ppermute x4, starting transfers between devices, neighbours(): return (lax.ppermute(last, 'rows', up), lax.ppermute(first, 'rows', down))  13.4 us
    pallas_call x13, Pallas kernels, call(): pl.pallas_call(kernel, out_shape=shapes, in_specs=[SMEM if a.dtype == jnp...  10.5 us
    ppermute x4, starting transfers between devices, sum_rows_far(): lax.ppermute(value, 'rows', [(i, i ^ mask) for i in range(16)])  10.1 us
    ppermute x6, starting transfers between devices, scatter_ch(): lax.ppermute(p, 'ch', ch_pairs(0, k))  9.4 us
    ppermute x4, starting transfers between devices, sum_rows_near(): value = value + lax.ppermute(value, 'rows', row_pairs(dz, dx, dc))  7.51 us
    ppermute x4, starting transfers between devices, body(): theirs = [lax.ppermute(p, 'rows', row_pairs(0, 0, 1)) for p in mine]  5.65 us
    ppermute x2, waiting for transfers between devices, scatter_ch(): return (near, lax.ppermute(far, 'ch', ch_pairs(1, 0)), got)  5.22 us
    ppermute x3, starting transfers between devices, body(): lax.ppermute(parts[k], 'rows', row_pairs(k, 0, 0))  5 us
  transfers between devices with their start and end apart: 44, of which 18 were waited for; matrix products, arithmetic and copies ran while one was open for 1% of the time, Pallas kernels for 10%

profile of v4, /device:TPU:1, one launch (start us, length us, event | category | flops | bytes accessed | tf_op | source)
XLA Modules:
  0.0 115.0 jit_solution(5522879979426857050)
XLA Ops:
  2.0 3.3 %collective-permute-start.1 = (bf16[128,128]{1,0:T(8,128)(2,1)S(1)}, bf16[128,128]{1,0:T(8,128)(2,1)S(1)}, u32[]{:S(2)}, u32[]{:S(2)}) collective-permute-start(bf16[128,128]{1,0:T(8,128)(2,1)S(1)} %pad_maximum_fusion.5), channel_id=1, source_target_pairs={{8,0},{16,8},{24,16},{32,24},{40,32},{48,40},{56,48},{64,56},{72,6... | collective-permute-start | bytes 98312 | tf_op jit(solution)/shard_map/ppermute | solution.py:329
  5.3 3.1 %collective-permute-start = (bf16[128,128]{1,0:T(8,128)(2,1)S(1)}, bf16[128,128]{1,0:T(8,128)(2,1)S(1)}, u32[]{:S(2)}, u32[]{:S(2)}) collective-permute-start(bf16[128,128]{1,0:T(8,128)(2,1)S(1)} %pad_maximum_fusion.4), channel_id=1, source_target_pairs={{0,8},{8,16},{16,24},{24,32},{32,40},{40,48},{48,56},{56,64},{64,7... | collective-permute-start | bytes 98312 | tf_op jit(solution)/shard_map/ppermute | solution.py:329
  9.5 2.8 %collective-permute-start.2 = (bf16[10,64,128]{2,1,0:T(8,128)(2,1)S(1)}, bf16[10,64,128]{2,1,0:T(8,128)(2,1)S(1)}, u32[]{:S(2)}, u32[]{:S(2)}) collective-permute-start(bf16[10,64,128]{2,1,0:T(8,128)(2,1)S(1)} %pad_maximum_fusion.1.refs_0_), channel_id=1, source_target_pairs={{0,4},{1,5},{2,6},{3,7},{4,0},{5,1},{6,2},{7,3},{8,12},{9,13},{10,... | collective-permute-start | bytes 491528 | tf_op jit(solution)/shard_map/ppermute | solution.py:299
  12.3 2.9 %collective-permute-start.5 = (bf16[10,64,128]{2,1,0:T(8,128)(2,1)S(1)}, bf16[10,64,128]{2,1,0:T(8,128)(2,1)S(1)}, u32[]{:S(2)}, u32[]{:S(2)}) collective-permute-start(bf16[10,64,128]{2,1,0:T(8,128)(2,1)S(1)} %pad_maximum_fusion.1.refs_0_), channel_id=1, source_target_pairs={{0,2},{1,3},{2,0},{3,1},{4,6},{5,7},{6,4},{7,5},{8,10},{9,11},{10,... | collective-permute-start | bytes 491528 | tf_op jit(solution)/shard_map/ppermute | solution.py:300
  16.9 2.7 %collective-permute-start.8 = (bf16[10,64,128]{2,1,0:T(8,128)(2,1)S(1)}, bf16[10,64,128]{2,1,0:T(8,128)(2,1)S(1)}, u32[]{:S(2)}, u32[]{:S(2)}) collective-permute-start(bf16[10,64,128]{2,1,0:T(8,128)(2,1)S(1)} %collective-permute-done.2.refs_1_), channel_id=1, source_target_pairs={{0,2},{1,3},{2,0},{3,1},{4,6},{5,7},{6,4},{7,5},{8,10},{9,11},{10,... | collective-permute-start | bytes 491528 | tf_op jit(solution)/shard_map/ppermute | solution.py:301
  27.0 3.0 %collective-permute-start.14 = (bf16[2,8,64,128]{3,2,1,0:T(8,128)(2,1)S(1)}, bf16[2,8,64,128]{3,2,1,0:T(8,128)(2,1)S(1)}, u32[]{:S(2)}, u32[]{:S(2)}) collective-permute-start(bf16[2,8,64,128]{3,2,1,0:T(8,128)(2,1)S(1)} %get-tuple-element.59), channel_id=1, source_target_pairs={{0,2},{1,3},{2,0},{3,1},{4,6},{5,7},{6,4},{7,5},{8,10},{9,11},{10,... | collective-permute-start | bytes 786440 | tf_op jit(solution)/shard_map/ppermute | solution.py:317
  34.0 2.5 %collective-permute-start.10 = (f32[8,128]{1,0:T(8,128)S(1)}, f32[8,128]{1,0:T(8,128)S(1)}, u32[]{:S(2)}, u32[]{:S(2)}) collective-permute-start(f32[8,128]{1,0:T(8,128)S(1)} %add.40), channel_id=1, source_target_pairs={{0,16},{8,24},{16,0},{24,8},{32,48},{40,56},{48,32},{56,40},{64,80... | collective-permute-start | bytes 12296 | tf_op jit(solution)/shard_map/ppermute | solution.py:334
  37.8 3.0 %collective-permute-start.11 = (f32[8,128]{1,0:T(8,128)S(1)}, f32[8,128]{1,0:T(8,128)S(1)}, u32[]{:S(2)}, u32[]{:S(2)}) collective-permute-start(f32[8,128]{1,0:T(8,128)S(1)} %add.41), channel_id=1, source_target_pairs={{0,32},{8,40},{16,48},{24,56},{32,0},{40,8},{48,16},{56,24},{64,96... | collective-permute-start | bytes 12296 | tf_op jit(solution)/shard_map/ppermute | solution.py:342
  42.0 4.0 %collective-permute-start.15 = (f32[8,128]{1,0:T(8,128)S(1)}, f32[8,128]{1,0:T(8,128)S(1)}, u32[]{:S(2)}, u32[]{:S(2)}) collective-permute-start(f32[8,128]{1,0:T(8,128)S(1)} %add.42), channel_id=1, source_target_pairs={{0,64},{8,72},{16,80},{24,88},{32,96},{40,104},{48,112},{56,120},{... | collective-permute-start | bytes 12296 | tf_op jit(solution)/shard_map/ppermute | solution.py:342
  47.2 2.1 %collective-permute-start.19 = (bf16[8,64,128]{2,1,0:T(8,128)(2,1)S(1)}, bf16[8,64,128]{2,1,0:T(8,128)(2,1)S(1)}, u32[]{:S(2)}, u32[]{:S(2)}) collective-permute-start(bf16[8,64,128]{2,1,0:T(8,128)(2,1)S(1)} %activation.1), channel_id=1, source_target_pairs={{0,4},{1,5},{2,6},{3,7},{4,0},{5,1},{6,2},{7,3},{8,12},{9,13},{10,... | collective-permute-start | bytes 393224 | tf_op jit(solution)/shard_map/ppermute | solution.py:306
  49.3 2.0 %collective-permute-done.16.far = bf16[8,64,128]{2,1,0:T(8,128)(2,1)S(1)} collective-permute-done((bf16[8,64,128]{2,1,0:T(8,128)(2,1)S(1)}, bf16[8,64,128]{2,1,0:T(8,128)(2,1)S(1)}, u32[]{:S(2)}, u32[]{:S(2)}) %collective-permute-start.16) | collective-permute-done | bytes 131104 | tf_op jit(solution)/shard_map/ppermute | solution.py:323
  51.5 3.6 %collective-permute-start.17 = (f32[8,128]{1,0:T(8,128)S(1)}, f32[8,128]{1,0:T(8,128)S(1)}, u32[]{:S(2)}, u32[]{:S(2)}) collective-permute-start(f32[8,128]{1,0:T(8,128)S(1)} %get-tuple-element.64), channel_id=1, source_target_pairs={{0,8},{8,0},{16,24},{24,16},{32,40},{40,32},{48,56},{56,48},{64,72... | collective-permute-start | bytes 12296 | tf_op jit(solution)/shard_map/ppermute | solution.py:334
  61.1 4.7 %collective-permute-start.24 = (f32[2,64,128]{2,1,0:T(8,128)S(1)}, f32[2,64,128]{2,1,0:T(8,128)S(1)}, u32[]{:S(2)}, u32[]{:S(2)}) collective-permute-start(f32[2,64,128]{2,1,0:T(8,128)S(1)} %pad_maximum_fusion.2), channel_id=1, source_target_pairs={{0,8},{8,16},{16,24},{24,32},{32,40},{40,48},{48,56},{56,64},{64,7... | collective-permute-start | bytes 196616 | tf_op jit(solution)/shard_map/ppermute | solution.py:329
  65.8 2.3 %collective-permute-start.21 = (f32[8,128]{1,0:T(8,128)S(1)}, f32[8,128]{1,0:T(8,128)S(1)}, u32[]{:S(2)}, u32[]{:S(2)}) collective-permute-start(f32[8,128]{1,0:T(8,128)S(1)} %add.46), channel_id=1, source_target_pairs={{0,64},{8,72},{16,80},{24,88},{32,96},{40,104},{48,112},{56,120},{... | collective-permute-start | bytes 12296 | tf_op jit(solution)/shard_map/ppermute | solution.py:342
  68.1 2.0 %collective-permute-done.21 = f32[8,128]{1,0:T(8,128)S(1)} collective-permute-done((f32[8,128]{1,0:T(8,128)S(1)}, f32[8,128]{1,0:T(8,128)S(1)}, u32[]{:S(2)}, u32[]{:S(2)}) %collective-permute-start.21) | collective-permute-done | bytes 4128 | tf_op jit(solution)/shard_map/ppermute | solution.py:342
  70.1 2.3 %collective-permute-start.25 = (f32[2,64,128]{2,1,0:T(8,128)S(1)}, f32[2,64,128]{2,1,0:T(8,128)S(1)}, u32[]{:S(2)}, u32[]{:S(2)}) collective-permute-start(f32[2,64,128]{2,1,0:T(8,128)S(1)} %pad_maximum_fusion.3), channel_id=1, source_target_pairs={{8,0},{16,8},{24,16},{32,24},{40,32},{48,40},{56,48},{64,56},{72,6... | collective-permute-start | bytes 196616 | tf_op jit(solution)/shard_map/ppermute | solution.py:329
  75.7 2.0 %band_grad.1 = (bf16[576,1024]{1,0:T(8,128)(2,1)S(1)}, bf16[2,8,64,128]{3,2,1,0:T(8,128)(2,1)S(1)}, bf16[2,8,64,128]{3,2,1,0:T(8,128)(2,1)S(1)}, bf16[2,8,64,128...) custom-call(s32[6]{0:T(128)S(1)} %stack.42.at, f32[8,64,128]{2,1,0:T(8,128)S(1)} %get-tuple-element.52.hid, ...), custom_call_target="tpu_custom_call" | custom-call | tf_op jit(solution)/shard_map/band_grad/pallas_call | solution.py:53
  81.9 2.2 %collective-permute-start.34 = (bf16[2,288,128]{2,1,0:T(8,128)(2,1)S(1)}, bf16[2,288,128]{2,1,0:T(8,128)(2,1)S(1)}, u32[]{:S(2)}, u32[]{:S(2)}) collective-permute-start(bf16[2,288,128]{2,1,0:T(8,128)(2,1)S(1)} %get-tuple-element.87), channel_id=1, source_target_pairs={{0,96},{8,104},{16,112},{24,120},{32,0},{40,8},{48,16},{56,24},{64... | collective-permute-start | bytes 442376 | tf_op jit(solution)/shard_map/ppermute | solution.py:434
  84.1 2.3 %collective-permute-start.35 = (bf16[2,288,128]{2,1,0:T(8,128)(2,1)S(1)}, bf16[2,288,128]{2,1,0:T(8,128)(2,1)S(1)}, u32[]{:S(2)}, u32[]{:S(2)}) collective-permute-start(bf16[2,288,128]{2,1,0:T(8,128)(2,1)S(1)} %get-tuple-element.88), channel_id=1, source_target_pairs={{0,64},{8,72},{16,80},{24,88},{32,96},{40,104},{48,112},{56,120},{... | collective-permute-start | bytes 442376 | tf_op jit(solution)/shard_map/ppermute | solution.py:434
  87.0 2.7 %collective-permute-start.30 = (bf16[2,8,64,128]{3,2,1,0:T(8,128)(2,1)S(1)}, bf16[2,8,64,128]{3,2,1,0:T(8,128)(2,1)S(1)}, u32[]{:S(2)}, u32[]{:S(2)}) collective-permute-start(bf16[2,8,64,128]{3,2,1,0:T(8,128)(2,1)S(1)} %get-tuple-element.80), channel_id=1, source_target_pairs={{0,3},{1,0},{2,1},{3,2},{4,7},{5,4},{6,5},{7,6},{8,11},{9,8},{10,9... | collective-permute-start | bytes 786440 | tf_op jit(solution)/shard_map/ppermute | solution.py:317
  92.6 4.2 %collective-permute-done.36.b = bf16[2,288,128]{2,1,0:T(8,128)(2,1)S(1)} collective-permute-done((bf16[2,288,128]{2,1,0:T(8,128)(2,1)S(1)}, bf16[2,288,128]{2,1,0:T(8,128)(2,1)S(1)}, u32[]{:S(2)}, u32[]{:S(2)}) %collective-permute-start.36) | collective-permute-done | bytes 147488 | tf_op jit(solution)/shard_map/ppermute | solution.py:440
  101.9 2.1 %collective-permute-start.37 = (bf16[2,288,128]{2,1,0:T(8,128)(2,1)S(1)}, bf16[2,288,128]{2,1,0:T(8,128)(2,1)S(1)}, u32[]{:S(2)}, u32[]{:S(2)}) collective-permute-start(bf16[2,288,128]{2,1,0:T(8,128)(2,1)S(1)} %pair_sum.1.refs_0_), channel_id=1, source_target_pairs={{0,8},{8,0},{16,24},{24,16},{32,40},{40,32},{48,56},{56,48},{64,72... | collective-permute-start | bytes 442376 | tf_op jit(solution)/shard_map/ppermute | solution.py:443
  104.0 3.2 %collective-permute-done.32.far = bf16[8,64,128]{2,1,0:T(8,128)(2,1)S(1)} collective-permute-done((bf16[8,64,128]{2,1,0:T(8,128)(2,1)S(1)}, bf16[8,64,128]{2,1,0:T(8,128)(2,1)S(1)}, u32[]{:S(2)}, u32[]{:S(2)}) %collective-permute-start.32) | collective-permute-done | bytes 131104 | tf_op jit(solution)/shard_map/ppermute | solution.py:323
  108.0 3.1 %collective-permute-start.43 = (bf16[2,288,128]{2,1,0:T(8,128)(2,1)S(1)}, bf16[2,288,128]{2,1,0:T(8,128)(2,1)S(1)}, u32[]{:S(2)}, u32[]{:S(2)}) collective-permute-start(bf16[2,288,128]{2,1,0:T(8,128)(2,1)S(1)} %collective-permute-done.42.refs_3_), channel_id=1, source_target_pairs={{0,8},{8,0},{16,24},{24,16},{32,40},{40,32},{48,56},{56,48},{64,72... | collective-permute-start | bytes 442376 | tf_op jit(solution)/shard_map/ppermute | solution.py:443
  (112 shorter events, 46.0 us)
Async XLA Ops:
  12.3 8.1 %collective-permute-start.5 = (bf16[10,64,128]{2,1,0:T(8,128)(2,1)S(1)}, bf16[10,64,128]{2,1,0:T(8,128)(2,1)S(1)}, u32[]{:S(2)}, u32[]{:S(2)}) collective-permute-start(bf16[10,64,128]{2,1,0:T(8,128)(2,1)S(1)} %pad_maximum_fusion.1.refs_0_), channel_id=1, source_target_pairs={{0,2},{1,3},{2,0},{3,1},{4,6},{5,7},{6,4},{7,5},{8,10},{9,11},{10,... | collective-permute-start | bytes 491528 | tf_op jit(solution)/shard_map/ppermute | solution.py:300
  15.2 8.7 %collective-permute-start.4 = (bf16[10,64,128]{2,1,0:T(8,128)(2,1)S(1)}, bf16[10,64,128]{2,1,0:T(8,128)(2,1)S(1)}, u32[]{:S(2)}, u32[]{:S(2)}) collective-permute-start(bf16[10,64,128]{2,1,0:T(8,128)(2,1)S(1)} %pad_maximum_fusion.1.refs_0_), channel_id=1, source_target_pairs={{0,3},{1,0},{2,1},{3,2},{4,7},{5,4},{6,5},{7,6},{8,11},{9,8},{10,9... | collective-permute-start | bytes 491528 | tf_op jit(solution)/shard_map/ppermute | solution.py:300
  16.0 8.8 %collective-permute-start.3 = (bf16[10,64,128]{2,1,0:T(8,128)(2,1)S(1)}, bf16[10,64,128]{2,1,0:T(8,128)(2,1)S(1)}, u32[]{:S(2)}, u32[]{:S(2)}) collective-permute-start(bf16[10,64,128]{2,1,0:T(8,128)(2,1)S(1)} %pad_maximum_fusion.1.refs_0_), channel_id=1, source_target_pairs={{0,1},{1,2},{2,3},{3,0},{4,5},{5,6},{6,7},{7,4},{8,9},{9,10},{10,1... | collective-permute-start | bytes 491528 | tf_op jit(solution)/shard_map/ppermute | solution.py:300
  16.9 10.1 %collective-permute-start.8 = (bf16[10,64,128]{2,1,0:T(8,128)(2,1)S(1)}, bf16[10,64,128]{2,1,0:T(8,128)(2,1)S(1)}, u32[]{:S(2)}, u32[]{:S(2)}) collective-permute-start(bf16[10,64,128]{2,1,0:T(8,128)(2,1)S(1)} %collective-permute-done.2.refs_1_), channel_id=1, source_target_pairs={{0,2},{1,3},{2,0},{3,1},{4,6},{5,7},{6,4},{7,5},{8,10},{9,11},{10,... | collective-permute-start | bytes 491528 | tf_op jit(solution)/shard_map/ppermute | solution.py:301
  19.6 11.3 %collective-permute-start.7 = (bf16[10,64,128]{2,1,0:T(8,128)(2,1)S(1)}, bf16[10,64,128]{2,1,0:T(8,128)(2,1)S(1)}, u32[]{:S(2)}, u32[]{:S(2)}) collective-permute-start(bf16[10,64,128]{2,1,0:T(8,128)(2,1)S(1)} %collective-permute-done.2.refs_1_), channel_id=1, source_target_pairs={{0,3},{1,0},{2,1},{3,2},{4,7},{5,4},{6,5},{7,6},{8,11},{9,8},{10,9... | collective-permute-start | bytes 491528 | tf_op jit(solution)/shard_map/ppermute | solution.py:301
  20.4 10.6 %collective-permute-start.6 = (bf16[10,64,128]{2,1,0:T(8,128)(2,1)S(1)}, bf16[10,64,128]{2,1,0:T(8,128)(2,1)S(1)}, u32[]{:S(2)}, u32[]{:S(2)}) collective-permute-start(bf16[10,64,128]{2,1,0:T(8,128)(2,1)S(1)} %collective-permute-done.2.refs_1_), channel_id=1, source_target_pairs={{0,1},{1,2},{2,3},{3,0},{4,5},{5,6},{6,7},{7,4},{8,9},{9,10},{10,1... | collective-permute-start | bytes 491528 | tf_op jit(solution)/shard_map/ppermute | solution.py:301
  23.9 17.9 %collective-permute-start.12 = (bf16[2,8,64,128]{3,2,1,0:T(8,128)(2,1)S(1)}, bf16[2,8,64,128]{3,2,1,0:T(8,128)(2,1)S(1)}, u32[]{:S(2)}, u32[]{:S(2)}) collective-permute-start(bf16[2,8,64,128]{3,2,1,0:T(8,128)(2,1)S(1)} %get-tuple-element.57), channel_id=1, source_target_pairs={{0,1},{1,2},{2,3},{3,0},{4,5},{5,6},{6,7},{7,4},{8,9},{9,10},{10,1... | collective-permute-start | bytes 786440 | tf_op jit(solution)/shard_map/ppermute | solution.py:317
  24.8 17.0 %collective-permute-start.13 = (bf16[2,8,64,128]{3,2,1,0:T(8,128)(2,1)S(1)}, bf16[2,8,64,128]{3,2,1,0:T(8,128)(2,1)S(1)}, u32[]{:S(2)}, u32[]{:S(2)}) collective-permute-start(bf16[2,8,64,128]{3,2,1,0:T(8,128)(2,1)S(1)} %get-tuple-element.58), channel_id=1, source_target_pairs={{0,3},{1,0},{2,1},{3,2},{4,7},{5,4},{6,5},{7,6},{8,11},{9,8},{10,9... | collective-permute-start | bytes 786440 | tf_op jit(solution)/shard_map/ppermute | solution.py:317
  27.0 14.8 %collective-permute-start.14 = (bf16[2,8,64,128]{3,2,1,0:T(8,128)(2,1)S(1)}, bf16[2,8,64,128]{3,2,1,0:T(8,128)(2,1)S(1)}, u32[]{:S(2)}, u32[]{:S(2)}) collective-permute-start(bf16[2,8,64,128]{3,2,1,0:T(8,128)(2,1)S(1)} %get-tuple-element.59), channel_id=1, source_target_pairs={{0,2},{1,3},{2,0},{3,1},{4,6},{5,7},{6,4},{7,5},{8,10},{9,11},{10,... | collective-permute-start | bytes 786440 | tf_op jit(solution)/shard_map/ppermute | solution.py:317
  47.2 9.7 %collective-permute-start.19 = (bf16[8,64,128]{2,1,0:T(8,128)(2,1)S(1)}, bf16[8,64,128]{2,1,0:T(8,128)(2,1)S(1)}, u32[]{:S(2)}, u32[]{:S(2)}) collective-permute-start(bf16[8,64,128]{2,1,0:T(8,128)(2,1)S(1)} %activation.1), channel_id=1, source_target_pairs={{0,4},{1,5},{2,6},{3,7},{4,0},{5,1},{6,2},{7,3},{8,12},{9,13},{10,... | collective-permute-start | bytes 393224 | tf_op jit(solution)/shard_map/ppermute | solution.py:306
  56.9 15.5 %collective-permute-start.27 = (bf16[2,8,64,128]{3,2,1,0:T(8,128)(2,1)S(1)}, bf16[2,8,64,128]{3,2,1,0:T(8,128)(2,1)S(1)}, u32[]{:S(2)}, u32[]{:S(2)}) collective-permute-start(bf16[2,8,64,128]{3,2,1,0:T(8,128)(2,1)S(1)} %pad_maximum_fusion.refs_0_), channel_id=1, source_target_pairs={{0,2},{1,3},{2,0},{3,1},{4,6},{5,7},{6,4},{7,5},{8,10},{9,11},{10,... | collective-permute-start | bytes 786440 | tf_op jit(solution)/shard_map/ppermute | solution.py:307
  58.8 13.6 %collective-permute-start.23 = (bf16[2,8,64,128]{3,2,1,0:T(8,128)(2,1)S(1)}, bf16[2,8,64,128]{3,2,1,0:T(8,128)(2,1)S(1)}, u32[]{:S(2)}, u32[]{:S(2)}) collective-permute-start(bf16[2,8,64,128]{3,2,1,0:T(8,128)(2,1)S(1)} %pad_maximum_fusion.refs_0_), channel_id=1, source_target_pairs={{0,3},{1,0},{2,1},{3,2},{4,7},{5,4},{6,5},{7,6},{8,11},{9,8},{10,9... | collective-permute-start | bytes 786440 | tf_op jit(solution)/shard_map/ppermute | solution.py:307
  60.1 12.3 %collective-permute-start.22 = (bf16[2,8,64,128]{3,2,1,0:T(8,128)(2,1)S(1)}, bf16[2,8,64,128]{3,2,1,0:T(8,128)(2,1)S(1)}, u32[]{:S(2)}, u32[]{:S(2)}) collective-permute-start(bf16[2,8,64,128]{3,2,1,0:T(8,128)(2,1)S(1)} %pad_maximum_fusion.refs_0_), channel_id=1, source_target_pairs={{0,1},{1,2},{2,3},{3,0},{4,5},{5,6},{6,7},{7,4},{8,9},{9,10},{10,1... | collective-permute-start | bytes 786440 | tf_op jit(solution)/shard_map/ppermute | solution.py:307
  61.1 13.5 %collective-permute-start.24 = (f32[2,64,128]{2,1,0:T(8,128)S(1)}, f32[2,64,128]{2,1,0:T(8,128)S(1)}, u32[]{:S(2)}, u32[]{:S(2)}) collective-permute-start(f32[2,64,128]{2,1,0:T(8,128)S(1)} %pad_maximum_fusion.2), channel_id=1, source_target_pairs={{0,8},{8,16},{16,24},{24,32},{32,40},{40,48},{48,56},{56,64},{64,7... | collective-permute-start | bytes 196616 | tf_op jit(solution)/shard_map/ppermute | solution.py:329
  81.4 8.3 %collective-permute-start.33 = (bf16[2,288,128]{2,1,0:T(8,128)(2,1)S(1)}, bf16[2,288,128]{2,1,0:T(8,128)(2,1)S(1)}, u32[]{:S(2)}, u32[]{:S(2)}) collective-permute-start(bf16[2,288,128]{2,1,0:T(8,128)(2,1)S(1)} %get-tuple-element.86), channel_id=1, source_target_pairs={{0,32},{8,40},{16,48},{24,56},{32,64},{40,72},{48,80},{56,88},{64,... | collective-permute-start | bytes 442376 | tf_op jit(solution)/shard_map/ppermute | solution.py:434
  81.9 8.8 %collective-permute-start.34 = (bf16[2,288,128]{2,1,0:T(8,128)(2,1)S(1)}, bf16[2,288,128]{2,1,0:T(8,128)(2,1)S(1)}, u32[]{:S(2)}, u32[]{:S(2)}) collective-permute-start(bf16[2,288,128]{2,1,0:T(8,128)(2,1)S(1)} %get-tuple-element.87), channel_id=1, source_target_pairs={{0,96},{8,104},{16,112},{24,120},{32,0},{40,8},{48,16},{56,24},{64... | collective-permute-start | bytes 442376 | tf_op jit(solution)/shard_map/ppermute | solution.py:434
  84.1 7.9 %collective-permute-start.35 = (bf16[2,288,128]{2,1,0:T(8,128)(2,1)S(1)}, bf16[2,288,128]{2,1,0:T(8,128)(2,1)S(1)}, u32[]{:S(2)}, u32[]{:S(2)}) collective-permute-start(bf16[2,288,128]{2,1,0:T(8,128)(2,1)S(1)} %get-tuple-element.88), channel_id=1, source_target_pairs={{0,64},{8,72},{16,80},{24,88},{32,96},{40,104},{48,112},{56,120},{... | collective-permute-start | bytes 442376 | tf_op jit(solution)/shard_map/ppermute | solution.py:434
  87.0 12.7 %collective-permute-start.29 = (bf16[2,8,64,128]{3,2,1,0:T(8,128)(2,1)S(1)}, bf16[2,8,64,128]{3,2,1,0:T(8,128)(2,1)S(1)}, u32[]{:S(2)}, u32[]{:S(2)}) collective-permute-start(bf16[2,8,64,128]{3,2,1,0:T(8,128)(2,1)S(1)} %get-tuple-element.78), channel_id=1, source_target_pairs={{0,1},{1,2},{2,3},{3,0},{4,5},{5,6},{6,7},{7,4},{8,9},{9,10},{10,1... | collective-permute-start | bytes 786440 | tf_op jit(solution)/shard_map/ppermute | solution.py:317
  87.0 13.2 %collective-permute-start.30 = (bf16[2,8,64,128]{3,2,1,0:T(8,128)(2,1)S(1)}, bf16[2,8,64,128]{3,2,1,0:T(8,128)(2,1)S(1)}, u32[]{:S(2)}, u32[]{:S(2)}) collective-permute-start(bf16[2,8,64,128]{3,2,1,0:T(8,128)(2,1)S(1)} %get-tuple-element.80), channel_id=1, source_target_pairs={{0,3},{1,0},{2,1},{3,2},{4,7},{5,4},{6,5},{7,6},{8,11},{9,8},{10,9... | collective-permute-start | bytes 786440 | tf_op jit(solution)/shard_map/ppermute | solution.py:317
  89.7 12.0 %collective-permute-start.31 = (bf16[2,8,64,128]{3,2,1,0:T(8,128)(2,1)S(1)}, bf16[2,8,64,128]{3,2,1,0:T(8,128)(2,1)S(1)}, u32[]{:S(2)}, u32[]{:S(2)}) collective-permute-start(bf16[2,8,64,128]{3,2,1,0:T(8,128)(2,1)S(1)} %get-tuple-element.82), channel_id=1, source_target_pairs={{0,2},{1,3},{2,0},{3,1},{4,6},{5,7},{6,4},{7,5},{8,10},{9,11},{10,... | collective-permute-start | bytes 786440 | tf_op jit(solution)/shard_map/ppermute | solution.py:317
  96.8 11.2 %collective-permute-start.42 = (bf16[2,288,128]{2,1,0:T(8,128)(2,1)S(1)}, bf16[2,288,128]{2,1,0:T(8,128)(2,1)S(1)}, u32[]{:S(2)}, u32[]{:S(2)}) collective-permute-start(bf16[2,288,128]{2,1,0:T(8,128)(2,1)S(1)} %pair_sum.1.refs_0_), channel_id=1, source_target_pairs={{0,64},{8,72},{16,80},{24,88},{32,96},{40,104},{48,112},{56,120},{... | collective-permute-start | bytes 442376 | tf_op jit(solution)/shard_map/ppermute | solution.py:442
  98.6 12.4 %collective-permute-start.40 = (bf16[2,288,128]{2,1,0:T(8,128)(2,1)S(1)}, bf16[2,288,128]{2,1,0:T(8,128)(2,1)S(1)}, u32[]{:S(2)}, u32[]{:S(2)}) collective-permute-start(bf16[2,288,128]{2,1,0:T(8,128)(2,1)S(1)} %pair_sum.1.refs_0_), channel_id=1, source_target_pairs={{0,96},{8,104},{16,112},{24,120},{32,0},{40,8},{48,16},{56,24},{64... | collective-permute-start | bytes 442376 | tf_op jit(solution)/shard_map/ppermute | solution.py:442
  99.6 11.5 %collective-permute-start.38 = (bf16[2,288,128]{2,1,0:T(8,128)(2,1)S(1)}, bf16[2,288,128]{2,1,0:T(8,128)(2,1)S(1)}, u32[]{:S(2)}, u32[]{:S(2)}) collective-permute-start(bf16[2,288,128]{2,1,0:T(8,128)(2,1)S(1)} %pair_sum.1.refs_0_), channel_id=1, source_target_pairs={{0,32},{8,40},{16,48},{24,56},{32,64},{40,72},{48,80},{56,88},{64,... | collective-permute-start | bytes 442376 | tf_op jit(solution)/shard_map/ppermute | solution.py:442
  101.9 11.3 %collective-permute-start.37 = (bf16[2,288,128]{2,1,0:T(8,128)(2,1)S(1)}, bf16[2,288,128]{2,1,0:T(8,128)(2,1)S(1)}, u32[]{:S(2)}, u32[]{:S(2)}) collective-permute-start(bf16[2,288,128]{2,1,0:T(8,128)(2,1)S(1)} %pair_sum.1.refs_0_), channel_id=1, source_target_pairs={{0,8},{8,0},{16,24},{24,16},{32,40},{40,32},{48,56},{56,48},{64,72... | collective-permute-start | bytes 442376 | tf_op jit(solution)/shard_map/ppermute | solution.py:443
  (24 other events, 167.5 us)
